TPU v7x, 256 devices: a whole 4x4x8 slice. The times are simulated.
256 devices in a mesh: dp: 8 (over x, y_hi), ctx: 32 (over z, y_lo, core).
Axes of the slice: x: 4, y: 4 (y_hi: 2, y_lo: 2; y = y_hi * 2 + y_lo), z: 8, core: 2. Of those that a mesh axis runs over, the one named last changes fastest.
Arguments:
- tokens: bfloat16 [8, 8192, 1536], P('dp', 'ctx'), may hold values from -40 to 40, as said below
- segments: int32 [8, 8192], P('dp'), may hold values from 0 to 7, never falling along the last dimension, each value on 1 to 1536 neighbouring positions
- w_query: bfloat16 [1536, 1536], replicated, as said below
- w_keyval: bfloat16 [1536, 512], replicated, as said below
- grad_context: bfloat16 [8, 8192, 1536], P('dp', 'ctx'), may hold values from -6 to 6
Outputs:
- context: bfloat16 [8, 8192, 1536], P('dp', 'ctx')
- grad_tokens: bfloat16 [8, 8192, 1536], P('dp', 'ctx')
- grad_query_w: bfloat16 [1536, 1536], P('ctx')
- grad_keyval_w: bfloat16 [1536, 512], P('ctx')
Inputs may be any that keep to these rules, and one draw needn't show every extreme that they name: `segments`: document numbers never fall along a sequence; a document covers at most 1536 positions. `tokens`: activations of order one. `w_query`: a weight matrix of fan-in 1536. `w_keyval`: a weight matrix of fan-in 1536.
All inputs are finite; a program needn't handle non-finite values.
Results may differ from a plain program's by a relative error of at most 0.03.
The roundings to bfloat16 on the way count: a program that leaves them out, or rounds other values in their place, can miss the bound.
Values may be sent and summed in bfloat16 or wider, within the bound.
No kernel may reach another device: no remote copies, remote signals or barrier semaphores. Data moves between devices by JAX's collectives and lax.ppermute only.
A program may use at most 128 MiB of HBM per device.

v0:
```python
import jax
import jax.numpy as jnp
from jax import lax
from jax.sharding import PartitionSpec as P

HEADS = 12
KV_HEADS = 2
HEAD_DIM = 128
WINDOW = 512
BLOCK = 128


def shifted(value, axis, steps):
    count = lax.axis_size(axis)
    leading, last = (max(0, -steps), min(count, count - steps))
    return lax.ppermute(value, axis, [(source, source + steps) for source in range(leading, last)])


def shards(tokens, segments, w_query, w_keyval, grad_context):
    hidden_in = tokens[0]
    tok_rows = hidden_in.shape[0]
    model_width = hidden_in.shape[1]
    kv_width = KV_HEADS * HEAD_DIM
    group_size = HEADS // KV_HEADS
    score_scale = HEAD_DIM ** (-0.5)
    halo_rows = WINDOW - BLOCK
    ctx_index = lax.axis_index("ctx")
    hop_rows = []
    remain = halo_rows
    while remain > 0:
        hop_rows.append(min(tok_rows, remain))
        remain = remain - hop_rows[-1]
    queries = jnp.dot(hidden_in, w_query, preferred_element_type=jnp.float32).astype(jnp.bfloat16)
    keyval = jnp.dot(hidden_in, w_keyval, preferred_element_type=jnp.float32).astype(jnp.bfloat16)
    pieces = []
    for stride, count_rows in enumerate(hop_rows):
        pieces.append(shifted(keyval[tok_rows - count_rows :], "ctx", stride + 1))
    keys_all = jnp.concatenate(pieces[::-1] + [keyval], axis=0)
    key_count = keys_all.shape[0]
    query_heads = queries.reshape(tok_rows, KV_HEADS, group_size, HEAD_DIM)
    key_heads = keys_all[:, :kv_width].reshape(key_count, KV_HEADS, HEAD_DIM)
    val_heads = keys_all[:, kv_width:].reshape(key_count, KV_HEADS, HEAD_DIM)
    doc_ids = segments[0]
    padded_ids = jnp.concatenate([jnp.full((halo_rows,), -1, jnp.int32), doc_ids], axis=0)
    first_pos = ctx_index * tok_rows
    query_pos = first_pos + jnp.arange(tok_rows, dtype=jnp.int32)
    key_pos = first_pos - halo_rows + jnp.arange(key_count, dtype=jnp.int32)
    query_ids = lax.dynamic_slice_in_dim(doc_ids, first_pos, tok_rows, 0)
    key_ids = lax.dynamic_slice_in_dim(padded_ids, first_pos, key_count, 0)
    lowest = (query_pos // BLOCK - WINDOW // BLOCK + 1) * BLOCK
    allowed = (key_pos[None, :] <= query_pos[:, None]) & (key_pos[None, :] >= lowest[:, None])
    allowed = allowed & (key_ids[None, :] == query_ids[:, None])
    scores = (
        jnp.einsum("tgha,kga->ghtk", query_heads, key_heads, preferred_element_type=jnp.float32)
        * score_scale
    )
    masked = jnp.where(allowed[None, None], scores, -1e30)
    row_max = jnp.max(masked, axis=-1, keepdims=True)
    expo = jnp.exp(masked - row_max)
    attn_probs = expo / jnp.sum(expo, axis=-1, keepdims=True)
    probs_low = attn_probs.astype(jnp.bfloat16)
    ctx_heads = jnp.einsum(
        "ghtk,kga->tgha", probs_low, val_heads, preferred_element_type=jnp.float32
    ).astype(jnp.bfloat16)
    context = ctx_heads.reshape(tok_rows, model_width)
    grad_out = grad_context[0].reshape(tok_rows, KV_HEADS, group_size, HEAD_DIM)
    row_delta = jnp.einsum(
        "tgha,tgha->ght", grad_out, ctx_heads, preferred_element_type=jnp.float32
    )
    grad_probs = jnp.einsum(
        "tgha,kga->ghtk", grad_out, val_heads, preferred_element_type=jnp.float32
    )
    grad_scores = (attn_probs * (grad_probs - row_delta[..., None]) * score_scale).astype(
        jnp.bfloat16
    )
    grad_queries = jnp.einsum(
        "ghtk,kga->tgha", grad_scores, key_heads, preferred_element_type=jnp.float32
    )
    grad_queries = grad_queries.astype(jnp.bfloat16).reshape(tok_rows, model_width)
    grad_key = jnp.einsum(
        "ghtk,tgha->kga", grad_scores, query_heads, preferred_element_type=jnp.float32
    )
    grad_val = jnp.einsum("ghtk,tgha->kga", probs_low, grad_out, preferred_element_type=jnp.float32)
    grad_kv = jnp.concatenate(
        [grad_key.reshape(key_count, kv_width), grad_val.reshape(key_count, kv_width)], axis=1
    )
    halo_grads = grad_kv[:halo_rows]
    own_grads = grad_kv[halo_rows:]
    bounds = []
    upper = halo_rows
    for count_rows in hop_rows:
        bounds.append((upper - count_rows, upper))
        upper = upper - count_rows
    for stride, (first_row, last_row) in enumerate(bounds):
        arrived = shifted(halo_grads[first_row:last_row], "ctx", -(stride + 1))
        own_grads = own_grads + jnp.pad(arrived, ((tok_rows - arrived.shape[0], 0), (0, 0)))
    grad_keyval = own_grads.astype(jnp.bfloat16)
    contract_rows = (((1,), (1,)), ((), ()))
    grad_in = lax.dot_general(
        grad_queries, w_query, contract_rows, preferred_element_type=jnp.float32
    )
    grad_in = grad_in + lax.dot_general(
        grad_keyval, w_keyval, contract_rows, preferred_element_type=jnp.float32
    )
    combined = jnp.concatenate([grad_queries, grad_keyval], axis=1)
    contract_tokens = (((0,), (0,)), ((), ()))
    shard_sum = lax.psum_scatter(
        lax.dot_general(hidden_in, combined, contract_tokens, preferred_element_type=jnp.float32),
        "ctx",
        scatter_dimension=0,
        tiled=True,
    )
    grand_sum = lax.psum(shard_sum, "dp")
    weight_low = grand_sum.astype(jnp.bfloat16)
    return (
        context[None],
        grad_in.astype(jnp.bfloat16)[None],
        weight_low[:, :model_width],
        weight_low[:, model_width:],
    )


def solution(mesh):
    placed = (P("dp", "ctx", None), P("dp", None), P(), P(), P("dp", "ctx", None))
    return jax.shard_map(
        shards,
        mesh=mesh,
        in_specs=placed,
        out_specs=(P("dp", "ctx", None), P("dp", "ctx", None), P("ctx", None), P("ctx", None)),
        check_vma=False,
    )
```

profile of v0, /device:TPU:64, one launch (start us, length us, event | category | flops | bytes accessed | tf_op | source)
XLA Modules:
  0.0 326.8 jit_solution(16342258954147465209)
XLA Ops:
  7.2 0.0 copy-start
  7.2 0.0 reduce-scatter.4.cloned.1.call-start
  7.2 1.4 copy-done
  8.6 1.7 convolution_convert_fusion.3
  10.3 1.9 collective-permute-start.1
  12.2 0.7 slice.35
  12.9 3.5 %collective-permute-start = (bf16[128,512]{1,0:T(8,128)(2,1)}, bf16[128,512]{1,0:T(8,128)(2,1)S(1)}, u32[]{:S(2)}, u32[]{:S(2)}) collective-permute-start(bf16[128,512]{1,0:T(8,128)(2,1)} %slice.35), channel_id=1, source_target_pairs={{0,2},{1,3},{2,4},{3,5},{4,6},{5,7},{6,8},{7,9},{8,10},{9,11},{10,... | collective-permute-start | bytes 393224 | tf_op jit(solution)/shard_map/ppermute | solution.py:16
  16.4 0.0 copy-start.6
  16.4 0.0 copy-start.5
  16.4 4.9 %convolution_convert_fusion = bf16[256,1536]{1,0:T(8,128)(2,1)} fusion(bf16[1536,1536]{1,0:T(8,128)(2,1)} %param.7, bf16[1,256,1536]{2,1,0:T(8,128)(2,1)} %param.5), kind=kOutput, calls=%fused_computation.16 | convolution fusion | flops 1208352768 | bytes 6291456 | tf_op jit(solution)/shard_map/dot_general | solution.py:33
  21.3 0.0 copy-done.6
  21.3 0.1 pad_dynamic-slice_fusion
  21.4 0.6 constant_dynamic-slice_fusion
  22.0 0.0 copy-done.5
  22.0 0.3 copy.44
  22.2 1.4 copy.39
  23.6 1.6 compare_and_fusion
  25.2 0.0 collective-permute-done
  25.3 0.0 collective-permute-done.1
  25.3 1.0 pad_maximum_fusion
  26.3 0.8 fusion.30
  27.0 1.8 reshape.143
  28.8 0.8 reshape.144
  29.6 1.3 copy.66
  30.9 5.7 %fusion.31 = (f32[2,6,256]{2,1,0:T(8,128)S(1)}, f32[2,6,256,640]{2,3,1,0:T(8,128)}) fusion(pred[256,640]{0,1:T(8,128)(4,1)} %compare_and_fusion, bf16[640,2,128,1]{0,2,3,1:T(8,128)(2,1)S(1)} %copy.66, bf16[256,2,6,128]{0,3,2,1:T(8,128)(2,1)S(1)} %bitcast.92), kind=kOutput, calls=%fused_computation.57 | convolution fusion | flops 511181440 | bytes 9154560 | tf_op jit(solution)/shard_map/sub | solution.py:59
  36.7 4.0 %fusion.8 = bf16[2,6,256,640]{2,3,1,0:T(8,128)(2,1)S(1)} fusion(f32[2,6,256,640]{2,3,1,0:T(8,128)} %get-tuple-element.19, f32[2,6,256]{2,1,0:T(8,128)S(1)} %get-tuple-element.18), kind=kLoop, calls=%fused_computation.13 | loop fusion | flops 3932160 | bytes 11808768 | tf_op jit(solution)/shard_map/convert_element_type | solution.py:61
  40.7 0.0 copy-start.3
  40.7 0.0 copy-start.1
  40.7 1.3 fusion.34
  42.0 0.0 copy-done.3
  42.0 1.8 fusion.11
  43.8 0.5 copy-done.1
  44.3 1.6 fusion.3
  45.8 1.3 fusion.33
  47.2 4.3 %collective-permute-start.2 = (f32[256,512]{0,1:T(8,128)S(1)}, f32[256,512]{0,1:T(8,128)S(1)}, u32[]{:S(2)}, u32[]{:S(2)}) collective-permute-start(f32[256,512]{0,1:T(8,128)S(1)} %fusion.20), channel_id=1, source_target_pairs={{1,0},{2,1},{3,2},{4,3},{5,4},{6,5},{7,6},{8,7},{9,8},{10,9},{11,1... | collective-permute-start | bytes 1572872 | tf_op jit(solution)/shard_map/ppermute | solution.py:16
  51.5 0.0 copy-start.4
  51.5 2.7 collective-permute-start.3
  54.2 0.8 convolution_convert_fusion.1
  55.0 10.1 %collective-permute-done.3 = f32[128,512]{0,1:T(8,128)S(1)} collective-permute-done((f32[128,512]{0,1:T(8,128)S(1)}, f32[128,512]{0,1:T(8,128)S(1)}, u32[]{:S(2)}, u32[]{:S(2)}) %collective-permute-start.3) | collective-permute-done | bytes 262176 | tf_op jit(solution)/shard_map/ppermute | solution.py:16
  65.2 0.0 collective-permute-done.2
  65.2 0.1 fusion.24
  65.3 0.0 copy-done.4
  65.3 6.3 %convolution_bitcast_fusion = f32[1536,2048]{0,1:T(8,128)} fusion(bf16[256,512]{0,1:T(8,128)(2,1)S(1)} %fusion.24, bf16[256,1536]{0,1:T(8,128)(2,1)S(1)} %bitcast.90, bf16[1,256,1536]{2,1,0:T(8,128)(2,1)S(1)} %copy-done.4), kind=kOutput, calls=%fused_computation.1 | convolution fusion | flops 1612709888 | bytes 14417920 | tf_op jit(solution)/shard_map/dot_general | solution.py:108
  71.5 12.7 %copy.82 = f32[1536,2048]{1,0:T(8,128)} copy(f32[1536,2048]{0,1:T(8,128)} %convolution_bitcast_fusion) | data formatting | bytes 25165824
  84.3 0.0 copy-start.2
  84.3 0.0 reduce-scatter.4.cloned.1.call-update
  84.3 1.1 copy-done.2
  85.4 1.2 copy.51
  86.6 3.8 %fusion.32 = f32[256,1536]{1,0:T(8,128)S(1)} fusion(bf16[256,1536]{0,1:T(8,128)(2,1)S(1)} %bitcast.91, bf16[1536,1536]{1,0:T(8,128)(2,1)} %param.7), kind=kOutput, calls=%fused_computation.58 | convolution fusion | flops 1207959552 | bytes 7077888 | tf_op jit(solution)/shard_map/dot_general | solution.py:99
  90.3 1.5 fusion.10
  91.8 139.2 %reduce-scatter.4.cloned.1.call-done = f32[48,2048]{1,0:T(8,128)} async-done(((f32[1536,2048]{1,0:T(8,128)}), f32[48,2048]{1,0:T(8,128)}) %reduce-scatter.4.cloned.1.call-update) | async-done | bytes 393232
  231.0 1.3 copy.83
  232.4 85.9 %all-reduce.3 = bf16[48,2048]{0,1:T(8,128)(2,1)S(1)} all-reduce(f32[48,2048]{0,1:T(8,128)S(1)} %copy.83), channel_id=1, replica_groups=mesh['dp'=8,'ctx'=32] {'dp'}, use_global_device_ids=true, to_apply=%region_3.4 | all-reduce | flops 98304 | bytes 589824 | tf_op jit(solution)/shard_map/psum | solution.py:113
  318.4 0.8 copy.52
  319.2 0.7 copy.53
  (5 shorter events, 0.1 us)
Async XLA Ops:
  7.2 1.4 copy-start
  7.2 223.9 %reduce-scatter.4.cloned.1.call-start = ((), (), s32[]{:S(2)}) async-start(), calls=%async_computation.1 | async-start | bytes 12976128
  10.3 15.0 %collective-permute-start.1 = (bf16[256,512]{1,0:T(8,128)(2,1)S(1)}, bf16[256,512]{1,0:T(8,128)(2,1)}, u32[]{:S(2)}, u32[]{:S(2)}) collective-permute-start(bf16[256,512]{1,0:T(8,128)(2,1)S(1)} %convolution_convert_fusion.3), channel_id=1, source_target_pairs={{0,1},{1,2},{2,3},{3,4},{4,5},{5,6},{6,7},{7,8},{8,9},{9,10},{10,1... | collective-permute-start | bytes 786440 | tf_op jit(solution)/shard_map/ppermute | solution.py:16
  12.9 12.4 %collective-permute-start = (bf16[128,512]{1,0:T(8,128)(2,1)}, bf16[128,512]{1,0:T(8,128)(2,1)S(1)}, u32[]{:S(2)}, u32[]{:S(2)}) collective-permute-start(bf16[128,512]{1,0:T(8,128)(2,1)} %slice.35), channel_id=1, source_target_pairs={{0,2},{1,3},{2,4},{3,5},{4,6},{5,7},{6,8},{7,9},{8,10},{9,11},{10,... | collective-permute-start | bytes 393224 | tf_op jit(solution)/shard_map/ppermute | solution.py:16
  16.4 4.9 %copy-start.6 = (s32[1,8192]{1,0:T(1,128)S(1)}, s32[1,8192]{1,0:T(1,128)}, u32[]{:S(2)}) copy-start(s32[1,8192]{1,0:T(1,128)} %param.6) | copy-start | bytes 98308
  16.4 5.6 %copy-start.5 = (bf16[1,256,1536]{2,1,0:T(8,128)(2,1)S(1)}, bf16[1,256,1536]{2,1,0:T(8,128)(2,1)}, u32[]{:S(2)}) copy-start(bf16[1,256,1536]{2,1,0:T(8,128)(2,1)} %param.9) | copy-start | bytes 2359300
  40.7 1.3 copy-start.3
  40.7 3.6 %copy-start.1 = (f32[2,6,256,640]{2,3,1,0:T(8,128)S(1)}, f32[2,6,256,640]{2,3,1,0:T(8,128)}, u32[]{:S(2)}) copy-start(f32[2,6,256,640]{2,3,1,0:T(8,128)} %get-tuple-element.19) | copy-start | bytes 23592964
  47.2 18.0 %collective-permute-start.2 = (f32[256,512]{0,1:T(8,128)S(1)}, f32[256,512]{0,1:T(8,128)S(1)}, u32[]{:S(2)}, u32[]{:S(2)}) collective-permute-start(f32[256,512]{0,1:T(8,128)S(1)} %fusion.20), channel_id=1, source_target_pairs={{1,0},{2,1},{3,2},{4,3},{5,4},{6,5},{7,6},{8,7},{9,8},{10,9},{11,1... | collective-permute-start | bytes 1572872 | tf_op jit(solution)/shard_map/ppermute | solution.py:16
  51.5 13.7 %copy-start.4 = (bf16[1,256,1536]{2,1,0:T(8,128)(2,1)S(1)}, bf16[1,256,1536]{2,1,0:T(8,128)(2,1)}, u32[]{:S(2)}) copy-start(bf16[1,256,1536]{2,1,0:T(8,128)(2,1)} %param.5) | copy-start | bytes 2359300
  51.5 13.6 %collective-permute-start.3 = (f32[128,512]{0,1:T(8,128)S(1)}, f32[128,512]{0,1:T(8,128)S(1)}, u32[]{:S(2)}, u32[]{:S(2)}) collective-permute-start(f32[128,512]{0,1:T(8,128)S(1)} %pad_maximum_fusion.1), channel_id=1, source_target_pairs={{2,0},{3,1},{4,2},{5,3},{6,4},{7,5},{8,6},{9,7},{10,8},{11,9},{12,... | collective-permute-start | bytes 786440 | tf_op jit(solution)/shard_map/ppermute | solution.py:16
  84.3 1.1 copy-start.2
Sparse Core Ops, SparseCore 0:
  84.4 146.5 reduce-scatter.3
where the time goes:
time: 328 us; the launch traced here: 327 us
  waiting for transfers between devices  149 us (45%)
  blocking collectives  85.9 us (26%)
  matrix products  30.6 us (9%)
  local copies, waits for them, and re-layouts  27.4 us (8%)
  between operations  14.3 us (4%)
  starting transfers between devices  12.4 us (4%)
  other arithmetic  6.82 us (2%)
    unnamed x2, waiting for transfers between devices  139 us
    psum x1, blocking collectives, shards(): grand_sum = lax.psum(shard_sum, 'dp')  85.9 us
    unnamed x20, local copies, waits for them, and re-layouts  20 us
    ppermute x4, starting transfers between devices, shifted(): lax.ppermute(value, axis, [(source, source + steps) for source in range(l...  12.3 us
    ppermute x4, waiting for transfers between devices, shifted(): lax.ppermute(value, axis, [(source, source + steps) for source in range(l...  10.2 us
  transfers between devices with their start and end apart: 5, of which 2 were waited for; matrix products, arithmetic and copies ran while one was open for 5% of the time, Pallas kernels for 0%

commit v1 on v0

v1 whole, which is shorter than its diff:
```python
import functools

import jax
import jax.numpy as jnp
from jax import lax
from jax.experimental import pallas as pl
from jax.experimental.pallas import tpu as pltpu
from jax.sharding import Mesh
from jax.sharding import PartitionSpec as P

HEAD_DIM = 128
GROUP = 6
KV_HEADS = 2
WINDOW = 512
BLOCK = 128
HALO = WINDOW - BLOCK
OWN = 256
PAIR = 2 * OWN
KEYS = HALO + PAIR
QCOLS = GROUP * HEAD_DIM
KVCOLS = 2 * HEAD_DIM
D = 1536
SCALE = HEAD_DIM ** (-0.5)
F32 = jnp.float32
BF16 = jnp.bfloat16
NT = (((1,), (1,)), ((), ()))
TN = (((0,), (0,)), ((), ()))
SUBS = 8
BIG = 48 * 1024 * 1024


def whole(shape):
    return pl.BlockSpec(shape, lambda *_: (0,) * len(shape))


def params():
    return pltpu.CompilerParams(vmem_limit_bytes=BIG)


def cost(flops, moved, trans=0):
    return pl.CostEstimate(flops=flops, bytes_accessed=moved, transcendentals=trans)


def nn(a, b):
    return jnp.dot(a, b, preferred_element_type=F32)


def nt(a, b):
    return lax.dot_general(a, b, NT, preferred_element_type=F32)


def tn(a, b):
    return lax.dot_general(a, b, TN, preferred_element_type=F32)


def project_own_body(core, x, wq, wk, wv, q, kv):
    xv = x[...]
    kv[...] = nn(xv, jnp.concatenate([wk[...], wv[...]], axis=1)).astype(BF16)
    q[...] = nn(xv, wq[...]).astype(BF16)


def project_own(core, x, w_query, w_keyval):
    return pl.pallas_call(
        project_own_body,
        grid_spec=pltpu.PrefetchScalarGridSpec(
            num_scalar_prefetch=1,
            grid=(1,),
            in_specs=[
                whole((OWN, D)),
                pl.BlockSpec((D, QCOLS), lambda i, c: (0, c[0])),
                pl.BlockSpec((D, HEAD_DIM), lambda i, c: (0, c[0])),
                pl.BlockSpec((D, HEAD_DIM), lambda i, c: (0, KV_HEADS + c[0])),
            ],
            out_specs=[whole((OWN, QCOLS)), whole((OWN, KVCOLS))],
        ),
        out_shape=[
            jax.ShapeDtypeStruct((OWN, QCOLS), BF16),
            jax.ShapeDtypeStruct((OWN, KVCOLS), BF16),
        ],
        compiler_params=params(),
        cost_estimate=cost(2 * OWN * D * 1024, 4 << 20),
        name="project_own",
    )(core, x, w_query, w_keyval, w_keyval)


def project_kv_body(core, x, kv_own, wk, wv, kv, sent):
    c = core[0]
    other = nn(x[...], jnp.concatenate([wk[...], wv[...]], axis=1)).astype(BF16)
    own = kv_own[...]
    low = jnp.where(c == 0, own, other)
    high = jnp.where(c == 0, other, own)
    kv[:OWN] = low
    kv[OWN:] = high
    sent[: HALO - OWN] = low[PAIR - HALO :]
    sent[HALO - OWN :] = high


def project_kv(core, x, kv_own, w_keyval):
    return pl.pallas_call(
        project_kv_body,
        grid_spec=pltpu.PrefetchScalarGridSpec(
            num_scalar_prefetch=1,
            grid=(1,),
            in_specs=[
                whole((OWN, D)),
                whole((OWN, KVCOLS)),
                pl.BlockSpec((D, HEAD_DIM), lambda i, c: (0, c[0])),
                pl.BlockSpec((D, HEAD_DIM), lambda i, c: (0, KV_HEADS + c[0])),
            ],
            out_specs=[whole((PAIR, KVCOLS)), whole((HALO, KVCOLS))],
        ),
        out_shape=[
            jax.ShapeDtypeStruct((PAIR, KVCOLS), BF16),
            jax.ShapeDtypeStruct((HALO, KVCOLS), BF16),
        ],
        compiler_params=params(),
        cost_estimate=cost(2 * OWN * D * KVCOLS, 2 << 20),
        name="project_kv",
    )(core, x, kv_own, w_keyval, w_keyval)


def project_q_body(core, x, wq, q):
    q[...] = nn(x[...], wq[...]).astype(BF16)


def project_q(core, x, w_query):
    return pl.pallas_call(
        project_q_body,
        grid_spec=pltpu.PrefetchScalarGridSpec(
            num_scalar_prefetch=1,
            grid=(1,),
            in_specs=[whole((OWN, D)), pl.BlockSpec((D, QCOLS), lambda i, c: (0, c[0]))],
            out_specs=whole((OWN, QCOLS)),
        ),
        out_shape=jax.ShapeDtypeStruct((OWN, QCOLS), BF16),
        compiler_params=params(),
        cost_estimate=cost(2 * OWN * D * QCOLS, 4 << 20),
        name="project_q",
    )(core, x, w_query)


def attend_body(
    place,
    q_own,
    q_oth,
    do_own,
    do_oth,
    kv,
    halo,
    segs,
    ctx_out,
    dq_out,
    dkv_out,
    sent_out,
    keys,
    vals_t,
    keys_t,
    ids,
    dkv,
):
    c = place[0]
    chip = place[1]
    b = pl.program_id(0)
    blocks = PAIR // BLOCK

    @pl.when(b == 0)
    def _():
        keys[:HALO] = halo[...]
        keys[HALO:] = kv[...]
        dkv[...] = jnp.zeros_like(dkv)
        for t in range(KEYS // BLOCK):
            rows = slice(t * BLOCK, (t + 1) * BLOCK)
            tile = keys[rows, :].astype(F32)
            keys_t[:, rows] = tile[:, :HEAD_DIM].T.astype(BF16)
            vals_t[:, rows] = tile[:, HEAD_DIM:].T.astype(BF16)
            row = chip * blocks - HALO // BLOCK + t
            line = segs[pl.ds(jnp.maximum(row, 0), 1), :]
            line = jnp.where(row >= 0, line, -1)
            ids[rows, :] = jnp.broadcast_to(line, (BLOCK, BLOCK)).T

    half = b // 2
    own = half == c
    inner = pl.multiple_of((b % 2) * BLOCK, BLOCK)
    here = pl.ds(inner, BLOCK)
    q_blk = jnp.where(own, q_own[here, :], q_oth[here, :])
    do_blk = jnp.where(own, do_own[here, :], do_oth[here, :])
    first = pl.multiple_of(b * BLOCK, BLOCK)
    win = pl.ds(first, WINDOW)
    k_win = keys[win, :HEAD_DIM]
    v_win = keys[win, HEAD_DIM:]
    kt_win = keys_t[:, win]
    vt_win = vals_t[:, win]
    query_ids = segs[pl.ds(chip * blocks + b, 1), :]
    j_pos = lax.broadcasted_iota(jnp.int32, (WINDOW, BLOCK), 0)
    i_pos = lax.broadcasted_iota(jnp.int32, (WINDOW, BLOCK), 1)
    seen = (ids[win, :] == query_ids) & (j_pos <= i_pos + HALO)
    seen2 = jnp.concatenate([seen, seen], axis=1)
    dk = jnp.zeros((WINDOW, HEAD_DIM), F32)
    dv = jnp.zeros((WINDOW, HEAD_DIM), F32)
    ctx_parts = []
    dq_parts = []
    for pair in range(GROUP // 2):
        h0 = slice(2 * pair * HEAD_DIM, (2 * pair + 1) * HEAD_DIM)
        h1 = slice((2 * pair + 1) * HEAD_DIM, (2 * pair + 2) * HEAD_DIM)
        q2 = jnp.concatenate([q_blk[:, h0], q_blk[:, h1]], axis=0)
        do2 = jnp.concatenate([do_blk[:, h0], do_blk[:, h1]], axis=0)
        scores = jnp.where(seen2, nt(k_win, q2) * SCALE, -1e30)
        top = jnp.max(scores, axis=0, keepdims=True)
        expo = jnp.exp(scores - top)
        probs = expo * (1.0 / jnp.sum(expo, axis=0, keepdims=True))
        probs_low = probs.astype(BF16)
        ctx_t = nn(vt_win, probs_low).astype(BF16).astype(F32)
        delta = jnp.sum(do2.astype(F32).T * ctx_t, axis=0, keepdims=True)
        dp = nt(v_win, do2)
        ds = (probs * (dp - delta) * SCALE).astype(BF16)
        dv = dv + nn(probs_low, do2)
        dk = dk + nn(ds, q2)
        dq2 = nn(kt_win, ds).T
        ctx2 = ctx_t.T
        ctx_parts += [ctx2[:BLOCK], ctx2[BLOCK:]]
        dq_parts += [dq2[:BLOCK], dq2[BLOCK:]]
    to = pl.ds(pl.multiple_of(jnp.where(own, 0, OWN) + inner, BLOCK), BLOCK)
    ctx_out[to, :] = jnp.concatenate(ctx_parts, axis=1).astype(BF16)
    dq_out[to, :] = jnp.concatenate(dq_parts, axis=1).astype(BF16)
    dkv[win, :] += jnp.concatenate([dk, dv], axis=1)

    @pl.when(b == blocks - 1)
    def _():
        sent_out[...] = dkv[:HALO, :].astype(BF16)
        dkv_out[...] = dkv[HALO:, :]


def attend(place, q_own, q_oth, do_own, do_oth, kv, halo, segs):
    return pl.pallas_call(
        attend_body,
        grid_spec=pltpu.PrefetchScalarGridSpec(
            num_scalar_prefetch=1,
            grid=(PAIR // BLOCK,),
            in_specs=[
                whole((OWN, QCOLS)),
                whole((OWN, QCOLS)),
                pl.BlockSpec((OWN, QCOLS), lambda i, p: (0, p[0])),
                whole((OWN, QCOLS)),
                whole((PAIR, KVCOLS)),
                whole((HALO, KVCOLS)),
                whole(segs.shape),
            ],
            out_specs=[
                whole((PAIR, QCOLS)),
                whole((PAIR, QCOLS)),
                whole((PAIR, KVCOLS)),
                whole((HALO, KVCOLS)),
            ],
            scratch_shapes=[
                pltpu.VMEM((KEYS, KVCOLS), BF16),
                pltpu.VMEM((HEAD_DIM, KEYS), BF16),
                pltpu.VMEM((HEAD_DIM, KEYS), BF16),
                pltpu.VMEM((KEYS, BLOCK), jnp.int32),
                pltpu.VMEM((KEYS, KVCOLS), F32),
            ],
        ),
        out_shape=[
            jax.ShapeDtypeStruct((PAIR, QCOLS), BF16),
            jax.ShapeDtypeStruct((PAIR, QCOLS), BF16),
            jax.ShapeDtypeStruct((PAIR, KVCOLS), F32),
            jax.ShapeDtypeStruct((HALO, KVCOLS), BF16),
        ],
        compiler_params=params(),
        cost_estimate=cost(2 * PAIR * WINDOW * QCOLS * 6, 4 << 20, PAIR * WINDOW * GROUP),
        name="attend",
    )(place, q_own, q_oth, do_own, do_oth, kv, halo, segs)


def spread(value, out, zs):
    rows = D // (2 * zs)
    low = value.astype(BF16)
    for s in range(2):
        for z in range(zs):
            for y in range(2):
                start = (z * 2 + y) * rows
                out[s * 2 + y, z * rows : (z + 1) * rows, :] = low[
                    start : start + rows, s * HEAD_DIM : (s + 1) * HEAD_DIM
                ]


def weight_q_body(x_own, x_oth, g, out):
    spread(tn(x_own[...], g[:OWN]) + tn(x_oth[...], g[OWN:]), out, 8)


def weight_q(x_own, x_oth, dq):
    return pl.pallas_call(
        weight_q_body,
        grid=(3,),
        in_specs=[
            whole((OWN, D)),
            whole((OWN, D)),
            pl.BlockSpec((PAIR, 256), lambda i: (0, i)),
        ],
        out_specs=pl.BlockSpec((4, D // 2, HEAD_DIM), lambda i: (i, 0, 0)),
        out_shape=jax.ShapeDtypeStruct((16, D // 2, HEAD_DIM), BF16),
        compiler_params=params(),
        cost_estimate=cost(2 * PAIR * D * QCOLS, 4 << 20),
        name="weight_q",
    )(x_own, x_oth, dq)


def weight_kv_body(place, x_own, x_oth, dkv, arrived, before, out, g_out):
    c = place[0]
    low = dkv[:OWN]
    skip = PAIR - HALO
    low = jnp.concatenate([low[:skip], low[skip:] + arrived[: OWN - skip].astype(F32)], axis=0)
    high = dkv[OWN:] + arrived[OWN - skip :].astype(F32)
    low = low.astype(BF16)
    high = high.astype(BF16)
    own = jnp.where(c == 0, low, high)
    oth = jnp.where(c == 0, high, low)
    g_out[:OWN] = own
    g_out[OWN:] = oth
    spread(tn(x_own[...], own) + tn(x_oth[...], oth), out, 8)


def weight_kv(place, x_own, x_oth, dkv, arrived, before):
    return pl.pallas_call(
        weight_kv_body,
        grid_spec=pltpu.PrefetchScalarGridSpec(
            num_scalar_prefetch=1,
            grid=(1,),
            in_specs=[
                whole((OWN, D)),
                whole((OWN, D)),
                whole((PAIR, KVCOLS)),
                whole((HALO, KVCOLS)),
                pl.BlockSpec(memory_space=pl.ANY),
            ],
            out_specs=[
                pl.BlockSpec((4, D // 2, HEAD_DIM), lambda i, p: (3, 0, 0)),
                whole((PAIR, KVCOLS)),
            ],
        ),
        out_shape=[
            jax.ShapeDtypeStruct((16, D // 2, HEAD_DIM), BF16),
            jax.ShapeDtypeStruct((PAIR, KVCOLS), BF16),
        ],
        input_output_aliases={5: 0},
        compiler_params=params(),
        cost_estimate=cost(2 * PAIR * D * KVCOLS, 3 << 20),
        name="weight_kv",
    )(place, x_own, x_oth, dkv, arrived, before)


def ordered(first, own, oth):
    return jnp.where(
        first, jnp.concatenate([own, oth], axis=1), jnp.concatenate([oth, own], axis=1)
    )


def grad_tokens_body(place, dq, dkv, ctx, dq_in, dkv_in, ctx_in, wq, wkv, out, ctx_out):
    first = place[0] == 0
    dq_full = ordered(first, dq[...], dq_in[...])
    kv = dkv[...]
    kv_in = dkv_in[...]
    keys = ordered(first, kv[:, :HEAD_DIM], kv_in[:, :HEAD_DIM])
    vals = ordered(first, kv[:, HEAD_DIM:], kv_in[:, HEAD_DIM:])
    kv_full = jnp.concatenate([keys, vals], axis=1)
    out[...] = (nt(dq_full, wq[...]) + nt(kv_full, wkv[...])).astype(BF16)

    @pl.when(pl.program_id(0) == 0)
    def _():
        ctx_out[...] = ordered(first, ctx[...], ctx_in[...])


def grad_tokens(place, dq, dkv, ctx, dq_in, dkv_in, ctx_in, w_query, w_keyval):
    step = 512
    return pl.pallas_call(
        grad_tokens_body,
        grid_spec=pltpu.PrefetchScalarGridSpec(
            num_scalar_prefetch=1,
            grid=(D // step,),
            in_specs=[
                whole((OWN, QCOLS)),
                whole((OWN, KVCOLS)),
                whole((OWN, QCOLS)),
                whole((OWN, QCOLS)),
                whole((OWN, KVCOLS)),
                whole((OWN, QCOLS)),
                pl.BlockSpec((step, D), lambda i, p: (i, 0)),
                pl.BlockSpec((step, 512), lambda i, p: (i, 0)),
            ],
            out_specs=[
                pl.BlockSpec((OWN, step), lambda i, p: (0, i)),
                whole((OWN, D)),
            ],
        ),
        out_shape=[
            jax.ShapeDtypeStruct((OWN, D), BF16),
            jax.ShapeDtypeStruct((OWN, D), BF16),
        ],
        compiler_params=params(),
        cost_estimate=cost(2 * OWN * D * 2048, 8 << 20),
        name="grad_tokens",
    )(place, dq, dkv, ctx, dq_in, dkv_in, ctx_in, w_query, w_keyval)


def swap(value):
    return lax.ppermute(value, "c", [(0, 1), (1, 0)])


def shards(tokens, segments, w_query, w_keyval, grad_context):
    x_own = tokens[0]
    core = lax.axis_index("c")
    chip = lax.axis_index(("z", "yl"))
    place = jnp.stack([core, chip]).astype(jnp.int32)
    away = lax.dynamic_slice_in_dim(grad_context[0], (1 - core) * QCOLS, QCOLS, 1)
    x_oth = swap(x_own)
    do_oth = swap(away)
    count = 32
    ring = ("z", "yl", "c")
    q_own, kv_own = project_own(place, x_own, w_query, w_keyval)
    kv, kv_sent = project_kv(place, x_oth, kv_own, w_keyval)
    halo = lax.ppermute(kv_sent, ring, [(i, i + 2) for i in range(count - 2)])
    q_oth = project_q(place, x_oth, w_query)
    segs = segments.reshape(-1, BLOCK)
    ctx, dq, dkv, dkv_sent = attend(
        place, q_own, q_oth, grad_context[0], do_oth, kv, halo, segs
    )
    arrived = lax.ppermute(dkv_sent, ring, [(i + 2, i) for i in range(count - 2)])
    ctx_in = swap(ctx[OWN:])
    dq_in = swap(dq[OWN:])
    partial = weight_q(x_own, x_oth, dq)
    partial, dkv_low = weight_kv(place, x_own, x_oth, dkv, arrived, partial)
    dkv_in = swap(dkv_low[OWN:])
    grad_in, context = grad_tokens(
        place, dq[:OWN], dkv_low[:OWN], ctx[:OWN], dq_in, dkv_in, ctx_in, w_query, w_keyval
    )
    pieces = lax.all_to_all(partial, ("x", "yh", "yl"), 0, 0)
    plane = jnp.sum(pieces.astype(F32), axis=0).astype(BF16)
    columns = lax.all_to_all(plane.reshape(8, 96, HEAD_DIM), "z", 0, 0)
    mine = jnp.sum(columns.astype(F32), axis=0).astype(BF16).reshape(1, 2, 48, HEAD_DIM)
    copies = jnp.broadcast_to(mine, (SUBS, 2, 48, HEAD_DIM)).reshape(16, 48, HEAD_DIM)
    final = lax.all_to_all(copies, ("x", "yh", "c"), 0, 0).reshape(SUBS, 2, 48, HEAD_DIM)
    query_w = final[:GROUP].transpose(2, 1, 0, 3).reshape(48, D)
    keyval_w = final[GROUP:].transpose(2, 0, 1, 3).reshape(48, 512)
    return context[None], grad_in[None], query_w, keyval_w


def solution(mesh):
    fine = Mesh(mesh.devices.reshape(4, 2, 8, 2, 2), ("x", "yh", "z", "yl", "c"))
    dp = ("x", "yh")
    ctx = ("z", "yl", "c")
    return jax.shard_map(
        shards,
        mesh=fine,
        in_specs=(P(dp, ctx, None), P(dp, None), P(), P(), P(dp, ctx, None)),
        out_specs=(P(dp, ctx, None), P(dp, ctx, None), P(ctx, None), P(ctx, None)),
        check_vma=False,
    )
```

time: 328 us -> 136 us (0.41)
  the two profiles are of different devices: /device:TPU:64 before, /device:TPU:1 now
where the time goes in v1:
time: 136 us
  starting transfers between devices  46 us (34%)
  waiting for transfers between devices  40.4 us (30%)
  Pallas kernels  26.4 us (19%)
  local copies, waits for them, and re-layouts  17.3 us (13%)
  other arithmetic  4.69 us (3%)
    all_to_all x1, waiting for transfers between devices, shards(): pieces = lax.all_to_all(partial, ('x', 'yh', 'yl'), 0, 0)  31.5 us
    all_to_all x1, starting transfers between devices, shards(): lax.all_to_all(copies, ('x', 'yh', 'c'), 0, 0)  13.4 us
    ppermute x5, starting transfers between devices, swap(): return lax.ppermute(value, 'c', [(0, 1), (1, 0)])  13.3 us
    pallas_call x1, Pallas kernels, attend(): pl.pallas_call(attend_body, grid_spec=pltpu.PrefetchScalarGridSpec(num_sc...  11.7 us
    all_to_all x1, starting transfers between devices, shards(): columns = lax.all_to_all(plane.reshape(8, 96, HEAD_DIM), 'z', 0, 0)  8.37 us
    all_to_all x1, starting transfers between devices, shards(): pieces = lax.all_to_all(partial, ('x', 'yh', 'yl'), 0, 0)  8.04 us
    unnamed x24, local copies, waits for them, and re-layouts  7.8 us
    pallas_call x1, Pallas kernels, grad_tokens(): pl.pallas_call(grad_tokens_body, grid_spec=pltpu.PrefetchScalarGridSpec(n...  5.97 us
  transfers between devices with their start and end apart: 10, of which 5 were waited for; matrix products, arithmetic and copies ran while one was open for 8% of the time, Pallas kernels for 10%

profile of v1, /device:TPU:1, one launch (start us, length us, event | category | flops | bytes accessed | tf_op | source)
XLA Modules:
  0.0 135.6 jit_solution(16864952403327879273)
XLA Ops:
  0.6 3.3 %collective-permute-start = (bf16[256,1536]{1,0:T(8,128)(2,1)}, bf16[256,1536]{1,0:T(8,128)(2,1)S(1)}, u32[]{:S(2)}, u32[]{:S(2)}) collective-permute-start(bf16[256,1536]{1,0:T(8,128)(2,1)} %bitcast.20), channel_id=1, source_target_pairs={{0,1},{1,0},{2,3},{3,2},{4,5},{5,4},{6,7},{7,6},{8,9},{9,8},{10,11... | collective-permute-start | bytes 2359304 | tf_op jit(solution)/shard_map/ppermute | solution.py:405
  4.0 1.0 dynamic-slice_bitcast_fusion
  5.0 0.1 collective-permute-start.1
  5.1 0.0 slice-start
  5.1 0.1 pad_add_fusion.core.place
  5.2 0.0 copy-start
  5.2 1.6 %copy-done = bf16[1536,512]{1,0:T(8,128)(2,1)S(1)} copy-done((bf16[1536,512]{1,0:T(8,128)(2,1)S(1)}, bf16[1536,512]{1,0:T(8,128)(2,1)}, u32[]{:S(2)}) %copy-start) | copy-done | bytes 1572888
  6.7 0.0 copy-start.3
  6.7 1.2 copy-done.3
  8.0 0.0 copy-start.1
  8.0 0.0 slice-start.1
  8.0 3.3 %project_own.1 = (bf16[256,768]{1,0:T(8,128)(2,1)S(1)}, bf16[256,256]{1,0:T(8,128)(2,1)S(1)}) custom-call(s32[2]{0:T(128)S(1)} %pad_add_fusion.core.place, bf16[256,1536]{1,0:T(8,128)(2,1)S(1)} %bitcast.21, bf16[1536,1536]{1,0:T(8,128)(2,1)} %wq.5, bf16[1536,512]{1,0:T(8,128)(2,1)S(1)} %copy-done, bf16[1536,512]{1,0:T(8,128)(2,1)S(1)} %copy-done), custom_call_target="tpu_custom_call" | custom-call | flops 805306368 | bytes 4194304 | tf_op jit(solution)/shard_map/project_own/pallas_call | solution.py:63
  11.2 0.0 collective-permute-done.x.x_oth
  11.3 0.0 copy-done.1
  11.3 1.0 project_kv.1
  12.3 0.0 copy-start.6
  12.3 0.0 copy-start.9
  12.3 1.6 %collective-permute-start.2 = (bf16[384,256]{1,0:T(8,128)(2,1)S(1)}, bf16[384,256]{1,0:T(8,128)(2,1)S(1)}, u32[]{:S(2)}, u32[]{:S(2)}) collective-permute-start(bf16[384,256]{1,0:T(8,128)(2,1)S(1)} %get-tuple-element.19), channel_id=1, source_target_pairs={{0,2},{1,3},{2,4},{3,5},{4,6},{5,7},{6,8},{7,9},{8,10},{9,11},{10,... | collective-permute-start | bytes 589832 | tf_op jit(solution)/shard_map/ppermute | solution.py:420
  13.9 0.0 slice-done
  13.9 0.0 slice-done.1
  14.0 1.3 project_q.1.q_oth
  15.3 0.0 collective-permute-done.1.do_oth
  15.3 0.0 copy-start.7
  15.3 0.7 copy-done.7
  16.1 1.6 %collective-permute-done.2.halo = bf16[384,256]{1,0:T(8,128)(2,1)S(1)} collective-permute-done((bf16[384,256]{1,0:T(8,128)(2,1)S(1)}, bf16[384,256]{1,0:T(8,128)(2,1)S(1)}, u32[]{:S(2)}, u32[]{:S(2)}) %collective-permute-start.2) | collective-permute-done | bytes 196640 | tf_op jit(solution)/shard_map/ppermute | solution.py:420
  17.7 0.0 copy-done.6
  17.7 0.0 copy-done.9
  17.7 0.0 copy-start.8
  17.7 1.0 copy-done.8
  18.7 11.7 %attend.1 = (bf16[512,768]{1,0:T(8,128)(2,1)S(1)}, bf16[512,768]{1,0:T(8,128)(2,1)S(1)}, f32[512,256]{1,0:T(8,128)S(1)}, bf16[384,256]{1,0:T(8,128)(2,1)S(1)}) custom-call(s32[2]{0:T(128)S(1)} %pad_add_fusion.core.place, bf16[256,768]{1,0:T(8,128)(2,1)S(1)} %get-tuple-element.16.q_own, bf16[256,768]{1,0:T(8,128)(2,1)S(1)} %project_q.1.q_oth, ...), custom_call_target="tpu_custom_call" | custom-call | flops 2415919104 | bytes 4194304 | tf_op jit(solution)/shard_map/attend/pallas_call | solution.py:234
  30.4 0.0 copy-start.4
  30.4 0.9 copy-done.4
  31.3 1.3 collective-permute-start.3
  32.5 2.0 %weight_q.1.before = bf16[16,768,128]{2,1,0:T(8,128)(2,1)S(1)} custom-call(bf16[256,1536]{1,0:T(8,128)(2,1)S(1)} %bitcast.22, bf16[256,1536]{1,0:T(8,128)(2,1)S(1)} %collective-permute-done.x.x_oth, bf16[512,768]{1,0:T(8,128)(2,1)S(1)} %get-tuple-element.20.g), custom_call_target="tpu_custom_call" | custom-call | flops 1207959552 | bytes 4194304 | tf_op jit(solution)/shard_map/weight_q/pallas_call | solution.py:291
  34.5 4.7 %collective-permute-done.3.arrived = bf16[384,256]{1,0:T(8,128)(2,1)S(1)} collective-permute-done((bf16[384,256]{1,0:T(8,128)(2,1)S(1)}, bf16[384,256]{1,0:T(8,128)(2,1)S(1)}, u32[]{:S(2)}, u32[]{:S(2)}) %collective-permute-start.3) | collective-permute-done | bytes 196640 | tf_op jit(solution)/shard_map/ppermute | solution.py:426
  39.2 1.2 weight_kv.1
  40.4 0.0 copy-start.2
  40.4 1.7 %copy-done.2 = bf16[16,768,128]{2,1,0:T(8,128)(2,1)} copy-done((bf16[16,768,128]{2,1,0:T(8,128)(2,1)}, bf16[16,768,128]{2,1,0:T(8,128)(2,1)S(1)}, u32[]{:S(2)}) %copy-start.2) | copy-done | bytes 3145752
  42.1 0.0 copy-start.5
  42.1 0.7 copy-done.5
  42.8 8.0 %all-to-all-start = ((bf16[16,768,128]{2,1,0:T(8,128)(2,1)}), bf16[16,768,128]{2,1,0:T(8,128)(2,1)}, u32[]{:S(2)}, u32[]{:S(2)}) async-start(bf16[16,768,128]{2,1,0:T(8,128)(2,1)} %copy-done.2), calls=%async_computation | async-start | bytes 6291456 | tf_op jit(solution)/shard_map/all_to_all | solution.py:435
  50.8 1.9 %fusion = (bf16[256,768]{1,0:T(8,128)(2,1)}, bf16[256,768]{1,0:T(8,128)(2,1)S(1)}) fusion(bf16[512,768]{1,0:T(8,128)(2,1)} %copy-done.4), kind=kLoop, calls=%fused_computation.2 | loop fusion | bytes 1572864 | tf_op jit(solution)/shard_map/slice | solution.py:427
  52.7 2.2 %collective-permute-start.6 = (bf16[256,768]{1,0:T(8,128)(2,1)}, bf16[256,768]{1,0:T(8,128)(2,1)S(1)}, u32[]{:S(2)}, u32[]{:S(2)}) collective-permute-start(bf16[256,768]{1,0:T(8,128)(2,1)} %get-tuple-element.28), channel_id=1, source_target_pairs={{0,1},{1,0},{2,3},{3,2},{4,5},{5,4},{6,7},{7,6},{8,9},{9,8},{10,11... | collective-permute-start | bytes 1179656 | tf_op jit(solution)/shard_map/ppermute | solution.py:405
  55.0 0.8 fusion.1
  55.8 0.0 collective-permute-start.4
  55.8 31.5 %all-to-all-done = bf16[16,768,128]{2,1,0:T(8,128)(2,1)} async-done(((bf16[16,768,128]{2,1,0:T(8,128)(2,1)}), bf16[16,768,128]{2,1,0:T(8,128)(2,1)}, u32[]{:S(2)}, u32[]{:S(2)}) %all-to-all-start) | async-done | bytes 3145760 | tf_op jit(solution)/shard_map/all_to_all | solution.py:435
  87.3 3.0 %reduce_sum.24 = bf16[768,128]{1,0:T(8,128)(2,1)} reduce(bf16[16,768,128]{2,1,0:T(8,128)(2,1)} %all-to-all-done, bf16[]{:T(256)} %constant.26.clone.1), dimensions={0}, to_apply=%region_0.0 | reduce | flops 1474560 | bytes 3342338 | tf_op jit(solution)/shard_map/reduce_sum | solution.py:436
  90.4 8.4 %all-to-all-start.1 = ((bf16[8,96,128]{2,1,0:T(8,128)(2,1)}), bf16[8,96,128]{2,1,0:T(8,128)(2,1)}, u32[]{:S(2)}, u32[]{:S(2)}) async-start(bf16[8,96,128]{2,1,0:T(8,128)(2,1)} %bitcast.8), calls=%async_computation.1 | async-start | bytes 393216 | tf_op jit(solution)/shard_map/all_to_all | solution.py:437
  98.7 1.0 fusion.2
  99.7 7.6 %collective-permute-start.5 = (bf16[256,256]{1,0:T(8,128)(2,1)S(1)}, bf16[256,256]{1,0:T(8,128)(2,1)S(1)}, u32[]{:S(2)}, u32[]{:S(2)}) collective-permute-start(bf16[256,256]{1,0:T(8,128)(2,1)S(1)} %get-tuple-element.32), channel_id=1, source_target_pairs={{0,1},{1,0},{2,3},{3,2},{4,5},{5,4},{6,7},{7,6},{8,9},{9,8},{10,11... | collective-permute-start | bytes 393224 | tf_op jit(solution)/shard_map/ppermute | solution.py:405
  107.4 0.1 all-to-all-done.1
  107.5 1.6 %reduce_sum.25 = bf16[96,128]{1,0:T(8,128)(2,1)} reduce(bf16[8,96,128]{2,1,0:T(8,128)(2,1)} %all-to-all-done.1, bf16[]{:T(256)} %constant.26.clone.1), dimensions={0}, to_apply=%region_1.0 | reduce | flops 86016 | bytes 221186 | tf_op jit(solution)/shard_map/reduce_sum | solution.py:438
  109.1 1.4 %broadcast_in_dim.16 = bf16[8,2,48,128]{3,2,1,0:T(8,128)(2,1)} broadcast(bf16[2,48,128]{2,1,0:T(8,128)(2,1)} %bitcast.29), dimensions={1,2,3} | broadcast | bytes 221184 | tf_op jit(solution)/shard_map/broadcast_in_dim | solution.py:439
  110.5 13.4 %all-to-all-start.2 = ((bf16[16,48,128]{2,1,0:T(8,128)(2,1)}), bf16[16,48,128]{2,1,0:T(8,128)(2,1)}, u32[]{:S(2)}, u32[]{:S(2)}) async-start(bf16[16,48,128]{2,1,0:T(8,128)(2,1)} %bitcast.26), calls=%async_computation.2 | async-start | bytes 393216 | tf_op jit(solution)/shard_map/all_to_all | solution.py:440
  123.9 0.0 collective-permute-done.5.dkv_in
  123.9 0.0 collective-permute-done.6.ctx_in
  123.9 0.0 collective-permute-done.4.dq_in
  123.9 6.0 %grad_tokens.1 = (bf16[256,1536]{1,0:T(8,128)(2,1)}, bf16[256,1536]{1,0:T(8,128)(2,1)}) custom-call(s32[2]{0:T(128)S(1)} %pad_add_fusion.core.place, bf16[256,768]{1,0:T(8,128)(2,1)S(1)} %get-tuple-element.31.dq, bf16[256,256]{1,0:T(8,128)(2,1)S(1)} %get-tuple-element.33.dkv, bf16[256,768]{1,0:T(8,128)(2,1)S(1)} %get-tuple-element.29.ctx, ...), custom_call_target="tpu_custom_call" | custom-call | flops 1610612736 | bytes 8388608 | tf_op jit(solution)/shard_map/grad_tokens/pallas_call | solution.py:374
  129.9 2.4 %all-to-all-done.2 = bf16[16,48,128]{2,1,0:T(8,128)(2,1)} async-done(((bf16[16,48,128]{2,1,0:T(8,128)(2,1)}), bf16[16,48,128]{2,1,0:T(8,128)(2,1)}, u32[]{:S(2)}, u32[]{:S(2)}) %all-to-all-start.2) | async-done | bytes 196640 | tf_op jit(solution)/shard_map/all_to_all | solution.py:440
  132.3 0.8 slice.41
  133.1 0.6 reshape.33
  133.8 0.9 slice.40
  134.7 0.1 copy.12
  134.8 0.8 reshape.32
  (2 shorter events, 0.0 us)
Async XLA Ops:
  0.6 10.6 %collective-permute-start = (bf16[256,1536]{1,0:T(8,128)(2,1)}, bf16[256,1536]{1,0:T(8,128)(2,1)S(1)}, u32[]{:S(2)}, u32[]{:S(2)}) collective-permute-start(bf16[256,1536]{1,0:T(8,128)(2,1)} %bitcast.20), channel_id=1, source_target_pairs={{0,1},{1,0},{2,3},{3,2},{4,5},{5,4},{6,7},{7,6},{8,9},{9,8},{10,11... | collective-permute-start | bytes 2359304 | tf_op jit(solution)/shard_map/ppermute | solution.py:405
  5.0 10.3 %collective-permute-start.1 = (bf16[256,768]{1,0:T(8,128)(2,1)S(1)}, bf16[256,768]{1,0:T(8,128)(2,1)S(1)}, u32[]{:S(2)}, u32[]{:S(2)}) collective-permute-start(bf16[256,768]{1,0:T(8,128)(2,1)S(1)} %dynamic-slice_bitcast_fusion), channel_id=1, source_target_pairs={{0,1},{1,0},{2,3},{3,2},{4,5},{5,4},{6,7},{7,6},{8,9},{9,8},{10,11... | collective-permute-start | bytes 1179656 | tf_op jit(solution)/shard_map/ppermute | solution.py:405
  5.1 8.8 %slice-start = ((s8[4718592]{0:T(1024)(128)(4,1)}), s8[4194304]{0:T(1024)(128)(4,1)S(1)}, s32[]{:S(2)}) async-start(s8[4718592]{0:T(1024)(128)(4,1)} %bitcast.18), calls=%async_computation.3 | async-start | bytes 8388608
  5.2 1.6 %copy-start = (bf16[1536,512]{1,0:T(8,128)(2,1)S(1)}, bf16[1536,512]{1,0:T(8,128)(2,1)}, u32[]{:S(2)}) copy-start(bf16[1536,512]{1,0:T(8,128)(2,1)} %wkv.1) | copy-start | bytes 4718596
  6.7 1.2 copy-start.3
  8.0 3.3 %copy-start.1 = (bf16[1536,512]{1,0:T(8,128)(2,1)S(1)}, bf16[1536,512]{1,0:T(8,128)(2,1)}, u32[]{:S(2)}) copy-start(bf16[1536,512]{1,0:T(8,128)(2,1)} %wkv.1) | copy-start | bytes 4718596
  8.0 6.0 %slice-start.1 = ((s8[4718592]{0:T(1024)(128)(4,1)}), s8[524288]{0:T(1024)(128)(4,1)S(1)}, s32[]{:S(2)}) async-start(s8[4718592]{0:T(1024)(128)(4,1)} %bitcast.18), calls=%async_computation.4 | async-start | bytes 1048576
  12.3 5.4 %copy-start.6 = (bf16[1,256,1536]{2,1,0:T(8,128)(2,1)S(1)}, bf16[1,256,1536]{2,1,0:T(8,128)(2,1)}, u32[]{:S(2)}) copy-start(bf16[1,256,1536]{2,1,0:T(8,128)(2,1)} %param.9) | copy-start | bytes 2359300
  12.3 5.4 %copy-start.9 = (s32[1,8192]{1,0:T(1,128)S(1)}, s32[1,8192]{1,0:T(1,128)}, u32[]{:S(2)}) copy-start(s32[1,8192]{1,0:T(1,128)} %param.6) | copy-start | bytes 98308
  12.3 5.4 %collective-permute-start.2 = (bf16[384,256]{1,0:T(8,128)(2,1)S(1)}, bf16[384,256]{1,0:T(8,128)(2,1)S(1)}, u32[]{:S(2)}, u32[]{:S(2)}) collective-permute-start(bf16[384,256]{1,0:T(8,128)(2,1)S(1)} %get-tuple-element.19), channel_id=1, source_target_pairs={{0,2},{1,3},{2,4},{3,5},{4,6},{5,7},{6,8},{7,9},{8,10},{9,11},{10,... | collective-permute-start | bytes 589832 | tf_op jit(solution)/shard_map/ppermute | solution.py:420
  15.3 0.7 copy-start.7
  17.7 1.0 copy-start.8
  30.4 0.9 copy-start.4
  31.3 8.0 %collective-permute-start.3 = (bf16[384,256]{1,0:T(8,128)(2,1)S(1)}, bf16[384,256]{1,0:T(8,128)(2,1)S(1)}, u32[]{:S(2)}, u32[]{:S(2)}) collective-permute-start(bf16[384,256]{1,0:T(8,128)(2,1)S(1)} %get-tuple-element.22), channel_id=1, source_target_pairs={{2,0},{3,1},{4,2},{5,3},{6,4},{7,5},{8,6},{9,7},{10,8},{11,9},{12,... | collective-permute-start | bytes 589832 | tf_op jit(solution)/shard_map/ppermute | solution.py:426
  40.4 1.7 %copy-start.2 = (bf16[16,768,128]{2,1,0:T(8,128)(2,1)}, bf16[16,768,128]{2,1,0:T(8,128)(2,1)S(1)}, u32[]{:S(2)}) copy-start(bf16[16,768,128]{2,1,0:T(8,128)(2,1)S(1)} %get-tuple-element.27) | copy-start | bytes 9437188
  42.1 0.7 copy-start.5
  42.8 44.5 %all-to-all-start = ((bf16[16,768,128]{2,1,0:T(8,128)(2,1)}), bf16[16,768,128]{2,1,0:T(8,128)(2,1)}, u32[]{:S(2)}, u32[]{:S(2)}) async-start(bf16[16,768,128]{2,1,0:T(8,128)(2,1)} %copy-done.2), calls=%async_computation | async-start | bytes 6291456 | tf_op jit(solution)/shard_map/all_to_all | solution.py:435
  52.7 71.2 %collective-permute-start.6 = (bf16[256,768]{1,0:T(8,128)(2,1)}, bf16[256,768]{1,0:T(8,128)(2,1)S(1)}, u32[]{:S(2)}, u32[]{:S(2)}) collective-permute-start(bf16[256,768]{1,0:T(8,128)(2,1)} %get-tuple-element.28), channel_id=1, source_target_pairs={{0,1},{1,0},{2,3},{3,2},{4,5},{5,4},{6,7},{7,6},{8,9},{9,8},{10,11... | collective-permute-start | bytes 1179656 | tf_op jit(solution)/shard_map/ppermute | solution.py:405
  55.8 68.1 %collective-permute-start.4 = (bf16[256,768]{1,0:T(8,128)(2,1)}, bf16[256,768]{1,0:T(8,128)(2,1)S(1)}, u32[]{:S(2)}, u32[]{:S(2)}) collective-permute-start(bf16[256,768]{1,0:T(8,128)(2,1)} %get-tuple-element.30), channel_id=1, source_target_pairs={{0,1},{1,0},{2,3},{3,2},{4,5},{5,4},{6,7},{7,6},{8,9},{9,8},{10,11... | collective-permute-start | bytes 1179656 | tf_op jit(solution)/shard_map/ppermute | solution.py:405
  90.4 17.1 %all-to-all-start.1 = ((bf16[8,96,128]{2,1,0:T(8,128)(2,1)}), bf16[8,96,128]{2,1,0:T(8,128)(2,1)}, u32[]{:S(2)}, u32[]{:S(2)}) async-start(bf16[8,96,128]{2,1,0:T(8,128)(2,1)} %bitcast.8), calls=%async_computation.1 | async-start | bytes 393216 | tf_op jit(solution)/shard_map/all_to_all | solution.py:437
  99.7 24.2 %collective-permute-start.5 = (bf16[256,256]{1,0:T(8,128)(2,1)S(1)}, bf16[256,256]{1,0:T(8,128)(2,1)S(1)}, u32[]{:S(2)}, u32[]{:S(2)}) collective-permute-start(bf16[256,256]{1,0:T(8,128)(2,1)S(1)} %get-tuple-element.32), channel_id=1, source_target_pairs={{0,1},{1,0},{2,3},{3,2},{4,5},{5,4},{6,7},{7,6},{8,9},{9,8},{10,11... | collective-permute-start | bytes 393224 | tf_op jit(solution)/shard_map/ppermute | solution.py:405
  110.5 21.8 %all-to-all-start.2 = ((bf16[16,48,128]{2,1,0:T(8,128)(2,1)}), bf16[16,48,128]{2,1,0:T(8,128)(2,1)}, u32[]{:S(2)}, u32[]{:S(2)}) async-start(bf16[16,48,128]{2,1,0:T(8,128)(2,1)} %bitcast.26), calls=%async_computation.2 | async-start | bytes 393216 | tf_op jit(solution)/shard_map/all_to_all | solution.py:440

commit v2 on v1

v2 whole, which is shorter than its diff:
```python
import functools

import jax
import jax.numpy as jnp
from jax import lax
from jax.experimental import pallas as pl
from jax.experimental.pallas import tpu as pltpu
from jax.sharding import Mesh
from jax.sharding import PartitionSpec as P

HEAD_DIM = 128
GROUP = 6
KV_HEADS = 2
WINDOW = 512
BLOCK = 128
HALO = WINDOW - BLOCK
OWN = 256
PAIR = 2 * OWN
KEYS = HALO + PAIR
QCOLS = GROUP * HEAD_DIM
KVCOLS = 2 * HEAD_DIM
D = 1536
SCALE = HEAD_DIM ** (-0.5)
F32 = jnp.float32
BF16 = jnp.bfloat16
NT = (((1,), (1,)), ((), ()))
TN = (((0,), (0,)), ((), ()))
WIDE = 512
REST = 256
SLAB = 24
BIG = 60 * 1024 * 1024
MID = 12 * 1024 * 1024


def whole(shape):
    return pl.BlockSpec(shape, lambda *_: (0,) * len(shape))


def params(limit=BIG):
    return pltpu.CompilerParams(vmem_limit_bytes=limit)


def cost(flops, moved, trans=0):
    return pl.CostEstimate(flops=flops, bytes_accessed=moved, transcendentals=trans)


def nn(a, b):
    return jnp.dot(a, b, preferred_element_type=F32)


def nt(a, b):
    return lax.dot_general(a, b, NT, preferred_element_type=F32)


def tn(a, b):
    return lax.dot_general(a, b, TN, preferred_element_type=F32)


def project_own_body(core, x, wq, wk, wv, q, kv):
    xv = x[...]
    q[...] = nn(xv, wq[...]).astype(BF16)

    @pl.when(pl.program_id(0) == 0)
    def _():
        kv[...] = nn(xv, jnp.concatenate([wk[...], wv[...]], axis=1)).astype(BF16)


def project_own(core, x, w_query, w_keyval):
    return pl.pallas_call(
        project_own_body,
        grid_spec=pltpu.PrefetchScalarGridSpec(
            num_scalar_prefetch=1,
            grid=(3,),
            in_specs=[
                whole((OWN, D)),
                pl.BlockSpec((D, 256), lambda i, c: (0, 3 * c[0] + i)),
                pl.BlockSpec((D, HEAD_DIM), lambda i, c: (0, c[0])),
                pl.BlockSpec((D, HEAD_DIM), lambda i, c: (0, KV_HEADS + c[0])),
            ],
            out_specs=[pl.BlockSpec((OWN, 256), lambda i, c: (0, i)), whole((OWN, KVCOLS))],
        ),
        out_shape=[
            jax.ShapeDtypeStruct((OWN, QCOLS), BF16),
            jax.ShapeDtypeStruct((OWN, KVCOLS), BF16),
        ],
        compiler_params=params(),
        cost_estimate=cost(2 * OWN * D * 1024, 4 << 20),
        name="project_own",
    )(core, x, w_query, w_keyval, w_keyval)


def project_kv_body(core, x, kv_own, wk, wv, kv, sent):
    c = core[0]
    other = nn(x[...], jnp.concatenate([wk[...], wv[...]], axis=1)).astype(BF16)
    own = kv_own[...]
    low = jnp.where(c == 0, own, other)
    high = jnp.where(c == 0, other, own)
    kv[:OWN] = low
    kv[OWN:] = high
    sent[: HALO - OWN] = low[PAIR - HALO :]
    sent[HALO - OWN :] = high


def project_kv(core, x, kv_own, w_keyval):
    return pl.pallas_call(
        project_kv_body,
        grid_spec=pltpu.PrefetchScalarGridSpec(
            num_scalar_prefetch=1,
            grid=(1,),
            in_specs=[
                whole((OWN, D)),
                whole((OWN, KVCOLS)),
                pl.BlockSpec((D, HEAD_DIM), lambda i, c: (0, c[0])),
                pl.BlockSpec((D, HEAD_DIM), lambda i, c: (0, KV_HEADS + c[0])),
            ],
            out_specs=[whole((PAIR, KVCOLS)), whole((HALO, KVCOLS))],
        ),
        out_shape=[
            jax.ShapeDtypeStruct((PAIR, KVCOLS), BF16),
            jax.ShapeDtypeStruct((HALO, KVCOLS), BF16),
        ],
        compiler_params=params(),
        cost_estimate=cost(2 * OWN * D * KVCOLS, 2 << 20),
        name="project_kv",
    )(core, x, kv_own, w_keyval, w_keyval)


def project_q_body(core, x, wq, q):
    q[...] = nn(x[...], wq[...]).astype(BF16)


def project_q(core, x, w_query):
    return pl.pallas_call(
        project_q_body,
        grid_spec=pltpu.PrefetchScalarGridSpec(
            num_scalar_prefetch=1,
            grid=(3,),
            in_specs=[whole((OWN, D)), pl.BlockSpec((D, 256), lambda i, c: (0, 3 * c[0] + i))],
            out_specs=pl.BlockSpec((OWN, 256), lambda i, c: (0, i)),
        ),
        out_shape=jax.ShapeDtypeStruct((OWN, QCOLS), BF16),
        compiler_params=params(),
        cost_estimate=cost(2 * OWN * D * QCOLS, 4 << 20),
        name="project_q",
    )(core, x, w_query)


def attend_body(
    start,
    width,
    more,
    place,
    q_own,
    q_oth,
    do_own,
    do_oth,
    kv,
    halo,
    segs,
    *rest,
):
    if more:
        dkv_in, mix_own, mix_oth, dkv_out, sent_out, keys, vals_t, keys_t, bias, dkv = rest
    else:
        mix_own, mix_oth, dkv_out, keys, vals_t, keys_t, bias, dkv = rest
    c = place[0]
    chip = place[1]
    b = pl.program_id(0)
    blocks = PAIR // BLOCK

    @pl.when(b == 0)
    def _():
        keys[:HALO] = halo[...]
        keys[HALO:] = kv[...]
        if more:
            dkv[...] = dkv_in[...]
        else:
            dkv[...] = jnp.zeros_like(dkv)
        for t in range(KEYS // BLOCK):
            rows = slice(t * BLOCK, (t + 1) * BLOCK)
            tile = keys[rows, :].astype(F32)
            keys_t[:, rows] = tile[:, :HEAD_DIM].T.astype(BF16)
            vals_t[:, rows] = tile[:, HEAD_DIM:].T.astype(BF16)
            row = chip * blocks - HALO // BLOCK + t
            line = segs[pl.ds(jnp.maximum(row, 0), 1), :]
            line = jnp.where(row >= 0, line, -1)
            bias[rows, :] = jnp.broadcast_to(line, (BLOCK, BLOCK)).T

    half = b // 2
    own = half == c
    inner = pl.multiple_of((b % 2) * BLOCK, BLOCK)
    here = pl.ds(inner, BLOCK)
    q_blk = jnp.where(own, q_own[here, :], q_oth[here, :])
    do_cols = slice(start, start + width)
    do_blk = jnp.where(own, do_own[here, do_cols], do_oth[here, do_cols])
    first = pl.multiple_of(b * BLOCK, BLOCK)
    win = pl.ds(first, WINDOW)
    k_win = keys[win, :HEAD_DIM]
    v_win = keys[win, HEAD_DIM:]
    kt_win = keys_t[:, win]
    vt_win = vals_t[:, win]
    query_ids = segs[pl.ds(chip * blocks + b, 1), :]
    j_pos = lax.broadcasted_iota(jnp.int32, (WINDOW, BLOCK), 0)
    i_pos = lax.broadcasted_iota(jnp.int32, (WINDOW, BLOCK), 1)
    seen = (bias[win, :] == query_ids) & (j_pos <= i_pos + HALO)
    seen2 = jnp.concatenate([seen, seen], axis=1)
    dk = jnp.zeros((WINDOW, HEAD_DIM), F32)
    dv = jnp.zeros((WINDOW, HEAD_DIM), F32)
    ctx_parts = []
    dq_parts = []
    for pair in range(width // 256):
        h0 = slice(2 * pair * HEAD_DIM, (2 * pair + 1) * HEAD_DIM)
        h1 = slice((2 * pair + 1) * HEAD_DIM, (2 * pair + 2) * HEAD_DIM)
        q2 = jnp.concatenate([q_blk[:, h0], q_blk[:, h1]], axis=0)
        do2 = jnp.concatenate([do_blk[:, h0], do_blk[:, h1]], axis=0)
        scores = jnp.where(seen2, nt(k_win, q2) * SCALE, -1e30)
        top = jnp.max(scores, axis=0, keepdims=True)
        expo = jnp.exp(scores - top)
        probs = expo * (1.0 / jnp.sum(expo, axis=0, keepdims=True))
        probs_low = probs.astype(BF16)
        ctx_t = nn(vt_win, probs_low).astype(BF16).astype(F32)
        delta = jnp.sum(do2.astype(F32).T * ctx_t, axis=0, keepdims=True)
        dp = nt(v_win, do2)
        ds = (probs * (dp - delta) * SCALE).astype(BF16)
        dv = dv + nn(probs_low, do2)
        dk = dk + nn(ds, q2)
        dq2 = nn(kt_win, ds).T
        ctx2 = ctx_t.T
        ctx_parts += [ctx2[:BLOCK], ctx2[BLOCK:]]
        dq_parts += [dq2[:BLOCK], dq2[BLOCK:]]
    mix = jnp.concatenate(ctx_parts + dq_parts, axis=1).astype(BF16)

    @pl.when(own)
    def _():
        mix_own[here, :] = mix

    @pl.when(jnp.logical_not(own))
    def _():
        mix_oth[here, :] = mix

    dkv[win, :] += jnp.concatenate([dk, dv], axis=1)

    @pl.when(b == blocks - 1)
    def _():
        if more:
            sent_out[...] = dkv[:HALO, :].astype(BF16)
            dkv_out[...] = dkv[HALO:, :]
        else:
            dkv_out[...] = dkv[...]


def attend(place, q_own, q_oth, do_own, do_oth, kv, halo, segs, dkv=None):
    more = dkv is not None
    start, width = (WIDE, REST) if more else (0, WIDE)
    mix = jax.ShapeDtypeStruct((OWN, 2 * width), BF16)
    outs = [mix, mix, jax.ShapeDtypeStruct((PAIR if more else KEYS, KVCOLS), F32)]
    if more:
        outs.append(jax.ShapeDtypeStruct((HALO, KVCOLS), BF16))
    extra = [dkv] if more else []
    return pl.pallas_call(
        functools.partial(attend_body, start, width, more),
        grid_spec=pltpu.PrefetchScalarGridSpec(
            num_scalar_prefetch=1,
            grid=(PAIR // BLOCK,),
            in_specs=[
                pl.BlockSpec((OWN, width), lambda i, p: (0, start // width)),
                pl.BlockSpec((OWN, width), lambda i, p: (0, start // width)),
                pl.BlockSpec((OWN, QCOLS), lambda i, p: (0, p[0])),
                pl.BlockSpec((OWN, QCOLS), lambda i, p: (0, p[0])),
                whole((PAIR, KVCOLS)),
                whole((HALO, KVCOLS)),
                whole(segs.shape),
            ]
            + [whole(v.shape) for v in extra],
            out_specs=[whole(o.shape) for o in outs],
            scratch_shapes=[
                pltpu.VMEM((KEYS, KVCOLS), BF16),
                pltpu.VMEM((HEAD_DIM, KEYS), BF16),
                pltpu.VMEM((HEAD_DIM, KEYS), BF16),
                pltpu.VMEM((KEYS, BLOCK), jnp.int32),
                pltpu.VMEM((KEYS, KVCOLS), F32),
            ],
        ),
        out_shape=outs,
        compiler_params=params(),
        cost_estimate=cost(2 * PAIR * WINDOW * width * 6, 4 << 20, PAIR * WINDOW * 6),
        name="attend_last" if more else "attend_first",
    )(place, q_own, q_oth, do_own, do_oth, kv, halo, segs, *extra)


def spread(value, out):
    for s in range(2):
        for y in range(4):
            for z in range(8):
                for core in range(2):
                    row = z * 192 + (y % 2) * 96 + core * 48 + (y // 2) * SLAB
                    piece = value[row : row + SLAB, s * HEAD_DIM : (s + 1) * HEAD_DIM]
                    out[s * 4 + y, z, core] = piece.astype(BF16)


PIECES = (16, 8, 2, SLAB, HEAD_DIM)


def weight_body(x_own, x_oth, g_own, g_oth, out):
    spread(tn(x_own[...], g_own[...]) + tn(x_oth[...], g_oth[...]), out)


def weight(x_own, x_oth, mix_own, mix_oth, first, steps):
    return pl.pallas_call(
        weight_body,
        grid=(steps,),
        in_specs=[
            whole((OWN, D)),
            whole((OWN, D)),
            pl.BlockSpec((OWN, 256), lambda i: (0, first + i)),
            pl.BlockSpec((OWN, 256), lambda i: (0, first + i)),
        ],
        out_specs=pl.BlockSpec((8,) + PIECES[1:], lambda i: (i, 0, 0, 0, 0)),
        out_shape=jax.ShapeDtypeStruct(PIECES, BF16),
        compiler_params=params(),
        cost_estimate=cost(2 * PAIR * D * 256 * steps, 4 << 20),
        name="weight_q",
    )(x_own, x_oth, mix_own, mix_oth)


def weight_kv_body(place, x_own, x_oth, dkv, arrived, before, out, own_out, oth_out):
    c = place[0]
    low = dkv[:OWN]
    skip = PAIR - HALO
    low = jnp.concatenate([low[:skip], low[skip:] + arrived[: OWN - skip].astype(F32)], axis=0)
    high = dkv[OWN:] + arrived[OWN - skip :].astype(F32)
    low = low.astype(BF16)
    high = high.astype(BF16)
    own = jnp.where(c == 0, low, high)
    oth = jnp.where(c == 0, high, low)
    own_out[...] = own
    oth_out[...] = oth
    spread(tn(x_own[...], own) + tn(x_oth[...], oth), out)


def weight_kv(place, x_own, x_oth, dkv, arrived, before):
    return pl.pallas_call(
        weight_kv_body,
        grid_spec=pltpu.PrefetchScalarGridSpec(
            num_scalar_prefetch=1,
            grid=(1,),
            in_specs=[
                whole((OWN, D)),
                whole((OWN, D)),
                whole((PAIR, KVCOLS)),
                whole((HALO, KVCOLS)),
                pl.BlockSpec(memory_space=pl.ANY),
            ],
            out_specs=[
                pl.BlockSpec((8,) + PIECES[1:], lambda i, p: (1, 0, 0, 0, 0)),
                whole((OWN, KVCOLS)),
                whole((OWN, KVCOLS)),
            ],
        ),
        out_shape=[
            jax.ShapeDtypeStruct(PIECES, BF16),
            jax.ShapeDtypeStruct((OWN, KVCOLS), BF16),
            jax.ShapeDtypeStruct((OWN, KVCOLS), BF16),
        ],
        input_output_aliases={5: 0},
        compiler_params=params(),
        cost_estimate=cost(2 * PAIR * D * KVCOLS, 3 << 20),
        name="weight_kv",
    )(place, x_own, x_oth, dkv, arrived, before)


def ordered(first, own, oth):
    return jnp.where(
        first, jnp.concatenate([own, oth], axis=1), jnp.concatenate([oth, own], axis=1)
    )


def grad_tokens_body(place, wide, slim, dkv, wide_in, slim_in, dkv_in, wq, wkv, out, ctx_out):
    first = place[0] == 0
    dq = jnp.concatenate([wide[:, WIDE:], slim[:, REST:]], axis=1)
    dq_in = jnp.concatenate([wide_in[:, WIDE:], slim_in[:, REST:]], axis=1)
    dq_full = ordered(first, dq, dq_in)
    kv = dkv[...]
    kv_in = dkv_in[...]
    keys = ordered(first, kv[:, :HEAD_DIM], kv_in[:, :HEAD_DIM])
    vals = ordered(first, kv[:, HEAD_DIM:], kv_in[:, HEAD_DIM:])
    kv_full = jnp.concatenate([keys, vals], axis=1)
    out[...] = (nt(dq_full, wq[...]) + nt(kv_full, wkv[...])).astype(BF16)

    @pl.when(pl.program_id(0) == 0)
    def _():
        ctx = jnp.concatenate([wide[:, :WIDE], slim[:, :REST]], axis=1)
        ctx_in = jnp.concatenate([wide_in[:, :WIDE], slim_in[:, :REST]], axis=1)
        ctx_out[...] = ordered(first, ctx, ctx_in)


def grad_tokens(place, wide, slim, dkv, wide_in, slim_in, dkv_in, w_query, w_keyval):
    step = 512
    return pl.pallas_call(
        grad_tokens_body,
        grid_spec=pltpu.PrefetchScalarGridSpec(
            num_scalar_prefetch=1,
            grid=(D // step,),
            in_specs=[whole(v.shape) for v in (wide, slim, dkv, wide_in, slim_in, dkv_in)]
            + [
                pl.BlockSpec((step, D), lambda i, p: (i, 0)),
                pl.BlockSpec((step, 512), lambda i, p: (i, 0)),
            ],
            out_specs=[
                pl.BlockSpec((OWN, step), lambda i, p: (0, i)),
                whole((OWN, D)),
            ],
        ),
        out_shape=[
            jax.ShapeDtypeStruct((OWN, D), BF16),
            jax.ShapeDtypeStruct((OWN, D), BF16),
        ],
        compiler_params=params(),
        cost_estimate=cost(2 * OWN * D * 2048, 8 << 20),
        name="grad_tokens",
    )(place, wide, slim, dkv, wide_in, slim_in, dkv_in, w_query, w_keyval)


PLANE = (8, 2, SLAB, HEAD_DIM)


def sum_first_body(pieces, after, out):
    out[...] = jnp.sum(pieces[...].astype(F32), axis=0).astype(BF16)


def sum_first(pieces, after):
    return pl.pallas_call(
        sum_first_body,
        grid=(4,),
        in_specs=[
            pl.BlockSpec((16, 2) + PIECES[2:], lambda i: (0, i, 0, 0, 0)),
            pl.BlockSpec(memory_space=pl.ANY),
        ],
        out_specs=pl.BlockSpec((2,) + PLANE[1:], lambda i: (i, 0, 0, 0)),
        out_shape=jax.ShapeDtypeStruct(PLANE, BF16),
        compiler_params=params(MID),
        cost_estimate=cost(16 * 8 * 2 * SLAB * HEAD_DIM, 2 << 20),
        name="sum_first",
    )(pieces, after)


def sum_last_body(pieces, plane, out):
    out[:, :, 0] = plane[...]
    out[:, :, 1] = jnp.sum(pieces[...].astype(F32), axis=0).astype(BF16)


def sum_last(pieces, plane):
    return pl.pallas_call(
        sum_last_body,
        grid=(4,),
        in_specs=[
            pl.BlockSpec((16, 2) + PIECES[2:], lambda i: (0, i, 0, 0, 0)),
            pl.BlockSpec((2,) + PLANE[1:], lambda i: (i, 0, 0, 0)),
        ],
        out_specs=pl.BlockSpec((2, 2, 2, SLAB, HEAD_DIM), lambda i: (i, 0, 0, 0, 0)),
        out_shape=jax.ShapeDtypeStruct((8, 2, 2, SLAB, HEAD_DIM), BF16),
        compiler_params=params(MID),
        cost_estimate=cost(16 * 8 * 2 * SLAB * HEAD_DIM, 2 << 20),
        name="sum_last",
    )(pieces, plane)


def sum_line_body(lines, out):
    out[...] = jnp.sum(lines[...].astype(F32), axis=0).astype(BF16)


def sum_line(lines):
    return pl.pallas_call(
        sum_line_body,
        in_specs=[pl.BlockSpec(memory_space=pltpu.VMEM)],
        out_specs=pl.BlockSpec(memory_space=pltpu.VMEM),
        out_shape=jax.ShapeDtypeStruct(lines.shape[1:], BF16),
        compiler_params=params(MID),
        name="sum_line",
    )(lines)


def finish_body(place, near, far, *rest):
    near_in, far_in, (query_w, keyval_w) = rest[:3], rest[3:6], rest[6:]
    x = place[2]
    flip = place[3] == 1
    nears = [near] + list(near_in)
    fars = [far] + list(far_in)
    for source in range(4):
        for core in range(2):
            for part in range(2):
                one = nears[0][core, part]
                two = fars[0][core, part]
                for d in range(1, 4):
                    hit = (source + d) % 4 == x
                    one = jnp.where(hit, nears[d][core, part], one)
                    two = jnp.where(hit, fars[d][core, part], two)
                one = one.astype(F32)
                two = two.astype(F32)
                rows = jnp.concatenate(
                    [jnp.where(flip, two, one), jnp.where(flip, one, two)], axis=0
                ).astype(BF16)
                if part == 0 or source < 2:
                    at = (core * GROUP + part * 4 + source) * HEAD_DIM
                    query_w[:, at : at + HEAD_DIM] = rows
                else:
                    at = ((source - 2) * KV_HEADS + core) * HEAD_DIM
                    keyval_w[:, at : at + HEAD_DIM] = rows


def finish(place, near, far, near_in, far_in):
    vmem = pl.BlockSpec(memory_space=pltpu.VMEM)
    return pl.pallas_call(
        finish_body,
        in_specs=[pl.BlockSpec(memory_space=pltpu.SMEM)] + [vmem] * 8,
        out_specs=[vmem, vmem],
        out_shape=[
            jax.ShapeDtypeStruct((48, D), BF16),
            jax.ShapeDtypeStruct((48, 512), BF16),
        ],
        compiler_params=params(MID),
        name="finish",
    )(place, near, far, *near_in, *far_in)


def swap(value):
    return lax.ppermute(value, "c", [(0, 1), (1, 0)])


def shards(tokens, segments, w_query, w_keyval, grad_context):
    x_own = tokens[0]
    do_own = grad_context[0]
    place = jnp.stack(
        [lax.axis_index("c"), lax.axis_index(("z", "yl")), lax.axis_index("x"), lax.axis_index("yh")]
    ).astype(jnp.int32)
    x_oth = swap(x_own)
    do_oth = swap(do_own)
    count = 32
    ring = ("z", "yl", "c")
    q_own, kv_own = project_own(place, x_own, w_query, w_keyval)
    kv, kv_sent = project_kv(place, x_oth, kv_own, w_keyval)
    halo = lax.ppermute(kv_sent, ring, [(i, i + 2) for i in range(count - 2)])
    q_oth = project_q(place, x_oth, w_query)
    segs = segments.reshape(-1, BLOCK)
    inputs = (place, q_own, q_oth, do_own, do_oth, kv, halo, segs)
    wide, wide_oth, dkv = attend(*inputs)
    pieces = weight(x_own, x_oth, wide, wide_oth, 2, 2)
    pieces = lax.all_to_all(pieces, ("x", "yh", "yl"), 0, 0)
    slim, slim_oth, dkv, dkv_sent = attend(*inputs, dkv)
    arrived = lax.ppermute(dkv_sent, ring, [(i + 2, i) for i in range(count - 2)])
    wide_in = swap(wide_oth)
    slim_in = swap(slim_oth)
    last = weight(x_own, x_oth, slim, slim_oth, 1, 1)
    last, dkv_own, dkv_oth = weight_kv(place, x_own, x_oth, dkv, arrived, last)
    last = lax.all_to_all(last, ("x", "yh", "yl"), 0, 0)
    dkv_in = swap(dkv_oth)
    grad_in, context = grad_tokens(
        place, wide, slim, dkv_own, wide_in, slim_in, dkv_in, w_query, w_keyval
    )
    plane = sum_first(pieces, grad_in)
    plane = sum_last(last, plane)
    lines = lax.all_to_all(plane.reshape(16, 2, SLAB, HEAD_DIM), ("z", "c"), 0, 0)
    near = sum_line(lines.reshape(8, 2, 2, SLAB, HEAD_DIM))
    far = lax.ppermute(near, "yh", [(0, 1), (1, 0)])
    turns = [[(i, (i + d) % 4) for i in range(4)] for d in range(1, 4)]
    near_in = [lax.ppermute(near, "x", turn) for turn in turns]
    far_in = [lax.ppermute(far, "x", turn) for turn in turns]
    query_w, keyval_w = finish(place, near, far, near_in, far_in)
    return context[None], grad_in[None], query_w, keyval_w


def solution(mesh):
    fine = Mesh(mesh.devices.reshape(4, 2, 8, 2, 2), ("x", "yh", "z", "yl", "c"))
    dp = ("x", "yh")
    ctx = ("z", "yl", "c")
    return jax.shard_map(
        shards,
        mesh=fine,
        in_specs=(P(dp, ctx, None), P(dp, None), P(), P(), P(dp, ctx, None)),
        out_specs=(P(dp, ctx, None), P(dp, ctx, None), P(ctx, None), P(ctx, None)),
        check_vma=False,
    )
```

time: 136 us -> 137 us (level)
  Pallas kernels: 26.4 us -> 52.7 us
  blocking collectives: 0 us -> 24.9 us
  waiting for transfers between devices: 40.4 us -> 22.2 us
  starting transfers between devices: 46 us -> 29.6 us
  local copies, waits for them, and re-layouts: 17.3 us -> 5.05 us
  other arithmetic: 4.69 us -> 0.61 us
    all_to_all x3 -> x2, waiting for transfers between devices: 34 us -> 7.4 us  [the longest x1 7.4 us: shards(): last = lax.all_to_all(last, ('x', 'yh', 'yl'), 0, 0)]
    all_to_all x0 -> x1, blocking collectives: none -> 24.9 us  [shards(): lax.all_to_all(plane.reshape(16, 2, SLAB, HEAD_DIM), ('z', 'c'), 0, 0)]
    all_to_all x3 -> x2, starting transfers between devices: 29.8 us -> 13.8 us  [the longest x1 7.09 us: shards(): pieces = lax.all_to_all(pieces, ('x', 'yh', 'yl'), 0, 0)]
    pallas_call x2 -> x8, Pallas kernels: 13.7 us -> 28.8 us  [the longest x2 20 us: attend(): pl.pallas_call(functools.partial(attend_body, start, width, more), grid_s...]
    ppermute x5, starting transfers between devices: 13.3 us -> 5.03 us  [swap(): return lax.ppermute(value, 'c', [(0, 1), (1, 0)])]
    ppermute x0 -> x7, starting transfers between devices: none -> 8.02 us  [the longest x3 4.4 us: shards(): near_in = [lax.ppermute(near, 'x', turn) for turn in turns]]
    ppermute x1, waiting for transfers between devices: 4.7 us -> 11.5 us  [shards(): lax.ppermute(dkv_sent, ring, [(i + 2, i) for i in range(count - 2)])]
    slice x5 -> x0, local copies, waits for them, and re-layouts: 5.42 us -> none  [the longest x1 1.91 us: shards(): ctx_in = swap(ctx[OWN:])]
  transfers between devices with their start and end apart: 10 -> 16, of which waited for: 5 -> 6; matrix products, arithmetic and copies ran while one was open for 8% -> 0% of each run, Pallas kernels for 10% -> 26%
where the time goes in v2:
time: 137 us; the launch traced here: 136 us
  Pallas kernels  52.7 us (38%)
  starting transfers between devices  29.6 us (22%)
  blocking collectives  24.9 us (18%)
  waiting for transfers between devices  22.2 us (16%)
  local copies, waits for them, and re-layouts  5.05 us (4%)
    all_to_all x1, blocking collectives, shards(): lax.all_to_all(plane.reshape(16, 2, SLAB, HEAD_DIM), ('z', 'c'), 0, 0)  24.9 us
    pallas_call x2, Pallas kernels, attend(): pl.pallas_call(functools.partial(attend_body, start, width, more), grid_s...  20 us
    ppermute x1, waiting for transfers between devices, shards(): lax.ppermute(dkv_sent, ring, [(i + 2, i) for i in range(count - 2)])  11.5 us
    all_to_all x1, waiting for transfers between devices, shards(): last = lax.all_to_all(last, ('x', 'yh', 'yl'), 0, 0)  7.4 us
    all_to_all x1, starting transfers between devices, shards(): pieces = lax.all_to_all(pieces, ('x', 'yh', 'yl'), 0, 0)  7.09 us
    pallas_call x1, Pallas kernels, grad_tokens(): pl.pallas_call(grad_tokens_body, grid_spec=pltpu.PrefetchScalarGridSpec(n...  6.88 us
    all_to_all x1, starting transfers between devices, shards(): last = lax.all_to_all(last, ('x', 'yh', 'yl'), 0, 0)  6.71 us
    pallas_call x2, Pallas kernels, weight(): pl.pallas_call(weight_body, grid=(steps,), in_specs=[whole((OWN, D)), who...  6.68 us
  transfers between devices with their start and end apart: 16, of which 6 were waited for; matrix products, arithmetic and copies ran while one was open for 0% of the time, Pallas kernels for 26%

profile of v2, /device:TPU:1, one launch (start us, length us, event | category | flops | bytes accessed | tf_op | source)
XLA Modules:
  0.0 135.7 jit_solution(14657663739133614938)
XLA Ops:
  0.6 3.3 %collective-permute-start = (bf16[256,1536]{1,0:T(8,128)(2,1)}, bf16[256,1536]{1,0:T(8,128)(2,1)S(1)}, u32[]{:S(2)}, u32[]{:S(2)}) collective-permute-start(bf16[256,1536]{1,0:T(8,128)(2,1)} %bitcast.14), channel_id=1, source_target_pairs={{0,1},{1,0},{2,3},{3,2},{4,5},{5,4},{6,7},{7,6},{8,9},{9,8},{10,11... | collective-permute-start | bytes 2359304 | tf_op jit(solution)/shard_map/ppermute | solution.py:527
  4.0 0.1 collective-permute-start.1
  4.1 0.6 pad_add_fusion.core.place
  4.7 5.3 %project_own.1 = (bf16[256,768]{1,0:T(8,128)(2,1)}, bf16[256,256]{1,0:T(8,128)(2,1)}) custom-call(s32[4]{0:T(128)} %pad_add_fusion.core.place, bf16[256,1536]{1,0:T(8,128)(2,1)} %bitcast.15, bf16[1536,1536]{1,0:T(8,128)(2,1)} %wq.5, bf16[1536,512]{1,0:T(8,128)(2,1)} %wkv.1, bf16[1536,512]{1,0:T(8,128)(2,1)} %wkv.1), custom_call_target="tpu_custom_call" | custom-call | flops 805306368 | bytes 4194304 | tf_op jit(solution)/shard_map/project_own/pallas_call | solution.py:69
  10.0 0.0 collective-permute-done.x.x_oth
  10.0 0.0 copy-start.2
  10.0 0.9 copy-done.2
  10.9 3.3 %project_kv.1 = (bf16[512,256]{1,0:T(8,128)(2,1)}, bf16[384,256]{1,0:T(8,128)(2,1)}) custom-call(s32[4]{0:T(128)} %pad_add_fusion.core.place, bf16[256,1536]{1,0:T(8,128)(2,1)} %copy-done.2, bf16[256,256]{1,0:T(8,128)(2,1)} %get-tuple-element.23.kv_own, bf16[1536,512]{1,0:T(8,128)(2,1)} %wkv.1, bf16[1536,512]{1,0:T(8,128)(2,1)} %wkv.1), custom_call_target="tpu_custom_call" | custom-call | flops 201326592 | bytes 2097152 | tf_op jit(solution)/shard_map/project_kv/pallas_call | solution.py:105
  14.1 1.5 %collective-permute-start.2 = (bf16[384,256]{1,0:T(8,128)(2,1)}, bf16[384,256]{1,0:T(8,128)(2,1)S(1)}, u32[]{:S(2)}, u32[]{:S(2)}) collective-permute-start(bf16[384,256]{1,0:T(8,128)(2,1)} %get-tuple-element.25), channel_id=1, source_target_pairs={{0,2},{1,3},{2,4},{3,5},{4,6},{5,7},{6,8},{7,9},{8,10},{9,11},{10,... | collective-permute-start | bytes 589832 | tf_op jit(solution)/shard_map/ppermute | solution.py:542
  15.6 4.7 %project_q.1.q_oth = bf16[256,768]{1,0:T(8,128)(2,1)} custom-call(s32[4]{0:T(128)} %pad_add_fusion.core.place, bf16[256,1536]{1,0:T(8,128)(2,1)} %copy-done.2, bf16[1536,1536]{1,0:T(8,128)(2,1)} %wq.5), custom_call_target="tpu_custom_call" | custom-call | flops 603979776 | bytes 4194304 | tf_op jit(solution)/shard_map/project_q/pallas_call | solution.py:133
  20.3 0.0 collective-permute-done.1.do_oth
  20.3 0.0 copy-start.3
  20.3 0.0 collective-permute-done.2.halo
  20.3 0.0 copy-start.7
  20.3 0.9 copy-done.3
  21.2 0.0 copy-done.7
  21.2 11.7 %attend_first.1 = (bf16[256,1024]{1,0:T(8,128)(2,1)}, bf16[256,1024]{1,0:T(8,128)(2,1)}, f32[896,256]{1,0:T(8,128)}) custom-call(s32[4]{0:T(128)} %pad_add_fusion.core.place, bf16[256,768]{1,0:T(8,128)(2,1)} %get-tuple-element.22.q_own, bf16[256,768]{1,0:T(8,128)(2,1)} %project_q.1.q_oth, bf16[256,1536]{1,0:T(8,128)(2,1)} %bitcast.20, ...), custom_call_target="tpu_custom_call" | custom-call | flops 1610612736 | bytes 4194304 | tf_op jit(solution)/shard_map/attend_first/pallas_call | solution.py:260
  32.9 3.7 %weight_q.3 = bf16[16,8,2,24,128]{4,3,2,1,0:T(8,128)(2,1)} custom-call(bf16[256,1536]{1,0:T(8,128)(2,1)} %bitcast.16, bf16[256,1536]{1,0:T(8,128)(2,1)} %copy-done.2, bf16[256,1024]{1,0:T(8,128)(2,1)} %get-tuple-element.26.wide.g_own, bf16[256,1024]{1,0:T(8,128)(2,1)} %get-tuple-element.33.g_oth), custom_call_target="tpu_custom_call" | custom-call | flops 805306368 | bytes 4194304 | tf_op jit(solution)/shard_map/weight_q/pallas_call | solution.py:309
  36.7 7.1 %all-to-all-start.1 = ((bf16[16,8,2,24,128]{4,3,2,1,0:T(8,128)(2,1)}), bf16[16,8,2,24,128]{4,3,2,1,0:T(8,128)(2,1)S(1)}, u32[]{:S(2)}, u32[]{:S(2)}) async-start(bf16[16,8,2,24,128]{4,3,2,1,0:T(8,128)(2,1)} %weight_q.3), calls=%async_computation.1 | async-start | bytes 3145728 | tf_op jit(solution)/shard_map/all_to_all | solution.py:548
  43.7 8.3 %attend_last.1 = (bf16[256,512]{1,0:T(8,128)(2,1)}, bf16[256,512]{1,0:T(8,128)(2,1)}, f32[512,256]{1,0:T(8,128)}, bf16[384,256]{1,0:T(8,128)(2,1)}) custom-call(s32[4]{0:T(128)} %pad_add_fusion.core.place, bf16[256,768]{1,0:T(8,128)(2,1)} %get-tuple-element.22.q_own, bf16[256,768]{1,0:T(8,128)(2,1)} %project_q.1.q_oth, bf16[256,1536]{1,0:T(8,128)(2,1)} %bitcast.21, ...), custom_call_target="tpu_custom_call" | custom-call | flops 805306368 | bytes 4194304 | tf_op jit(solution)/shard_map/attend_last/pallas_call | solution.py:260
  52.1 1.3 collective-permute-start.3
  53.3 2.9 %weight_q.2.before = bf16[16,8,2,24,128]{4,3,2,1,0:T(8,128)(2,1)} custom-call(bf16[256,1536]{1,0:T(8,128)(2,1)} %bitcast.17, bf16[256,1536]{1,0:T(8,128)(2,1)} %copy-done.2, bf16[256,512]{1,0:T(8,128)(2,1)} %get-tuple-element.28.g_own.slim, bf16[256,512]{1,0:T(8,128)(2,1)} %get-tuple-element.31.g_oth), custom_call_target="tpu_custom_call" | custom-call | flops 402653184 | bytes 4194304 | tf_op jit(solution)/shard_map/weight_q/pallas_call | solution.py:309
  56.3 11.5 %collective-permute-done.3.arrived = bf16[384,256]{1,0:T(8,128)(2,1)S(1)} collective-permute-done((bf16[384,256]{1,0:T(8,128)(2,1)}, bf16[384,256]{1,0:T(8,128)(2,1)S(1)}, u32[]{:S(2)}, u32[]{:S(2)}) %collective-permute-start.3) | collective-permute-done | bytes 196640 | tf_op jit(solution)/shard_map/ppermute | solution.py:550
  67.8 0.0 copy-start.8
  67.8 0.7 copy-done.8
  68.5 3.7 %weight_kv.1 = (bf16[16,8,2,24,128]{4,3,2,1,0:T(8,128)(2,1)}, bf16[256,256]{1,0:T(8,128)(2,1)}, bf16[256,256]{1,0:T(8,128)(2,1)}) custom-call(s32[4]{0:T(128)} %pad_add_fusion.core.place, bf16[256,1536]{1,0:T(8,128)(2,1)} %bitcast.18, bf16[256,1536]{1,0:T(8,128)(2,1)} %copy-done.2, ...), custom_call_target="tpu_custom_call", output_to_operand_aliasing={{0}: (5, {})} | custom-call | flops 402653184 | bytes 3145728 | tf_op jit(solution)/shard_map/weight_kv/pallas_call | solution.py:342
  72.2 0.0 all-to-all-done.1.pieces
  72.2 6.7 %all-to-all-start = ((bf16[16,8,2,24,128]{4,3,2,1,0:T(8,128)(2,1)}), bf16[16,8,2,24,128]{4,3,2,1,0:T(8,128)(2,1)S(1)}, u32[]{:S(2)}, u32[]{:S(2)}) async-start(bf16[16,8,2,24,128]{4,3,2,1,0:T(8,128)(2,1)} %get-tuple-element.37), calls=%async_computation | async-start | bytes 3145728 | tf_op jit(solution)/shard_map/all_to_all | solution.py:555
  78.9 1.1 collective-permute-start.4
  80.0 0.0 copy-done.5
  80.0 0.1 collective-permute-start.5
  80.1 0.4 collective-permute-start.6
  80.5 1.6 %collective-permute-done.5.slim_in = bf16[256,512]{1,0:T(8,128)(2,1)S(1)} collective-permute-done((bf16[256,512]{1,0:T(8,128)(2,1)S(1)}, bf16[256,512]{1,0:T(8,128)(2,1)S(1)}, u32[]{:S(2)}, u32[]{:S(2)}) %collective-permute-start.5) | collective-permute-done | bytes 262176 | tf_op jit(solution)/shard_map/ppermute | solution.py:527
  82.1 0.0 copy-start.6
  82.1 0.0 collective-permute-done.6.dkv_in
  82.2 0.0 copy-start.9
  82.2 0.0 collective-permute-done.4.wide_in
  82.2 0.7 copy-done.6
  82.8 0.0 copy-start.4
  82.8 0.1 copy-done.9
  82.9 0.7 copy-done.4
  83.6 6.9 %grad_tokens.1 = (bf16[256,1536]{1,0:T(8,128)(2,1)}, bf16[256,1536]{1,0:T(8,128)(2,1)}) custom-call(s32[4]{0:T(128)} %pad_add_fusion.core.place, bf16[256,1024]{1,0:T(8,128)(2,1)} %get-tuple-element.26.wide.g_own, bf16[256,512]{1,0:T(8,128)(2,1)} %get-tuple-element.28.g_own.slim, bf16[256,256]{1,0:T(8,128)(2,1)} %get-tuple-element.32.dkv, ...), custom_call_target="tpu_custom_call" | custom-call | flops 1610612736 | bytes 8388608 | tf_op jit(solution)/shard_map/grad_tokens/pallas_call | solution.py:399
  90.5 1.1 copy-done
  91.6 0.4 sum_first.1.plane
  92.0 0.0 copy-start.1
  92.0 7.4 %all-to-all-done.pieces = bf16[16,8,2,24,128]{4,3,2,1,0:T(8,128)(2,1)S(1)} async-done(((bf16[16,8,2,24,128]{4,3,2,1,0:T(8,128)(2,1)}), bf16[16,8,2,24,128]{4,3,2,1,0:T(8,128)(2,1)S(1)}, u32[]{:S(2)}, u32[]{:S(2)}) %all-to-all-start) | async-done | bytes 1572896 | tf_op jit(solution)/shard_map/all_to_all | solution.py:555
  99.4 0.4 sum_last.1
  99.9 24.9 %all_to_all.15 = bf16[16,2,24,128]{3,2,1,0:T(8,128)(2,1)S(1)} all-to-all(bf16[16,2,24,128]{3,2,1,0:T(8,128)(2,1)S(1)} %bitcast.11), channel_id=1, replica_groups=mesh['x'=4,'yh'=2,'z'=8,'yl'=2,'c'=2] {'z','c'}, dimensions={0} | all-to-all | bytes 393216 | tf_op jit(solution)/shard_map/all_to_all | solution.py:562
  124.8 0.3 collective-permute-start.7
  125.0 0.6 collective-permute-start.8
  125.6 1.7 %collective-permute-start.9 = (bf16[2,2,24,128]{3,2,1,0:T(8,128)(2,1)S(1)}, bf16[2,2,24,128]{3,2,1,0:T(8,128)(2,1)S(1)}, u32[]{:S(2)}, u32[]{:S(2)}) collective-permute-start(bf16[2,2,24,128]{3,2,1,0:T(8,128)(2,1)S(1)} %sum_line.1.near), channel_id=1, source_target_pairs={{0,128},{64,192},{128,0},{192,64},{1,129},{65,193},{129,1},{193,65... | collective-permute-start | bytes 73736 | tf_op jit(solution)/shard_map/ppermute | solution.py:566
  127.4 2.0 %collective-permute-start.10 = (bf16[2,2,24,128]{3,2,1,0:T(8,128)(2,1)S(1)}, bf16[2,2,24,128]{3,2,1,0:T(8,128)(2,1)S(1)}, u32[]{:S(2)}, u32[]{:S(2)}) collective-permute-start(bf16[2,2,24,128]{3,2,1,0:T(8,128)(2,1)S(1)} %sum_line.1.near), channel_id=1, source_target_pairs={{0,192},{64,0},{128,64},{192,128},{1,193},{65,1},{129,65},{193,129... | collective-permute-start | bytes 73736 | tf_op jit(solution)/shard_map/ppermute | solution.py:566
  129.4 0.0 collective-permute-done.7.far
  129.4 0.0 collective-permute-start.11
  129.4 1.7 %collective-permute-start.12 = (bf16[2,2,24,128]{3,2,1,0:T(8,128)(2,1)S(1)}, bf16[2,2,24,128]{3,2,1,0:T(8,128)(2,1)S(1)}, u32[]{:S(2)}, u32[]{:S(2)}) collective-permute-start(bf16[2,2,24,128]{3,2,1,0:T(8,128)(2,1)S(1)} %collective-permute-done.7.far), channel_id=1, source_target_pairs={{0,128},{64,192},{128,0},{192,64},{1,129},{65,193},{129,1},{193,65... | collective-permute-start | bytes 73736 | tf_op jit(solution)/shard_map/ppermute | solution.py:567
  131.2 0.0 collective-permute-done.8.rest_0_
  131.2 1.6 %collective-permute-start.13 = (bf16[2,2,24,128]{3,2,1,0:T(8,128)(2,1)S(1)}, bf16[2,2,24,128]{3,2,1,0:T(8,128)(2,1)S(1)}, u32[]{:S(2)}, u32[]{:S(2)}) collective-permute-start(bf16[2,2,24,128]{3,2,1,0:T(8,128)(2,1)S(1)} %collective-permute-done.7.far), channel_id=1, source_target_pairs={{0,192},{64,0},{128,64},{192,128},{1,193},{65,1},{129,65},{193,129... | collective-permute-start | bytes 73736 | tf_op jit(solution)/shard_map/ppermute | solution.py:567
  132.8 0.0 collective-permute-done.9.rest_1_
  132.8 0.0 collective-permute-done.10.rest_2_
  132.8 0.5 collective-permute-done.11.rest_3_
  133.3 0.4 collective-permute-done.12.rest_4_
  133.7 0.8 collective-permute-done.13.rest_5_
  134.4 0.0 copy-done.1
  134.4 1.3 finish.1
  (3 shorter events, 0.0 us)
Async XLA Ops:
  0.6 9.4 %collective-permute-start = (bf16[256,1536]{1,0:T(8,128)(2,1)}, bf16[256,1536]{1,0:T(8,128)(2,1)S(1)}, u32[]{:S(2)}, u32[]{:S(2)}) collective-permute-start(bf16[256,1536]{1,0:T(8,128)(2,1)} %bitcast.14), channel_id=1, source_target_pairs={{0,1},{1,0},{2,3},{3,2},{4,5},{5,4},{6,7},{7,6},{8,9},{9,8},{10,11... | collective-permute-start | bytes 2359304 | tf_op jit(solution)/shard_map/ppermute | solution.py:527
  4.0 16.3 %collective-permute-start.1 = (bf16[256,1536]{1,0:T(8,128)(2,1)}, bf16[256,1536]{1,0:T(8,128)(2,1)S(1)}, u32[]{:S(2)}, u32[]{:S(2)}) collective-permute-start(bf16[256,1536]{1,0:T(8,128)(2,1)} %bitcast.19), channel_id=1, source_target_pairs={{0,1},{1,0},{2,3},{3,2},{4,5},{5,4},{6,7},{7,6},{8,9},{9,8},{10,11... | collective-permute-start | bytes 2359304 | tf_op jit(solution)/shard_map/ppermute | solution.py:527
  10.0 0.9 copy-start.2
  14.1 6.2 %collective-permute-start.2 = (bf16[384,256]{1,0:T(8,128)(2,1)}, bf16[384,256]{1,0:T(8,128)(2,1)S(1)}, u32[]{:S(2)}, u32[]{:S(2)}) collective-permute-start(bf16[384,256]{1,0:T(8,128)(2,1)} %get-tuple-element.25), channel_id=1, source_target_pairs={{0,2},{1,3},{2,4},{3,5},{4,6},{5,7},{6,8},{7,9},{8,10},{9,11},{10,... | collective-permute-start | bytes 589832 | tf_op jit(solution)/shard_map/ppermute | solution.py:542
  20.3 0.9 copy-start.3
  20.3 0.9 copy-start.7
  36.7 35.6 %all-to-all-start.1 = ((bf16[16,8,2,24,128]{4,3,2,1,0:T(8,128)(2,1)}), bf16[16,8,2,24,128]{4,3,2,1,0:T(8,128)(2,1)S(1)}, u32[]{:S(2)}, u32[]{:S(2)}) async-start(bf16[16,8,2,24,128]{4,3,2,1,0:T(8,128)(2,1)} %weight_q.3), calls=%async_computation.1 | async-start | bytes 3145728 | tf_op jit(solution)/shard_map/all_to_all | solution.py:548
  52.1 15.8 %collective-permute-start.3 = (bf16[384,256]{1,0:T(8,128)(2,1)}, bf16[384,256]{1,0:T(8,128)(2,1)S(1)}, u32[]{:S(2)}, u32[]{:S(2)}) collective-permute-start(bf16[384,256]{1,0:T(8,128)(2,1)} %get-tuple-element.30), channel_id=1, source_target_pairs={{2,0},{3,1},{4,2},{5,3},{6,4},{7,5},{8,6},{9,7},{10,8},{11,9},{12,... | collective-permute-start | bytes 589832 | tf_op jit(solution)/shard_map/ppermute | solution.py:550
  67.8 0.7 copy-start.8
  72.2 7.8 %copy-start.5 = (bf16[256,512]{1,0:T(8,128)(2,1)S(1)}, bf16[256,512]{1,0:T(8,128)(2,1)}, u32[]{:S(2)}) copy-start(bf16[256,512]{1,0:T(8,128)(2,1)} %get-tuple-element.31.g_oth) | copy-start | bytes 786436
  72.2 27.2 %all-to-all-start = ((bf16[16,8,2,24,128]{4,3,2,1,0:T(8,128)(2,1)}), bf16[16,8,2,24,128]{4,3,2,1,0:T(8,128)(2,1)S(1)}, u32[]{:S(2)}, u32[]{:S(2)}) async-start(bf16[16,8,2,24,128]{4,3,2,1,0:T(8,128)(2,1)} %get-tuple-element.37), calls=%async_computation | async-start | bytes 3145728 | tf_op jit(solution)/shard_map/all_to_all | solution.py:555
  78.9 3.2 %collective-permute-start.4 = (bf16[256,1024]{1,0:T(8,128)(2,1)}, bf16[256,1024]{1,0:T(8,128)(2,1)S(1)}, u32[]{:S(2)}, u32[]{:S(2)}) collective-permute-start(bf16[256,1024]{1,0:T(8,128)(2,1)} %get-tuple-element.33.g_oth), channel_id=1, source_target_pairs={{0,1},{1,0},{2,3},{3,2},{4,5},{5,4},{6,7},{7,6},{8,9},{9,8},{10,11... | collective-permute-start | bytes 1572872 | tf_op jit(solution)/shard_map/ppermute | solution.py:527
  80.0 2.1 %collective-permute-start.5 = (bf16[256,512]{1,0:T(8,128)(2,1)S(1)}, bf16[256,512]{1,0:T(8,128)(2,1)S(1)}, u32[]{:S(2)}, u32[]{:S(2)}) collective-permute-start(bf16[256,512]{1,0:T(8,128)(2,1)S(1)} %copy-done.5), channel_id=1, source_target_pairs={{0,1},{1,0},{2,3},{3,2},{4,5},{5,4},{6,7},{7,6},{8,9},{9,8},{10,11... | collective-permute-start | bytes 786440 | tf_op jit(solution)/shard_map/ppermute | solution.py:527
  80.1 2.0 %collective-permute-start.6 = (bf16[256,256]{1,0:T(8,128)(2,1)}, bf16[256,256]{1,0:T(8,128)(2,1)S(1)}, u32[]{:S(2)}, u32[]{:S(2)}) collective-permute-start(bf16[256,256]{1,0:T(8,128)(2,1)} %get-tuple-element.34), channel_id=1, source_target_pairs={{0,1},{1,0},{2,3},{3,2},{4,5},{5,4},{6,7},{7,6},{8,9},{9,8},{10,11... | collective-permute-start | bytes 393224 | tf_op jit(solution)/shard_map/ppermute | solution.py:527
  82.1 0.7 copy-start.6
  82.2 0.7 copy-start.9
  82.8 0.8 copy-start.4
  90.5 1.1 copy-start
  92.0 42.4 %copy-start.1 = (s32[4]{0:T(128)S(1)}, s32[4]{0:T(128)}, u32[]{:S(2)}) copy-start(s32[4]{0:T(128)} %pad_add_fusion.core.place) | copy-start | bytes 52
  124.8 4.7 %collective-permute-start.7 = (bf16[2,2,24,128]{3,2,1,0:T(8,128)(2,1)S(1)}, bf16[2,2,24,128]{3,2,1,0:T(8,128)(2,1)S(1)}, u32[]{:S(2)}, u32[]{:S(2)}) collective-permute-start(bf16[2,2,24,128]{3,2,1,0:T(8,128)(2,1)S(1)} %sum_line.1.near), channel_id=1, source_target_pairs={{0,32},{32,0},{1,33},{33,1},{2,34},{34,2},{3,35},{35,3},{4,36},{36... | collective-permute-start | bytes 73736 | tf_op jit(solution)/shard_map/ppermute | solution.py:564
  125.0 6.2 %collective-permute-start.8 = (bf16[2,2,24,128]{3,2,1,0:T(8,128)(2,1)S(1)}, bf16[2,2,24,128]{3,2,1,0:T(8,128)(2,1)S(1)}, u32[]{:S(2)}, u32[]{:S(2)}) collective-permute-start(bf16[2,2,24,128]{3,2,1,0:T(8,128)(2,1)S(1)} %sum_line.1.near), channel_id=1, source_target_pairs={{0,64},{64,128},{128,192},{192,0},{1,65},{65,129},{129,193},{193,1... | collective-permute-start | bytes 73736 | tf_op jit(solution)/shard_map/ppermute | solution.py:566
  125.6 7.1 %collective-permute-start.9 = (bf16[2,2,24,128]{3,2,1,0:T(8,128)(2,1)S(1)}, bf16[2,2,24,128]{3,2,1,0:T(8,128)(2,1)S(1)}, u32[]{:S(2)}, u32[]{:S(2)}) collective-permute-start(bf16[2,2,24,128]{3,2,1,0:T(8,128)(2,1)S(1)} %sum_line.1.near), channel_id=1, source_target_pairs={{0,128},{64,192},{128,0},{192,64},{1,129},{65,193},{129,1},{193,65... | collective-permute-start | bytes 73736 | tf_op jit(solution)/shard_map/ppermute | solution.py:566
  127.4 5.4 %collective-permute-start.10 = (bf16[2,2,24,128]{3,2,1,0:T(8,128)(2,1)S(1)}, bf16[2,2,24,128]{3,2,1,0:T(8,128)(2,1)S(1)}, u32[]{:S(2)}, u32[]{:S(2)}) collective-permute-start(bf16[2,2,24,128]{3,2,1,0:T(8,128)(2,1)S(1)} %sum_line.1.near), channel_id=1, source_target_pairs={{0,192},{64,0},{128,64},{192,128},{1,193},{65,1},{129,65},{193,129... | collective-permute-start | bytes 73736 | tf_op jit(solution)/shard_map/ppermute | solution.py:566
  129.4 3.9 %collective-permute-start.11 = (bf16[2,2,24,128]{3,2,1,0:T(8,128)(2,1)S(1)}, bf16[2,2,24,128]{3,2,1,0:T(8,128)(2,1)S(1)}, u32[]{:S(2)}, u32[]{:S(2)}) collective-permute-start(bf16[2,2,24,128]{3,2,1,0:T(8,128)(2,1)S(1)} %collective-permute-done.7.far), channel_id=1, source_target_pairs={{0,64},{64,128},{128,192},{192,0},{1,65},{65,129},{129,193},{193,1... | collective-permute-start | bytes 73736 | tf_op jit(solution)/shard_map/ppermute | solution.py:567
  129.4 4.3 %collective-permute-start.12 = (bf16[2,2,24,128]{3,2,1,0:T(8,128)(2,1)S(1)}, bf16[2,2,24,128]{3,2,1,0:T(8,128)(2,1)S(1)}, u32[]{:S(2)}, u32[]{:S(2)}) collective-permute-start(bf16[2,2,24,128]{3,2,1,0:T(8,128)(2,1)S(1)} %collective-permute-done.7.far), channel_id=1, source_target_pairs={{0,128},{64,192},{128,0},{192,64},{1,129},{65,193},{129,1},{193,65... | collective-permute-start | bytes 73736 | tf_op jit(solution)/shard_map/ppermute | solution.py:567
  131.2 3.3 %collective-permute-start.13 = (bf16[2,2,24,128]{3,2,1,0:T(8,128)(2,1)S(1)}, bf16[2,2,24,128]{3,2,1,0:T(8,128)(2,1)S(1)}, u32[]{:S(2)}, u32[]{:S(2)}) collective-permute-start(bf16[2,2,24,128]{3,2,1,0:T(8,128)(2,1)S(1)} %collective-permute-done.7.far), channel_id=1, source_target_pairs={{0,192},{64,0},{128,64},{192,128},{1,193},{65,1},{129,65},{193,129... | collective-permute-start | bytes 73736 | tf_op jit(solution)/shard_map/ppermute | solution.py:567

commit v3 on v0

v3 whole, which is shorter than its diff:
```python
import functools

import jax
import jax.numpy as jnp
from jax import lax
from jax.experimental import pallas as pl
from jax.experimental.pallas import tpu as pltpu
from jax.sharding import Mesh
from jax.sharding import PartitionSpec as P

HEAD_DIM = 128
GROUP = 6
KV_HEADS = 2
WINDOW = 512
BLOCK = 128
HALO = WINDOW - BLOCK
OWN = 256
PAIR = 2 * OWN
KEYS = HALO + PAIR
QCOLS = GROUP * HEAD_DIM
KVCOLS = 2 * HEAD_DIM
D = 1536
DOCS = 8
SCALE = HEAD_DIM ** (-0.5)
LOG2E = 1.4426950408889634
F32 = jnp.float32
BF16 = jnp.bfloat16
NT = (((1,), (1,)), ((), ()))
TN = (((0,), (0,)), ((), ()))
ROWS = 48
PIECES = (32, 4, 2, ROWS, HEAD_DIM)
LIMIT = 24 * 1024 * 1024
VM = pl.BlockSpec(memory_space=pltpu.VMEM)
ANY = pl.BlockSpec(memory_space=pl.ANY)


def params():
    return pltpu.CompilerParams(vmem_limit_bytes=LIMIT)


def cost(flops, moved, trans=0):
    return pl.CostEstimate(flops=flops, bytes_accessed=moved, transcendentals=trans)


def shape(dims, dtype=BF16):
    return jax.ShapeDtypeStruct(dims, dtype)


def nn(a, b):
    return jnp.dot(a, b, preferred_element_type=F32)


def nt(a, b):
    return lax.dot_general(a, b, NT, preferred_element_type=F32)


def tn(a, b):
    return lax.dot_general(a, b, TN, preferred_element_type=F32)


def eye(size):
    row = lax.broadcasted_iota(jnp.int32, (size, size), 0)
    col = lax.broadcasted_iota(jnp.int32, (size, size), 1)
    return jnp.where(row == col, 1.0, 0.0).astype(BF16)


def columns(start, width=HEAD_DIM):
    return pl.ds(pl.multiple_of(start, HEAD_DIM), width)


def project_own_body(x, wkv, wq, x_here, wkv_here, wq_here, q, kv, sems):
    c = lax.axis_index("c")
    chunk = 512
    copies = [
        pltpu.make_async_copy(x, x_here, sems.at[0]),
        pltpu.make_async_copy(wkv, wkv_here, sems.at[1]),
    ]
    for j in range(D // chunk):
        rows = pl.ds(j * chunk, chunk)
        copies.append(
            pltpu.make_async_copy(
                wq.at[rows, columns(c * QCOLS, QCOLS)], wq_here.at[rows], sems.at[2 + j]
            )
        )
    for copy in copies:
        copy.start()
    copies[0].wait()
    copies[1].wait()
    kv[...] = nn(x_here[...], head_columns(wkv_here, c)).astype(BF16)
    total = jnp.zeros((OWN, QCOLS), F32)
    for j in range(D // chunk):
        rows = slice(j * chunk, (j + 1) * chunk)
        copies[2 + j].wait()
        total = total + nn(x_here[:, rows], wq_here[rows, :])
    q[...] = total.astype(BF16)


def head_columns(wkv, c):
    keys_w = wkv[:, columns(c * HEAD_DIM)]
    vals_w = wkv[:, columns((KV_HEADS + c) * HEAD_DIM)]
    return jnp.concatenate([keys_w, vals_w], axis=1)


def project_own(x, w_keyval, w_query):
    return pl.pallas_call(
        project_own_body,
        in_specs=[ANY] * 3,
        out_specs=[VM] * 5,
        out_shape=[
            pltpu.VMEM((OWN, D), BF16),
            pltpu.VMEM((D, 512), BF16),
            pltpu.VMEM((D, QCOLS), BF16),
            shape((OWN, QCOLS)),
            shape((OWN, KVCOLS)),
        ],
        scratch_shapes=[pltpu.SemaphoreType.DMA((5,))],
        compiler_params=params(),
        cost_estimate=cost(2 * OWN * D * 1024, 5 << 20),
        name="project_own",
    )(*(pltpu.with_memory_space_constraint(v, pltpu.HBM) for v in (x, w_keyval, w_query)))


def project_kv_body(x_oth, kv_own, w, kv, sent):
    c = lax.axis_index("c")
    own = kv_own[...]
    oth = nn(x_oth[...], head_columns(w, c)).astype(BF16)
    low = jnp.where(c == 0, own, oth)
    high = jnp.where(c == 0, oth, own)
    kv[:OWN] = low
    kv[OWN:] = high
    sent[: HALO - OWN] = low[PAIR - HALO :]
    sent[HALO - OWN :] = high


def project_kv(x_oth, kv_own, w_keyval):
    return pl.pallas_call(
        project_kv_body,
        in_specs=[VM] * 3,
        out_specs=[VM] * 2,
        out_shape=[shape((PAIR, KVCOLS)), shape((HALO, KVCOLS))],
        compiler_params=params(),
        cost_estimate=cost(2 * OWN * D * KVCOLS, 2 << 20),
        name="project_kv",
    )(x_oth, kv_own, w_keyval)


def project_q_body(x_oth, q_own, w, q):
    q[:OWN] = q_own[...]
    for j in range(3):
        cols = slice(j * 256, (j + 1) * 256)
        q[OWN:, cols] = nn(x_oth[...], w[:, cols]).astype(BF16)


def project_q(x_oth, q_own, w_query):
    return pl.pallas_call(
        project_q_body,
        in_specs=[VM] * 3,
        out_specs=VM,
        out_shape=shape((PAIR, QCOLS)),
        compiler_params=params(),
        cost_estimate=cost(2 * OWN * D * QCOLS, 4 << 20),
        name="project_q",
    )(x_oth, q_own, w_query)


def attend_block(b, c, chip, q, do_own, do_oth, keys, keys_t, vals_t, starts, segs, ones):
    half, inner = b // 2, (b % 2) * BLOCK
    own = half == c
    here = slice(inner, inner + BLOCK)
    q_rows = pl.ds(pl.multiple_of(jnp.where(own, 0, OWN) + inner, BLOCK), BLOCK)
    win = slice(b * BLOCK, b * BLOCK + WINDOW)
    k_win = keys[win, :HEAD_DIM]
    v_win = keys[win, HEAD_DIM:]
    v_more = jnp.concatenate([v_win, ones[:HEAD_DIM, :HEAD_DIM]], axis=0)
    kt_win = keys_t[:, win]
    vt_win = vals_t[:, win]
    line = segs[pl.ds(chip * (PAIR // BLOCK) + b, 1), :]
    lowest = jnp.zeros_like(line)
    for d in range(DOCS):
        lowest = jnp.where(line == d, starts[d], lowest)
    j_pos = lax.broadcasted_iota(jnp.int32, (WINDOW, BLOCK), 0)
    i_pos = lax.broadcasted_iota(jnp.int32, (WINDOW, BLOCK), 1)
    seen = (j_pos + b * BLOCK >= lowest) & (j_pos <= i_pos + HALO)
    bias = jnp.where(seen, 0.0, -1e30)
    bias = jnp.concatenate([bias, bias], axis=1)
    dk = jnp.zeros((WINDOW, HEAD_DIM), F32)
    dv = jnp.zeros((WINDOW, HEAD_DIM), F32)
    ctx_parts = []
    dq_parts = []
    for pair in range(GROUP // 2):
        at = pair * 256
        q_two = q[q_rows, at : at + 256]
        do_cols = columns(c * QCOLS + at, 256)
        do_two = jnp.where(own, do_own[here, do_cols], do_oth[here, do_cols])
        q2 = jnp.concatenate([q_two[:, :HEAD_DIM], q_two[:, HEAD_DIM:]], axis=0)
        do2 = jnp.concatenate([do_two[:, :HEAD_DIM], do_two[:, HEAD_DIM:]], axis=0)
        scores = nt(k_win, q2) + bias
        top = jnp.max(scores, axis=0, keepdims=True)
        expo = jnp.exp2((scores - top) * (SCALE * LOG2E))
        probs = expo * (1.0 / jnp.sum(expo, axis=0, keepdims=True))
        probs_low = probs.astype(BF16)
        ctx_t = nn(vt_win, probs_low).astype(BF16)
        dp = nt(v_more, do2)
        delta = jnp.sum(dp[WINDOW:] * ctx_t.astype(F32), axis=0, keepdims=True)
        ds = (probs * (dp[:WINDOW] - delta) * SCALE).astype(BF16)
        dv = dv + nn(probs_low, do2)
        dk = dk + nn(ds, q2)
        dq_t = nn(kt_win, ds).astype(BF16)
        turned = nt(ones, jnp.concatenate([ctx_t, dq_t], axis=0)).astype(BF16)
        ctx_parts += [turned[:BLOCK, :HEAD_DIM], turned[BLOCK:, :HEAD_DIM]]
        dq_parts += [turned[:BLOCK, HEAD_DIM:], turned[BLOCK:, HEAD_DIM:]]
    return jnp.concatenate(ctx_parts + dq_parts, axis=1), jnp.concatenate([dk, dv], axis=1)


def turn_keys(ones, keys, keys_t, vals_t, rows):
    small = ones[:HEAD_DIM, :HEAD_DIM]
    keys_t[:, rows] = nt(small, keys[rows, :HEAD_DIM]).astype(BF16)
    vals_t[:, rows] = nt(small, keys[rows, HEAD_DIM:]).astype(BF16)


def document_starts(chip, segs):
    lines = []
    for t in range(KEYS // BLOCK):
        row = chip * (PAIR // BLOCK) - HALO // BLOCK + t
        line = segs[pl.ds(jnp.maximum(row, 0), 1), :]
        lines.append(jnp.where(row >= 0, line, -1))
    lines = jnp.concatenate(lines, axis=0)
    return [jnp.sum(jnp.where(lines < d, 1, 0)) for d in range(DOCS)]


def attend_last_body(q, do_own, do_oth, kv, segs, mix, dkv, keys, keys_t, vals_t):
    c = lax.axis_index("c")
    chip = lax.axis_index(("zh", "zl", "yl"))
    ones = eye(256)
    keys[HALO:] = kv[...]
    turn_keys(ones, keys, keys_t, vals_t, slice(HALO, KEYS))
    starts = document_starts(chip, segs)
    mix_block, dkv[...] = attend_block(
        3, c, chip, q, do_own, do_oth, keys, keys_t, vals_t, starts, segs, ones
    )
    mix[...] = mix_block


def attend_last(q, do_own, do_oth, kv, segs):
    return pl.pallas_call(
        attend_last_body,
        in_specs=[VM] * 5,
        out_specs=[VM] * 2,
        out_shape=[shape((BLOCK, 2 * QCOLS)), shape((WINDOW, KVCOLS), F32)],
        scratch_shapes=[
            pltpu.VMEM((KEYS, KVCOLS), BF16),
            pltpu.VMEM((HEAD_DIM, KEYS), BF16),
            pltpu.VMEM((HEAD_DIM, KEYS), BF16),
        ],
        compiler_params=params(),
        cost_estimate=cost(2 * BLOCK * WINDOW * QCOLS * 6, 3 << 20, BLOCK * WINDOW * GROUP),
        name="attend_last",
    )(q, do_own, do_oth, kv, segs)


def attend_body(
    q,
    do_own,
    do_oth,
    kv,
    halo,
    segs,
    mix_last,
    dkv_last,
    mix_own,
    mix_oth,
    dkv_out,
    sent_out,
    keys,
    keys_t,
    vals_t,
    dkv,
):
    c = lax.axis_index("c")
    chip = lax.axis_index(("zh", "zl", "yl"))
    ones = eye(256)
    keys[:HALO] = halo[...]
    keys[HALO:] = kv[...]
    turn_keys(ones, keys, keys_t, vals_t, slice(0, KEYS))
    starts = document_starts(chip, segs)
    dkv[:HALO] = jnp.zeros((HALO, KVCOLS), F32)
    dkv[HALO:] = dkv_last[...]

    def put(b, value):
        own = b // 2 == c
        here = slice((b % 2) * BLOCK, (b % 2 + 1) * BLOCK)

        @pl.when(own)
        def _():
            mix_own[here, :] = value

        @pl.when(jnp.logical_not(own))
        def _():
            mix_oth[here, :] = value

    for b in range(3):
        mix, grads = attend_block(
            b, c, chip, q, do_own, do_oth, keys, keys_t, vals_t, starts, segs, ones
        )
        dkv[b * BLOCK : b * BLOCK + WINDOW, :] += grads
        put(b, mix)
    put(3, mix_last[...])
    sent_out[...] = dkv[:HALO, :].astype(BF16)
    dkv_out[...] = dkv[HALO:, :]


def attend(q, do_own, do_oth, kv, halo, segs, mix_last, dkv_last):
    return pl.pallas_call(
        attend_body,
        in_specs=[VM] * 8,
        out_specs=[VM] * 4,
        out_shape=[
            shape((OWN, 2 * QCOLS)),
            shape((OWN, 2 * QCOLS)),
            shape((PAIR, KVCOLS), F32),
            shape((HALO, KVCOLS)),
        ],
        scratch_shapes=[
            pltpu.VMEM((KEYS, KVCOLS), BF16),
            pltpu.VMEM((HEAD_DIM, KEYS), BF16),
            pltpu.VMEM((HEAD_DIM, KEYS), BF16),
            pltpu.VMEM((KEYS, KVCOLS), F32),
        ],
        compiler_params=params(),
        cost_estimate=cost(3 * 2 * BLOCK * WINDOW * QCOLS * 6, 5 << 20, 3 * BLOCK * WINDOW * 6),
        name="attend",
    )(q, do_own, do_oth, kv, halo, segs, mix_last, dkv_last)


def spread(value, held):
    for s in range(2):
        for y in range(2):
            for zl in range(2):
                for zh in range(4):
                    for core in range(2):
                        row = (zh * 2 + zl) * 192 + y * 96 + core * ROWS
                        piece = value[row : row + ROWS, s * HEAD_DIM : (s + 1) * HEAD_DIM]
                        held[s * 4 + y * 2 + zl, zh, core] = piece.astype(BF16)


def weight_q_body(x_own, x_oth, mix_own, mix_oth, out, held, sems):
    copies = []
    for j in range(3):
        cols = slice(QCOLS + j * 256, QCOLS + (j + 1) * 256)
        value = tn(x_own[...], mix_own[:, cols]) + tn(x_oth[...], mix_oth[:, cols])
        spread(value, held.at[j])
        copy = pltpu.make_async_copy(held.at[j], out.at[pl.ds(8 * j, 8)], sems.at[j])
        copy.start()
        copies.append(copy)
    for copy in copies:
        copy.wait()


def weight_q(x_own, x_oth, mix_own, mix_oth):
    return pl.pallas_call(
        weight_q_body,
        in_specs=[VM] * 4,
        out_specs=ANY,
        out_shape=pltpu.HBM(PIECES, BF16),
        scratch_shapes=[
            pltpu.VMEM((3, 8) + PIECES[1:], BF16),
            pltpu.SemaphoreType.DMA((3,)),
        ],
        compiler_params=params(),
        cost_estimate=cost(2 * PAIR * D * QCOLS, 4 << 20),
        name="weight_q",
    )(x_own, x_oth, mix_own, mix_oth)


def weight_kv_body(x_own, x_oth, dkv, arrived, before, out, own_out, oth_out, held, sem):
    c = lax.axis_index("c")
    low = dkv[:OWN]
    skip = PAIR - HALO
    low = jnp.concatenate([low[:skip], low[skip:] + arrived[: OWN - skip].astype(F32)], axis=0)
    high = dkv[OWN:] + arrived[OWN - skip :].astype(F32)
    low = low.astype(BF16)
    high = high.astype(BF16)
    own = jnp.where(c == 0, low, high)
    oth = jnp.where(c == 0, high, low)
    own_out[...] = own
    oth_out[...] = oth
    spread(tn(x_own[...], own) + tn(x_oth[...], oth), held)
    copy = pltpu.make_async_copy(held, out.at[pl.ds(24, 8)], sem)
    copy.start()
    copy.wait()


def weight_kv(x_own, x_oth, dkv, arrived, before):
    return pl.pallas_call(
        weight_kv_body,
        in_specs=[VM] * 4 + [ANY],
        out_specs=[ANY, VM, VM],
        out_shape=[pltpu.HBM(PIECES, BF16), shape((OWN, KVCOLS)), shape((OWN, KVCOLS))],
        scratch_shapes=[pltpu.VMEM((8,) + PIECES[1:], BF16), pltpu.SemaphoreType.DMA],
        input_output_aliases={4: 0},
        compiler_params=params(),
        cost_estimate=cost(2 * PAIR * D * KVCOLS, 3 << 20),
        name="weight_kv",
    )(x_own, x_oth, dkv, arrived, before)


def ordered(first, own, oth):
    return jnp.where(
        first, jnp.concatenate([own, oth], axis=1), jnp.concatenate([oth, own], axis=1)
    )


def grad_tokens_body(mix, dkv, mix_in, dkv_in, wq, wkv, out, ctx_out, done):
    done[...] = jnp.zeros_like(done)
    first = lax.axis_index("c") == 0
    dq = ordered(first, mix[:, QCOLS:], mix_in[:, QCOLS:])
    kv = dkv[...]
    kv_in = dkv_in[...]
    keys = ordered(first, kv[:, :HEAD_DIM], kv_in[:, :HEAD_DIM])
    vals = ordered(first, kv[:, HEAD_DIM:], kv_in[:, HEAD_DIM:])
    kv_full = jnp.concatenate([keys, vals], axis=1)
    for j in range(3):
        rows = slice(j * 512, (j + 1) * 512)
        out[:, rows] = (nt(dq, wq[rows, :]) + nt(kv_full, wkv[rows, :])).astype(BF16)
    ctx_out[...] = ordered(first, mix[:, :QCOLS], mix_in[:, :QCOLS])


def grad_tokens(mix, dkv, mix_in, dkv_in, w_query, w_keyval):
    return pl.pallas_call(
        grad_tokens_body,
        in_specs=[VM] * 6,
        out_specs=[VM] * 3,
        out_shape=[shape((OWN, D)), shape((OWN, D)), shape((8, 128), F32)],
        compiler_params=params(),
        cost_estimate=cost(2 * OWN * D * 2048, 8 << 20),
        name="grad_tokens",
    )(mix, dkv, mix_in, dkv_in, w_query, w_keyval)


def sum_plane_body(pieces, after, out):
    out[...] = jnp.sum(pieces[...].astype(F32), axis=0).astype(BF16)


def sum_plane(pieces, after):
    return pl.pallas_call(
        sum_plane_body,
        in_specs=[VM, VM],
        out_specs=VM,
        out_shape=shape(PIECES[1:]),
        compiler_params=params(),
        cost_estimate=cost(32 * 8 * ROWS * HEAD_DIM, 3 << 20),
        name="sum_plane",
    )(pieces, after)


def sum_line_body(lines, out):
    total = jnp.sum(lines[...].astype(F32), axis=0).astype(BF16)
    for s in range(8):
        out[s] = total


def sum_line(lines):
    return pl.pallas_call(
        sum_line_body,
        in_specs=[VM],
        out_specs=VM,
        out_shape=shape((8, 2, ROWS, HEAD_DIM)),
        compiler_params=params(),
        name="sum_line",
    )(lines)


def finish_body(blocks, query_w, keyval_w):
    for s in range(8):
        for core in range(2):
            if s < GROUP:
                at = (core * GROUP + s) * HEAD_DIM
                query_w[:, at : at + HEAD_DIM] = blocks[s, core]
            else:
                at = ((s - GROUP) * KV_HEADS + core) * HEAD_DIM
                keyval_w[:, at : at + HEAD_DIM] = blocks[s, core]


def finish(blocks):
    return pl.pallas_call(
        finish_body,
        in_specs=[VM],
        out_specs=[VM, VM],
        out_shape=[shape((ROWS, D)), shape((ROWS, 512))],
        compiler_params=params(),
        name="finish",
    )(blocks)


def swap(value):
    return lax.ppermute(value, "c", [(0, 1), (1, 0)])


def shards(tokens, segments, w_query, w_keyval, grad_context):
    x_own = tokens[0]
    do_own = grad_context[0]
    x_oth = swap(x_own)
    do_oth = swap(do_own)
    count = 32
    ring = ("zh", "zl", "yl", "c")
    x_own, wkv_here, wq_here, q_own, kv_own = project_own(x_own, w_keyval, w_query)
    kv, kv_sent = project_kv(x_oth, kv_own, wkv_here)
    halo = lax.ppermute(kv_sent, ring, [(i, i + 2) for i in range(count - 2)])
    q = project_q(x_oth, q_own, wq_here)
    segs = segments.reshape(-1, BLOCK)
    mix_last, dkv_last = attend_last(q, do_own, do_oth, kv, segs)
    mix, mix_oth, dkv, dkv_sent = attend(q, do_own, do_oth, kv, halo, segs, mix_last, dkv_last)
    arrived = lax.ppermute(dkv_sent, ring, [(i + 2, i) for i in range(count - 2)])
    pieces = weight_q(x_own, x_oth, mix, mix_oth)
    pieces, dkv_own, dkv_oth = weight_kv(x_own, x_oth, dkv, arrived, pieces)
    pieces = lax.all_to_all(pieces, ("x", "yh", "yl", "zl"), 0, 0)
    mix_in = swap(mix_oth)
    dkv_in = swap(dkv_oth)
    grad_in, context, done = grad_tokens(mix, dkv_own, mix_in, dkv_in, w_query, w_keyval)
    plane = sum_plane(pieces, done)
    lines = lax.all_to_all(plane.reshape(8, ROWS, HEAD_DIM), ("zh", "c"), 0, 0)
    blocks = sum_line(lines.reshape(4, 2, ROWS, HEAD_DIM))
    blocks = lax.all_to_all(blocks, ("x", "yh"), 0, 0)
    query_w, keyval_w = finish(blocks)
    return context[None], grad_in[None], query_w, keyval_w


def solution(mesh):
    fine = Mesh(mesh.devices.reshape(4, 2, 4, 2, 2, 2), ("x", "yh", "zh", "zl", "yl", "c"))
    dp = ("x", "yh")
    ctx = ("zh", "zl", "yl", "c")
    return jax.shard_map(
        shards,
        mesh=fine,
        in_specs=(P(dp, ctx, None), P(dp, None), P(), P(), P(dp, ctx, None)),
        out_specs=(P(dp, ctx, None), P(dp, ctx, None), P(ctx, None), P(ctx, None)),
        check_vma=False,
    )
```

time: 328 us -> 117 us (0.36)
  the two profiles are of different devices: /device:TPU:64 before, /device:TPU:1 now
where the time goes in v3:
time: 117 us
  waiting for transfers between devices  38.1 us (33%)
  blocking collectives  28.7 us (25%)
  Pallas kernels  26.2 us (22%)
  starting transfers between devices  18.2 us (16%)
  local copies, waits for them, and re-layouts  4.9 us (4%)
    all_to_all x1, waiting for transfers between devices, shards(): pieces = lax.all_to_all(pieces, ('x', 'yh', 'yl', 'zl'), 0, 0)  32 us
    all_to_all x1, blocking collectives, shards(): lines = lax.all_to_all(plane.reshape(8, ROWS, HEAD_DIM), ('zh', 'c'), 0, 0)  19.2 us
    pallas_call x1, Pallas kernels, attend(): pl.pallas_call(attend_body, in_specs=[VM] * 8, out_specs=[VM] * 4, out_sh...  10.1 us
    all_to_all x1, starting transfers between devices, shards(): pieces = lax.all_to_all(pieces, ('x', 'yh', 'yl', 'zl'), 0, 0)  9.64 us
    all_to_all x1, blocking collectives, shards(): blocks = lax.all_to_all(blocks, ('x', 'yh'), 0, 0)  9.43 us
    ppermute x4, starting transfers between devices, swap(): return lax.ppermute(value, 'c', [(0, 1), (1, 0)])  5.75 us
    unnamed x14, local copies, waits for them, and re-layouts  4.9 us
    ppermute x1, waiting for transfers between devices, shards(): lax.ppermute(dkv_sent, ring, [(i + 2, i) for i in range(count - 2)])  3.92 us
  transfers between devices with their start and end apart: 7, of which 4 were waited for; matrix products, arithmetic and copies ran while one was open for 0% of the time, Pallas kernels for 12%

profile of v3, /device:TPU:1, one launch (start us, length us, event | category | flops | bytes accessed | tf_op | source)
XLA Modules:
  0.0 116.9 jit_solution(18001027234674802745)
XLA Ops:
  0.6 3.3 %collective-permute-start = (bf16[256,1536]{1,0:T(8,128)(2,1)}, bf16[256,1536]{1,0:T(8,128)(2,1)S(1)}, u32[]{:S(2)}, u32[]{:S(2)}) collective-permute-start(bf16[256,1536]{1,0:T(8,128)(2,1)} %bitcast.14), channel_id=1, source_target_pairs={{0,1},{1,0},{2,3},{3,2},{4,5},{5,4},{6,7},{7,6},{8,9},{9,8},{10,11... | collective-permute-start | bytes 2359304 | tf_op jit(solution)/shard_map/ppermute | solution.py:496
  4.0 0.1 collective-permute-start.1
  4.1 3.4 %project_own.1 = (bf16[256,1536]{1,0:T(8,128)(2,1)S(1)}, bf16[1536,512]{1,0:T(8,128)(2,1)S(1)}, bf16[1536,768]{1,0:T(8,128)(2,1)S(1)}, bf16[256,768]{1,0:T(8,128)(2,1)S(1)}, bf16[256,256]{1,0:T(8,128)(2,1)S(1)}) custom-call(bf16[256,1536]{1,0:T(8,128)(2,1)} %bitcast.15, bf16[1536,512]{1,0:T(8,128)(2,1)} %wkv.3, bf16[1536,1536]{1,0:T(8,128)(2,1)} %wq.3), custom_call_target="tpu_custom_call" | custom-call | flops 805306368 | bytes 5242880 | tf_op jit(solution)/shard_map/project_own/pallas_call | solution.py:105
  7.5 0.0 collective-permute-done.x_oth
  7.5 0.0 copy-start.5
  7.5 0.0 copy-start.6
  7.5 0.4 project_kv.1
  7.9 1.5 %collective-permute-start.2 = (bf16[384,256]{1,0:T(8,128)(2,1)S(1)}, bf16[384,256]{1,0:T(8,128)(2,1)S(1)}, u32[]{:S(2)}, u32[]{:S(2)}) collective-permute-start(bf16[384,256]{1,0:T(8,128)(2,1)S(1)} %get-tuple-element.30), channel_id=1, source_target_pairs={{0,2},{1,3},{2,4},{3,5},{4,6},{5,7},{6,8},{7,9},{8,10},{9,11},{10,... | collective-permute-start | bytes 589832 | tf_op jit(solution)/shard_map/ppermute | solution.py:508
  9.4 0.8 project_q.1.q
  10.2 0.0 collective-permute-done.1.do_oth
  10.2 0.0 copy-done.5
  10.2 0.0 copy-done.6
  10.2 3.3 %attend_last.1 = (bf16[128,1536]{1,0:T(8,128)(2,1)S(1)}, f32[512,256]{1,0:T(8,128)S(1)}) custom-call(bf16[512,768]{1,0:T(8,128)(2,1)S(1)} %project_q.1.q, bf16[256,1536]{1,0:T(8,128)(2,1)S(1)} %bitcast.8, bf16[256,1536]{1,0:T(8,128)(2,1)S(1)} %collective-permute-done.1.do_oth, bf16[512,256]{1,0:T(8,128)(2,1)S(1)} %get-tuple-element.29.kv, s32[64,128]{1,0:T(8,128)S(1)} %bitcast.12), custom_call_target="tpu_custom_call" | custom-call | flops 603979776 | bytes 3145728 | tf_op jit(solution)/shard_map/attend_last/pallas_call | solution.py:245
  13.5 0.0 collective-permute-done.2.halo
  13.5 10.1 %attend.1 = (bf16[256,1536]{1,0:T(8,128)(2,1)S(1)}, bf16[256,1536]{1,0:T(8,128)(2,1)S(1)}, f32[512,256]{1,0:T(8,128)S(1)}, bf16[384,256]{1,0:T(8,128)(2,1)S(1)}) custom-call(bf16[512,768]{1,0:T(8,128)(2,1)S(1)} %project_q.1.q, bf16[256,1536]{1,0:T(8,128)(2,1)S(1)} %bitcast.9, bf16[256,1536]{1,0:T(8,128)(2,1)S(1)} %collective-permute-done.1.do_oth, ...), custom_call_target="tpu_custom_call" | custom-call | flops 1811939328 | bytes 5242880 | tf_op jit(solution)/shard_map/attend/pallas_call | solution.py:313
  23.6 0.0 copy-start.2
  23.6 0.0 copy-start.4
  23.6 1.3 %collective-permute-start.3 = (bf16[384,256]{1,0:T(8,128)(2,1)S(1)}, bf16[384,256]{1,0:T(8,128)(2,1)S(1)}, u32[]{:S(2)}, u32[]{:S(2)}) collective-permute-start(bf16[384,256]{1,0:T(8,128)(2,1)S(1)} %get-tuple-element.36), channel_id=1, source_target_pairs={{2,0},{3,1},{4,2},{5,3},{6,4},{7,5},{8,6},{9,7},{10,8},{11,9},{12,... | collective-permute-start | bytes 589832 | tf_op jit(solution)/shard_map/ppermute | solution.py:513
  24.9 2.6 %weight_q.1.before = bf16[32,4,2,48,128]{4,3,2,1,0:T(8,128)(2,1)} custom-call(bf16[256,1536]{1,0:T(8,128)(2,1)S(1)} %get-tuple-element.34.x_own, bf16[256,1536]{1,0:T(8,128)(2,1)S(1)} %collective-permute-done.x_oth, bf16[256,1536]{1,0:T(8,128)(2,1)S(1)} %get-tuple-element.33.mix_own.mix, bf16[256,1536]{1,0:T(8,128)(2,1)S(1)} %get-tuple-element.37.mix_oth), custom_call_target="tpu_custom_call" | custom-call | flops 1207959552 | bytes 4194304 | tf_op jit(solution)/shard_map/weight_q/pallas_call | solution.py:360
  27.6 0.0 copy-done.2
  27.6 0.0 copy-done.4
  27.6 3.9 %collective-permute-done.3.arrived = bf16[384,256]{1,0:T(8,128)(2,1)S(1)} collective-permute-done((bf16[384,256]{1,0:T(8,128)(2,1)S(1)}, bf16[384,256]{1,0:T(8,128)(2,1)S(1)}, u32[]{:S(2)}, u32[]{:S(2)}) %collective-permute-start.3) | collective-permute-done | bytes 196640 | tf_op jit(solution)/shard_map/ppermute | solution.py:513
  31.5 1.5 %weight_kv.1 = (bf16[32,4,2,48,128]{4,3,2,1,0:T(8,128)(2,1)}, bf16[256,256]{1,0:T(8,128)(2,1)S(1)}, bf16[256,256]{1,0:T(8,128)(2,1)S(1)}) custom-call(bf16[256,1536]{1,0:T(8,128)(2,1)S(1)} %get-tuple-element.34.x_own, bf16[256,1536]{1,0:T(8,128)(2,1)S(1)} %collective-permute-done.x_oth, ...), custom_call_target="tpu_custom_call", output_to_operand_aliasing={{0}: (4, {})} | custom-call | flops 402653184 | bytes 3145728 | tf_op jit(solution)/shard_map/weight_kv/pallas_call | solution.py:394
  33.0 9.6 %all-to-all-start = ((bf16[32,4,2,48,128]{4,3,2,1,0:T(8,128)(2,1)}), bf16[32,4,2,48,128]{4,3,2,1,0:T(8,128)(2,1)S(1)}, u32[]{:S(2)}, u32[]{:S(2)}) async-start(bf16[32,4,2,48,128]{4,3,2,1,0:T(8,128)(2,1)} %get-tuple-element.42), calls=%async_computation | async-start | bytes 6291456 | tf_op jit(solution)/shard_map/all_to_all | solution.py:516
  42.7 2.2 %collective-permute-start.4 = (bf16[256,1536]{1,0:T(8,128)(2,1)}, bf16[256,1536]{1,0:T(8,128)(2,1)S(1)}, u32[]{:S(2)}, u32[]{:S(2)}) collective-permute-start(bf16[256,1536]{1,0:T(8,128)(2,1)} %copy-done.4), channel_id=1, source_target_pairs={{0,1},{1,0},{2,3},{3,2},{4,5},{5,4},{6,7},{7,6},{8,9},{9,8},{10,11... | collective-permute-start | bytes 2359304 | tf_op jit(solution)/shard_map/ppermute | solution.py:496
  44.9 0.1 collective-permute-start.5
  45.0 2.0 %collective-permute-done.5.dkv_in = bf16[256,256]{1,0:T(8,128)(2,1)S(1)} collective-permute-done((bf16[256,256]{1,0:T(8,128)(2,1)S(1)}, bf16[256,256]{1,0:T(8,128)(2,1)S(1)}, u32[]{:S(2)}, u32[]{:S(2)}) %collective-permute-start.5) | collective-permute-done | bytes 131104 | tf_op jit(solution)/shard_map/ppermute | solution.py:496
  47.0 0.1 collective-permute-done.4.mix_in
  47.2 0.0 copy-start
  47.2 2.3 %copy-done = bf16[1536,1536]{1,0:T(8,128)(2,1)S(1)} copy-done((bf16[1536,1536]{1,0:T(8,128)(2,1)S(1)}, bf16[1536,1536]{1,0:T(8,128)(2,1)}, u32[]{:S(2)}) %copy-start) | copy-done | bytes 4718616
  49.5 0.0 copy-start.1
  49.5 1.4 %copy-done.1 = bf16[1536,512]{1,0:T(8,128)(2,1)S(1)} copy-done((bf16[1536,512]{1,0:T(8,128)(2,1)S(1)}, bf16[1536,512]{1,0:T(8,128)(2,1)}, u32[]{:S(2)}) %copy-start.1) | copy-done | bytes 1572888
  50.9 0.0 copy-start.3
  50.9 1.1 copy-done.3
  52.0 3.0 %grad_tokens.1 = (bf16[256,1536]{1,0:T(8,128)(2,1)}, bf16[256,1536]{1,0:T(8,128)(2,1)}, f32[8,128]{1,0:T(8,128)S(1)}) custom-call(bf16[256,1536]{1,0:T(8,128)(2,1)S(1)} %copy-done.3, bf16[256,256]{1,0:T(8,128)(2,1)S(1)} %get-tuple-element.38.dkv, bf16[256,1536]{1,0:T(8,128)(2,1)S(1)} %collective-permute-done.4.mix_in, ...), custom_call_target="tpu_custom_call" | custom-call | flops 1610612736 | bytes 8388608 | tf_op jit(solution)/shard_map/grad_tokens/pallas_call | solution.py:429
  55.0 32.0 %all-to-all-done.pieces = bf16[32,4,2,48,128]{4,3,2,1,0:T(8,128)(2,1)S(1)} async-done(((bf16[32,4,2,48,128]{4,3,2,1,0:T(8,128)(2,1)}), bf16[32,4,2,48,128]{4,3,2,1,0:T(8,128)(2,1)S(1)}, u32[]{:S(2)}, u32[]{:S(2)}) %all-to-all-start) | async-done | bytes 3145760 | tf_op jit(solution)/shard_map/all_to_all | solution.py:516
  87.1 0.4 sum_plane.1
  87.5 19.2 %all_to_all.15 = bf16[8,48,128]{2,1,0:T(8,128)(2,1)S(1)} all-to-all(bf16[8,48,128]{2,1,0:T(8,128)(2,1)S(1)} %bitcast.10), channel_id=1, replica_groups=mesh['x'=4,'yh'=2,'zh'=4,'zl'=2,'yl'=2,'c'=2] {'zh','c'}, dimensions={0} | all-to-all | bytes 196608 | tf_op jit(solution)/shard_map/all_to_all | solution.py:521
  106.8 9.4 %all_to_all.16.blocks = bf16[8,2,48,128]{3,2,1,0:T(8,128)(2,1)S(1)} all-to-all(bf16[8,2,48,128]{3,2,1,0:T(8,128)(2,1)S(1)} %sum_line.1), channel_id=1, replica_groups=mesh['x'=4,'yh'=2,'zh'=4,'zl'=2,'yl'=2,'c'=2] {'x','yh'}, dimensions={0} | all-to-all | bytes 393216 | tf_op jit(solution)/shard_map/all_to_all | solution.py:523
  116.2 0.7 finish.1
  (1 shorter events, 0.0 us)
Async XLA Ops:
  0.6 6.9 %collective-permute-start = (bf16[256,1536]{1,0:T(8,128)(2,1)}, bf16[256,1536]{1,0:T(8,128)(2,1)S(1)}, u32[]{:S(2)}, u32[]{:S(2)}) collective-permute-start(bf16[256,1536]{1,0:T(8,128)(2,1)} %bitcast.14), channel_id=1, source_target_pairs={{0,1},{1,0},{2,3},{3,2},{4,5},{5,4},{6,7},{7,6},{8,9},{9,8},{10,11... | collective-permute-start | bytes 2359304 | tf_op jit(solution)/shard_map/ppermute | solution.py:496
  4.0 6.3 %collective-permute-start.1 = (bf16[256,1536]{1,0:T(8,128)(2,1)}, bf16[256,1536]{1,0:T(8,128)(2,1)S(1)}, u32[]{:S(2)}, u32[]{:S(2)}) collective-permute-start(bf16[256,1536]{1,0:T(8,128)(2,1)} %bitcast.7), channel_id=1, source_target_pairs={{0,1},{1,0},{2,3},{3,2},{4,5},{5,4},{6,7},{7,6},{8,9},{9,8},{10,11... | collective-permute-start | bytes 2359304 | tf_op jit(solution)/shard_map/ppermute | solution.py:496
  7.5 2.7 %copy-start.5 = (bf16[1,256,1536]{2,1,0:T(8,128)(2,1)S(1)}, bf16[1,256,1536]{2,1,0:T(8,128)(2,1)}, u32[]{:S(2)}) copy-start(bf16[1,256,1536]{2,1,0:T(8,128)(2,1)} %param.9) | copy-start | bytes 2359300
  7.5 2.7 %copy-start.6 = (s32[1,8192]{1,0:T(1,128)S(1)}, s32[1,8192]{1,0:T(1,128)}, u32[]{:S(2)}) copy-start(s32[1,8192]{1,0:T(1,128)} %param.6) | copy-start | bytes 98308
  7.9 5.6 %collective-permute-start.2 = (bf16[384,256]{1,0:T(8,128)(2,1)S(1)}, bf16[384,256]{1,0:T(8,128)(2,1)S(1)}, u32[]{:S(2)}, u32[]{:S(2)}) collective-permute-start(bf16[384,256]{1,0:T(8,128)(2,1)S(1)} %get-tuple-element.30), channel_id=1, source_target_pairs={{0,2},{1,3},{2,4},{3,5},{4,6},{5,7},{6,8},{7,9},{8,10},{9,11},{10,... | collective-permute-start | bytes 589832 | tf_op jit(solution)/shard_map/ppermute | solution.py:508
  23.6 4.0 %copy-start.2 = (bf16[256,1536]{1,0:T(8,128)(2,1)}, bf16[256,1536]{1,0:T(8,128)(2,1)S(1)}, u32[]{:S(2)}) copy-start(bf16[256,1536]{1,0:T(8,128)(2,1)S(1)} %get-tuple-element.33.mix_own.mix) | copy-start | bytes 2359300
  23.6 4.0 %copy-start.4 = (bf16[256,1536]{1,0:T(8,128)(2,1)}, bf16[256,1536]{1,0:T(8,128)(2,1)S(1)}, u32[]{:S(2)}) copy-start(bf16[256,1536]{1,0:T(8,128)(2,1)S(1)} %get-tuple-element.37.mix_oth) | copy-start | bytes 2359300
  23.6 7.9 %collective-permute-start.3 = (bf16[384,256]{1,0:T(8,128)(2,1)S(1)}, bf16[384,256]{1,0:T(8,128)(2,1)S(1)}, u32[]{:S(2)}, u32[]{:S(2)}) collective-permute-start(bf16[384,256]{1,0:T(8,128)(2,1)S(1)} %get-tuple-element.36), channel_id=1, source_target_pairs={{2,0},{3,1},{4,2},{5,3},{6,4},{7,5},{8,6},{9,7},{10,8},{11,9},{12,... | collective-permute-start | bytes 589832 | tf_op jit(solution)/shard_map/ppermute | solution.py:513
  33.0 54.0 %all-to-all-start = ((bf16[32,4,2,48,128]{4,3,2,1,0:T(8,128)(2,1)}), bf16[32,4,2,48,128]{4,3,2,1,0:T(8,128)(2,1)S(1)}, u32[]{:S(2)}, u32[]{:S(2)}) async-start(bf16[32,4,2,48,128]{4,3,2,1,0:T(8,128)(2,1)} %get-tuple-element.42), calls=%async_computation | async-start | bytes 6291456 | tf_op jit(solution)/shard_map/all_to_all | solution.py:516
  42.7 4.5 %collective-permute-start.4 = (bf16[256,1536]{1,0:T(8,128)(2,1)}, bf16[256,1536]{1,0:T(8,128)(2,1)S(1)}, u32[]{:S(2)}, u32[]{:S(2)}) collective-permute-start(bf16[256,1536]{1,0:T(8,128)(2,1)} %copy-done.4), channel_id=1, source_target_pairs={{0,1},{1,0},{2,3},{3,2},{4,5},{5,4},{6,7},{7,6},{8,9},{9,8},{10,11... | collective-permute-start | bytes 2359304 | tf_op jit(solution)/shard_map/ppermute | solution.py:496
  44.9 2.1 %collective-permute-start.5 = (bf16[256,256]{1,0:T(8,128)(2,1)S(1)}, bf16[256,256]{1,0:T(8,128)(2,1)S(1)}, u32[]{:S(2)}, u32[]{:S(2)}) collective-permute-start(bf16[256,256]{1,0:T(8,128)(2,1)S(1)} %get-tuple-element.39), channel_id=1, source_target_pairs={{0,1},{1,0},{2,3},{3,2},{4,5},{5,4},{6,7},{7,6},{8,9},{9,8},{10,11... | collective-permute-start | bytes 393224 | tf_op jit(solution)/shard_map/ppermute | solution.py:496
  47.2 2.3 %copy-start = (bf16[1536,1536]{1,0:T(8,128)(2,1)S(1)}, bf16[1536,1536]{1,0:T(8,128)(2,1)}, u32[]{:S(2)}) copy-start(bf16[1536,1536]{1,0:T(8,128)(2,1)} %wq.3) | copy-start | bytes 14155780
  49.5 1.4 %copy-start.1 = (bf16[1536,512]{1,0:T(8,128)(2,1)S(1)}, bf16[1536,512]{1,0:T(8,128)(2,1)}, u32[]{:S(2)}) copy-start(bf16[1536,512]{1,0:T(8,128)(2,1)} %wkv.3) | copy-start | bytes 4718596
  50.9 1.1 copy-start.3

commit v4 on v3

v4 whole, which is shorter than its diff:
```python
import functools

import jax
import jax.numpy as jnp
from jax import lax
from jax.experimental import pallas as pl
from jax.experimental.pallas import tpu as pltpu
from jax.sharding import Mesh
from jax.sharding import PartitionSpec as P

HEAD_DIM = 128
GROUP = 6
KV_HEADS = 2
WINDOW = 512
BLOCK = 128
HALO = WINDOW - BLOCK
OWN = 256
PAIR = 2 * OWN
KEYS = HALO + PAIR
QCOLS = GROUP * HEAD_DIM
KVCOLS = 2 * HEAD_DIM
D = 1536
DOCS = 8
SCALE = HEAD_DIM ** (-0.5)
LOG2E = 1.4426950408889634
F32 = jnp.float32
BF16 = jnp.bfloat16
NT = (((1,), (1,)), ((), ()))
TN = (((0,), (0,)), ((), ()))
ROWS = 48
SLAB = 24
WIDE = 512
REST = 256
PIECES = (32, 4, 2, SLAB, HEAD_DIM)
LIMIT = 24 * 1024 * 1024
VM = pl.BlockSpec(memory_space=pltpu.VMEM)
ANY = pl.BlockSpec(memory_space=pl.ANY)


def params():
    return pltpu.CompilerParams(vmem_limit_bytes=LIMIT)


def cost(flops, moved, trans=0):
    return pl.CostEstimate(flops=flops, bytes_accessed=moved, transcendentals=trans)


def shape(dims, dtype=BF16):
    return jax.ShapeDtypeStruct(dims, dtype)


def nn(a, b):
    return jnp.dot(a, b, preferred_element_type=F32)


def nt(a, b):
    return lax.dot_general(a, b, NT, preferred_element_type=F32)


def tn(a, b):
    return lax.dot_general(a, b, TN, preferred_element_type=F32)


def eye(size):
    row = lax.broadcasted_iota(jnp.int32, (size, size), 0)
    col = lax.broadcasted_iota(jnp.int32, (size, size), 1)
    return jnp.where(row == col, 1.0, 0.0).astype(BF16)


def columns(start, width=HEAD_DIM):
    return pl.ds(pl.multiple_of(start, HEAD_DIM), width)


def project_own_body(x, wkv, wq, x_here, wkv_here, wq_here, q, kv, sems):
    c = lax.axis_index("c")
    chunk = 512
    copies = [
        pltpu.make_async_copy(x, x_here, sems.at[0]),
        pltpu.make_async_copy(wkv, wkv_here, sems.at[1]),
    ]
    for j in range(D // chunk):
        rows = pl.ds(j * chunk, chunk)
        copies.append(
            pltpu.make_async_copy(
                wq.at[rows, columns(c * QCOLS, QCOLS)], wq_here.at[rows], sems.at[2 + j]
            )
        )
    for copy in copies:
        copy.start()
    copies[0].wait()
    copies[1].wait()
    kv[...] = nn(x_here[...], head_columns(wkv_here, c)).astype(BF16)
    total = jnp.zeros((OWN, QCOLS), F32)
    for j in range(D // chunk):
        rows = slice(j * chunk, (j + 1) * chunk)
        copies[2 + j].wait()
        total = total + nn(x_here[:, rows], wq_here[rows, :])
    q[...] = total.astype(BF16)


def head_columns(wkv, c):
    keys_w = wkv[:, columns(c * HEAD_DIM)]
    vals_w = wkv[:, columns((KV_HEADS + c) * HEAD_DIM)]
    return jnp.concatenate([keys_w, vals_w], axis=1)


def project_own(x, w_keyval, w_query):
    return pl.pallas_call(
        project_own_body,
        in_specs=[ANY] * 3,
        out_specs=[VM] * 5,
        out_shape=[
            pltpu.VMEM((OWN, D), BF16),
            pltpu.VMEM((D, 512), BF16),
            pltpu.VMEM((D, QCOLS), BF16),
            shape((OWN, QCOLS)),
            shape((OWN, KVCOLS)),
        ],
        scratch_shapes=[pltpu.SemaphoreType.DMA((5,))],
        compiler_params=params(),
        cost_estimate=cost(2 * OWN * D * 1024, 5 << 20),
        name="project_own",
    )(*(pltpu.with_memory_space_constraint(v, pltpu.HBM) for v in (x, w_keyval, w_query)))


def project_kv_body(x_oth, kv_own, w, kv, sent):
    c = lax.axis_index("c")
    own = kv_own[...]
    oth = nn(x_oth[...], head_columns(w, c)).astype(BF16)
    low = jnp.where(c == 0, own, oth)
    high = jnp.where(c == 0, oth, own)
    kv[:OWN] = low
    kv[OWN:] = high
    sent[: HALO - OWN] = low[PAIR - HALO :]
    sent[HALO - OWN :] = high


def project_kv(x_oth, kv_own, w_keyval):
    return pl.pallas_call(
        project_kv_body,
        in_specs=[VM] * 3,
        out_specs=[VM] * 2,
        out_shape=[shape((PAIR, KVCOLS)), shape((HALO, KVCOLS))],
        compiler_params=params(),
        cost_estimate=cost(2 * OWN * D * KVCOLS, 2 << 20),
        name="project_kv",
    )(x_oth, kv_own, w_keyval)


def project_q_body(x_oth, q_own, w, q):
    q[:OWN] = q_own[...]
    for j in range(3):
        cols = slice(j * 256, (j + 1) * 256)
        q[OWN:, cols] = nn(x_oth[...], w[:, cols]).astype(BF16)


def project_q(x_oth, q_own, w_query):
    return pl.pallas_call(
        project_q_body,
        in_specs=[VM] * 3,
        out_specs=VM,
        out_shape=shape((PAIR, QCOLS)),
        compiler_params=params(),
        cost_estimate=cost(2 * OWN * D * QCOLS, 4 << 20),
        name="project_q",
    )(x_oth, q_own, w_query)


def attend_block(b, pairs, c, q, do_own, do_oth, keys, keys_t, vals_t, low, ones):
    half, inner = b // 2, (b % 2) * BLOCK
    own = half == c
    here = slice(inner, inner + BLOCK)
    q_rows = pl.ds(pl.multiple_of(jnp.where(own, 0, OWN) + inner, BLOCK), BLOCK)
    win = slice(b * BLOCK, b * BLOCK + WINDOW)
    k_win = keys[win, :HEAD_DIM]
    v_win = keys[win, HEAD_DIM:]
    v_more = jnp.concatenate([v_win, ones[:HEAD_DIM, :HEAD_DIM]], axis=0)
    kt_win = keys_t[:, win]
    vt_win = vals_t[:, win]
    j_pos = lax.broadcasted_iota(jnp.int32, (WINDOW, BLOCK), 0)
    i_pos = lax.broadcasted_iota(jnp.int32, (WINDOW, BLOCK), 1)
    seen = (j_pos + b * BLOCK >= low[b : b + 1, :]) & (j_pos <= i_pos + HALO)
    bias = jnp.where(seen, 0.0, -1e30)
    bias = jnp.concatenate([bias, bias], axis=1)
    q2s, do2s = [], []
    for pair in pairs:
        at = pair * 256
        q_two = q[q_rows, at : at + 256]
        do_cols = columns(c * QCOLS + at, 256)
        do_two = jnp.where(own, do_own[here, do_cols], do_oth[here, do_cols])
        q2s.append(jnp.concatenate([q_two[:, :HEAD_DIM], q_two[:, HEAD_DIM:]], axis=0))
        do2s.append(jnp.concatenate([do_two[:, :HEAD_DIM], do_two[:, HEAD_DIM:]], axis=0))
    raw = [nt(k_win, q2) for q2 in q2s]
    probs = []
    for scores in raw:
        scores = scores + bias
        top = jnp.max(scores, axis=0, keepdims=True)
        expo = jnp.exp2((scores - top) * (SCALE * LOG2E))
        probs.append(expo * (1.0 / jnp.sum(expo, axis=0, keepdims=True)))
    lows = [p.astype(BF16) for p in probs]
    dps = [nt(v_more, do2) for do2 in do2s]
    ctx_ts = [nn(vt_win, p).astype(BF16) for p in lows]
    deltas = [
        jnp.sum(dp[WINDOW:] * ctx_t.astype(F32), axis=0, keepdims=True)
        for dp, ctx_t in zip(dps, ctx_ts)
    ]
    dvs = [nn(p, do2) for p, do2 in zip(lows, do2s)]
    dss = [
        (p * (dp[:WINDOW] - delta) * SCALE).astype(BF16)
        for p, dp, delta in zip(probs, dps, deltas)
    ]
    dks = [nn(ds, q2) for ds, q2 in zip(dss, q2s)]
    dq_ts = [nn(kt_win, ds).astype(BF16) for ds in dss]
    ctx_parts, dq_parts = [], []
    for ctx_t, dq_t in zip(ctx_ts, dq_ts):
        turned = nt(ones, jnp.concatenate([ctx_t, dq_t], axis=0)).astype(BF16)
        ctx_parts += [turned[:BLOCK, :HEAD_DIM], turned[BLOCK:, :HEAD_DIM]]
        dq_parts += [turned[:BLOCK, HEAD_DIM:], turned[BLOCK:, HEAD_DIM:]]
    grads = jnp.concatenate([sum(dks[1:], dks[0]), sum(dvs[1:], dvs[0])], axis=1)
    return ctx_parts, dq_parts, grads


def turn_keys(ones, keys, keys_t, vals_t, rows):
    small = ones[:HEAD_DIM, :HEAD_DIM]
    keys_t[:, rows] = nt(small, keys[rows, :HEAD_DIM]).astype(BF16)
    vals_t[:, rows] = nt(small, keys[rows, HEAD_DIM:]).astype(BF16)


def lowest_keys(chip, segs, low):
    lines = []
    for t in range(KEYS // BLOCK):
        row = chip * (PAIR // BLOCK) - HALO // BLOCK + t
        line = segs[pl.ds(jnp.maximum(row, 0), 1), :]
        lines.append(jnp.where(row >= 0, line, -1))
    own = jnp.concatenate(lines[HALO // BLOCK :], axis=0)
    lines = jnp.concatenate(lines, axis=0)
    first = jnp.zeros_like(own)
    for d in range(DOCS):
        first = jnp.where(own == d, jnp.sum(jnp.where(lines < d, 1, 0)), first)
    low[: PAIR // BLOCK, :] = first


def attend_last_body(
    q, do_own, do_oth, kv, segs, wide, slim, dkv, low, keys, keys_t, vals_t
):
    c = lax.axis_index("c")
    chip = lax.axis_index(("zh", "zl", "yl"))
    ones = eye(256)
    keys[HALO:] = kv[...]
    turn_keys(ones, keys, keys_t, vals_t, slice(HALO, KEYS))
    lowest_keys(chip, segs, low)
    ctx, dq, dkv[...] = attend_block(
        3, range(3), c, q, do_own, do_oth, keys, keys_t, vals_t, low, ones
    )
    wide[...] = jnp.concatenate(ctx[:4] + dq[:4], axis=1)
    slim[...] = jnp.concatenate(ctx[4:] + dq[4:], axis=1)


KEY_SCRATCH = [
    pltpu.VMEM((KEYS, KVCOLS), BF16),
    pltpu.VMEM((HEAD_DIM, KEYS), BF16),
    pltpu.VMEM((HEAD_DIM, KEYS), BF16),
]


def attend_last(q, do_own, do_oth, kv, segs):
    return pl.pallas_call(
        attend_last_body,
        in_specs=[VM] * 5,
        out_specs=[VM] * 4,
        out_shape=[
            shape((BLOCK, 2 * WIDE)),
            shape((BLOCK, 2 * REST)),
            shape((WINDOW, KVCOLS), F32),
            shape((8, BLOCK), jnp.int32),
        ],
        scratch_shapes=KEY_SCRATCH,
        compiler_params=params(),
        cost_estimate=cost(2 * BLOCK * WINDOW * QCOLS * 6, 3 << 20, BLOCK * WINDOW * GROUP),
        name="attend_last",
    )(q, do_own, do_oth, kv, segs)


def put(c, b, mix_own, mix_oth, value):
    own = b // 2 == c
    here = slice((b % 2) * BLOCK, (b % 2 + 1) * BLOCK)

    @pl.when(own)
    def _():
        mix_own[here, :] = value

    @pl.when(jnp.logical_not(own))
    def _():
        mix_oth[here, :] = value


def attend_rest(pairs, q, do_own, do_oth, kv, halo, low, mix_last, mix_own, mix_oth, dkv, held):
    keys, keys_t, vals_t = held
    c = lax.axis_index("c")
    ones = eye(256)
    keys[:HALO] = halo[...]
    keys[HALO:] = kv[...]
    turn_keys(ones, keys, keys_t, vals_t, slice(0, KEYS))
    put(c, 3, mix_own, mix_oth, mix_last[...])
    for b in range(3):
        ctx, dq, grads = attend_block(
            b, pairs, c, q, do_own, do_oth, keys, keys_t, vals_t, low, ones
        )
        dkv[b * BLOCK : b * BLOCK + WINDOW, :] += grads
        put(c, b, mix_own, mix_oth, jnp.concatenate(ctx + dq, axis=1))


def attend_wide_body(q, do_own, do_oth, kv, halo, low, mix_last, dkv_in, *rest):
    mix_own, mix_oth, dkv, *held = rest
    dkv[:HALO] = jnp.zeros((HALO, KVCOLS), F32)
    dkv[HALO:] = dkv_in[...]
    attend_rest(
        range(2), q, do_own, do_oth, kv, halo, low, mix_last, mix_own, mix_oth, dkv, held
    )


def attend_wide(q, do_own, do_oth, kv, halo, low, mix_last, dkv_in):
    return pl.pallas_call(
        attend_wide_body,
        in_specs=[VM] * 8,
        out_specs=[VM] * 3,
        out_shape=[
            shape((OWN, 2 * WIDE)),
            shape((OWN, 2 * WIDE)),
            shape((KEYS, KVCOLS), F32),
        ],
        scratch_shapes=KEY_SCRATCH,
        compiler_params=params(),
        cost_estimate=cost(3 * 2 * BLOCK * WINDOW * WIDE * 6, 5 << 20, 3 * BLOCK * WINDOW * 4),
        name="attend_wide",
    )(q, do_own, do_oth, kv, halo, low, mix_last, dkv_in)


def attend_slim_body(q, do_own, do_oth, kv, halo, low, mix_last, dkv_in, *rest):
    mix_own, mix_oth, dkv_out, sent, dkv, *held = rest
    dkv[...] = dkv_in[...]
    attend_rest(
        range(2, 3), q, do_own, do_oth, kv, halo, low, mix_last, mix_own, mix_oth, dkv, held
    )
    sent[...] = dkv[:HALO, :].astype(BF16)
    dkv_out[...] = dkv[HALO:, :]


def attend_slim(q, do_own, do_oth, kv, halo, low, mix_last, dkv_in):
    return pl.pallas_call(
        attend_slim_body,
        in_specs=[VM] * 8,
        out_specs=[VM] * 4,
        out_shape=[
            shape((OWN, 2 * REST)),
            shape((OWN, 2 * REST)),
            shape((PAIR, KVCOLS), F32),
            shape((HALO, KVCOLS)),
        ],
        scratch_shapes=[pltpu.VMEM((KEYS, KVCOLS), F32)] + KEY_SCRATCH,
        compiler_params=params(),
        cost_estimate=cost(3 * 2 * BLOCK * WINDOW * REST * 6, 5 << 20, 3 * BLOCK * WINDOW * 2),
        name="attend_slim",
    )(q, do_own, do_oth, kv, halo, low, mix_last, dkv_in)


def spread(value, held):
    for s in range(2):
        for yh in range(2):
            for yl in range(2):
                for zl in range(2):
                    for zh in range(4):
                        for core in range(2):
                            row = (zh * 2 + zl) * 192 + yl * 96 + core * ROWS + yh * SLAB
                            piece = value[row : row + SLAB, s * HEAD_DIM : (s + 1) * HEAD_DIM]
                            held[s * 8 + yh * 4 + yl * 2 + zl, zh, core] = piece.astype(BF16)


def weight_q_body(first, kept, x_own, x_oth, mix_own, mix_oth, *rest):
    keep, out, copied = rest[: kept - 2], rest[kept - 2], rest[kept - 1 : -2]
    held, sems = rest[-2:]
    steps = held.shape[0]
    copies = []
    if copied:
        for i, (source, target) in enumerate(zip((mix_own, mix_oth) + keep, copied)):
            copies.append(pltpu.make_async_copy(source, target, sems.at[steps + i]))
            copies[-1].start()
    for j in range(steps):
        cols = slice(first + j * 256, first + (j + 1) * 256)
        value = tn(x_own[...], mix_own[:, cols]) + tn(x_oth[...], mix_oth[:, cols])
        spread(value, held.at[j])
        copy = pltpu.make_async_copy(held.at[j], out.at[pl.ds(16 * j, 16)], sems.at[j])
        copy.start()
        copies.append(copy)
    for copy in copies:
        copy.wait()


def weight_q(x_own, x_oth, mix_own, mix_oth, *keep):
    width = mix_own.shape[1] // 2
    steps = width // 256
    copied = (mix_own, mix_oth) + keep if keep else ()
    return pl.pallas_call(
        functools.partial(weight_q_body, width, len(keep) + 2),
        in_specs=[VM] * (4 + len(keep)),
        out_specs=[ANY] * (1 + len(copied)),
        out_shape=[pltpu.HBM(PIECES, BF16)] + [pltpu.HBM(v.shape, v.dtype) for v in copied],
        scratch_shapes=[
            pltpu.VMEM((steps, 16) + PIECES[1:], BF16),
            pltpu.SemaphoreType.DMA((steps + len(copied),)),
        ],
        compiler_params=params(),
        cost_estimate=cost(2 * PAIR * D * width, 4 << 20),
        name="weight_q",
    )(x_own, x_oth, mix_own, mix_oth, *keep)


def weight_kv_body(x_own, x_oth, dkv, arrived, before, out, own_out, oth_out, held, sem):
    c = lax.axis_index("c")
    low = dkv[:OWN]
    skip = PAIR - HALO
    low = jnp.concatenate([low[:skip], low[skip:] + arrived[: OWN - skip].astype(F32)], axis=0)
    high = dkv[OWN:] + arrived[OWN - skip :].astype(F32)
    low = low.astype(BF16)
    high = high.astype(BF16)
    own = jnp.where(c == 0, low, high)
    oth = jnp.where(c == 0, high, low)
    own_out[...] = own
    oth_out[...] = oth
    spread(tn(x_own[...], own) + tn(x_oth[...], oth), held)
    copy = pltpu.make_async_copy(held, out.at[pl.ds(16, 16)], sem)
    copy.start()
    copy.wait()


def weight_kv(x_own, x_oth, dkv, arrived, before):
    return pl.pallas_call(
        weight_kv_body,
        in_specs=[VM] * 4 + [ANY],
        out_specs=[ANY, VM, VM],
        out_shape=[pltpu.HBM(PIECES, BF16), shape((OWN, KVCOLS)), shape((OWN, KVCOLS))],
        scratch_shapes=[pltpu.VMEM((16,) + PIECES[1:], BF16), pltpu.SemaphoreType.DMA],
        input_output_aliases={4: 0},
        compiler_params=params(),
        cost_estimate=cost(2 * PAIR * D * KVCOLS, 3 << 20),
        name="weight_kv",
    )(x_own, x_oth, dkv, arrived, before)


def ordered(first, own, oth):
    return jnp.where(
        first, jnp.concatenate([own, oth], axis=1), jnp.concatenate([oth, own], axis=1)
    )


def grad_tokens_body(wide, slim, dkv, wide_in, slim_in, dkv_in, wq, wkv, out, ctx_out, done):
    done[...] = jnp.zeros_like(done)
    first = lax.axis_index("c") == 0
    dq = jnp.concatenate([wide[:, WIDE:], slim[:, REST:]], axis=1)
    dq_in = jnp.concatenate([wide_in[:, WIDE:], slim_in[:, REST:]], axis=1)
    dq = ordered(first, dq, dq_in)
    kv = dkv[...]
    kv_in = dkv_in[...]
    keys = ordered(first, kv[:, :HEAD_DIM], kv_in[:, :HEAD_DIM])
    vals = ordered(first, kv[:, HEAD_DIM:], kv_in[:, HEAD_DIM:])
    kv_full = jnp.concatenate([keys, vals], axis=1)
    for j in range(3):
        rows = slice(j * 512, (j + 1) * 512)
        out[:, rows] = (nt(dq, wq[rows, :]) + nt(kv_full, wkv[rows, :])).astype(BF16)
    ctx = jnp.concatenate([wide[:, :WIDE], slim[:, :REST]], axis=1)
    ctx_in = jnp.concatenate([wide_in[:, :WIDE], slim_in[:, :REST]], axis=1)
    ctx_out[...] = ordered(first, ctx, ctx_in)


def grad_tokens(wide, slim, dkv, wide_in, slim_in, dkv_in, w_query, w_keyval):
    return pl.pallas_call(
        grad_tokens_body,
        in_specs=[VM] * 8,
        out_specs=[VM] * 3,
        out_shape=[shape((OWN, D)), shape((OWN, D)), shape((8, 128), F32)],
        compiler_params=params(),
        cost_estimate=cost(2 * OWN * D * 2048, 8 << 20),
        name="grad_tokens",
    )(wide, slim, dkv, wide_in, slim_in, dkv_in, w_query, w_keyval)


def sum_first_body(pieces, after, out):
    out[...] = jnp.sum(pieces[...].astype(F32), axis=0).astype(BF16)


def sum_first(pieces, after):
    return pl.pallas_call(
        sum_first_body,
        in_specs=[VM, VM],
        out_specs=VM,
        out_shape=shape(PIECES[1:]),
        compiler_params=params(),
        cost_estimate=cost(32 * 8 * SLAB * HEAD_DIM, 2 << 20),
        name="sum_first",
    )(pieces, after)


def sum_last_body(pieces, plane, out):
    out[:, :, 0] = plane[...]
    out[:, :, 1] = jnp.sum(pieces[...].astype(F32), axis=0).astype(BF16)


def sum_last(pieces, plane):
    return pl.pallas_call(
        sum_last_body,
        in_specs=[VM, VM],
        out_specs=VM,
        out_shape=shape((4, 2, 2, SLAB, HEAD_DIM)),
        compiler_params=params(),
        cost_estimate=cost(32 * 8 * SLAB * HEAD_DIM, 2 << 20),
        name="sum_last",
    )(pieces, plane)


def sum_line_body(lines, out):
    total = jnp.sum(lines[...].astype(F32), axis=0).astype(BF16)
    for s in range(8):
        out[s] = total


def sum_line(lines):
    return pl.pallas_call(
        sum_line_body,
        in_specs=[VM],
        out_specs=VM,
        out_shape=shape((8, 2, 2, SLAB, HEAD_DIM)),
        compiler_params=params(),
        name="sum_line",
    )(lines)


def finish_body(blocks, query_w, keyval_w):
    for x in range(4):
        for core in range(2):
            for part in range(2):
                rows = jnp.concatenate(
                    [blocks[2 * x, core, part].astype(F32), blocks[2 * x + 1, core, part].astype(F32)],
                    axis=0,
                ).astype(BF16)
                if part == 0 or x < 2:
                    at = (core * GROUP + part * 4 + x) * HEAD_DIM
                    query_w[:, at : at + HEAD_DIM] = rows
                else:
                    at = ((x - 2) * KV_HEADS + core) * HEAD_DIM
                    keyval_w[:, at : at + HEAD_DIM] = rows


def finish(blocks):
    return pl.pallas_call(
        finish_body,
        in_specs=[VM],
        out_specs=[VM, VM],
        out_shape=[shape((ROWS, D)), shape((ROWS, 512))],
        compiler_params=params(),
        name="finish",
    )(blocks)


def swap(value):
    return lax.ppermute(value, "c", [(0, 1), (1, 0)])


def shards(tokens, segments, w_query, w_keyval, grad_context):
    x_own = tokens[0]
    do_own = grad_context[0]
    x_oth = swap(x_own)
    do_oth = swap(do_own)
    count = 32
    ring = ("zh", "zl", "yl", "c")
    x_own, wkv_here, wq_here, q_own, kv_own = project_own(x_own, w_keyval, w_query)
    kv, kv_sent = project_kv(x_oth, kv_own, wkv_here)
    halo = lax.ppermute(kv_sent, ring, [(i, i + 2) for i in range(count - 2)])
    q = project_q(x_oth, q_own, wq_here)
    segs = segments.reshape(-1, BLOCK)
    wide_last, slim_last, dkv, low = attend_last(q, do_own, do_oth, kv, segs)
    wide, wide_oth, dkv = attend_wide(q, do_own, do_oth, kv, halo, low, wide_last, dkv)
    target = ("x", "yh", "yl", "zl")
    pieces, wide, wide_oth, dkv = weight_q(x_own, x_oth, wide, wide_oth, dkv)
    pieces = lax.all_to_all(pieces, target, 0, 0)
    slim, slim_oth, dkv, dkv_sent = attend_slim(
        q, do_own, do_oth, kv, halo, low, slim_last, dkv
    )
    arrived = lax.ppermute(dkv_sent, ring, [(i + 2, i) for i in range(count - 2)])
    (last,) = weight_q(x_own, x_oth, slim, slim_oth)
    last, dkv_own, dkv_oth = weight_kv(x_own, x_oth, dkv, arrived, last)
    last = lax.all_to_all(last, target, 0, 0)
    wide_in = swap(wide_oth)
    slim_in = swap(slim_oth)
    dkv_in = swap(dkv_oth)
    grad_in, context, done = grad_tokens(
        wide, slim, dkv_own, wide_in, slim_in, dkv_in, w_query, w_keyval
    )
    plane = sum_last(last, sum_first(pieces, done))
    lines = lax.all_to_all(plane.reshape(8, 2, SLAB, HEAD_DIM), ("zh", "c"), 0, 0)
    blocks = sum_line(lines.reshape(4, 2, 2, SLAB, HEAD_DIM))
    blocks = lax.all_to_all(blocks, ("x", "yh"), 0, 0)
    query_w, keyval_w = finish(blocks)
    return context[None], grad_in[None], query_w, keyval_w


def solution(mesh):
    fine = Mesh(mesh.devices.reshape(4, 2, 4, 2, 2, 2), ("x", "yh", "zh", "zl", "yl", "c"))
    dp = ("x", "yh")
    ctx = ("zh", "zl", "yl", "c")
    return jax.shard_map(
        shards,
        mesh=fine,
        in_specs=(P(dp, ctx, None), P(dp, None), P(), P(), P(dp, ctx, None)),
        out_specs=(P(dp, ctx, None), P(dp, ctx, None), P(ctx, None), P(ctx, None)),
        check_vma=False,
    )
```

time: 117 us -> 117 us (level)
  waiting for transfers between devices: 38.1 us -> 27.2 us
  starting transfers between devices: 18.2 us -> 26.1 us
  local copies, waits for them, and re-layouts: 4.9 us -> 8.55 us
  blocking collectives: 28.7 us -> 27.4 us
    all_to_all x1 -> x2, waiting for transfers between devices: 32 us -> 13 us  [the longest x1 13 us: shards(): last = lax.all_to_all(last, target, 0, 0)]
    all_to_all x1 -> x2, starting transfers between devices: 9.64 us -> 18.4 us  [the longest x1 10.3 us: shards(): pieces = lax.all_to_all(pieces, target, 0, 0)]
    ppermute x1, waiting for transfers between devices: 3.92 us -> 11.7 us  [shards(): lax.ppermute(dkv_sent, ring, [(i + 2, i) for i in range(count - 2)])]
    unnamed x14 -> x28, local copies, waits for them, and re-layouts: 4.9 us -> 8.55 us
    all_to_all x1, blocking collectives: 19.2 us -> 18 us  [shards(): lax.all_to_all(plane.reshape(8, 2, SLAB, HEAD_DIM), ('zh', 'c'), 0, 0)]
    ppermute x4 -> x5, starting transfers between devices: 5.75 us -> 4.92 us  [swap(): return lax.ppermute(value, 'c', [(0, 1), (1, 0)])]
    pallas_call x5 -> x8, Pallas kernels: 19.4 us -> 19.7 us  [the longest x1 5.02 us: attend_wide(): pl.pallas_call(attend_wide_body, in_specs=[VM] * 8, out_specs=[VM] * 3, o...]
  transfers between devices with their start and end apart: 7 -> 9, of which waited for: 4 -> 5; matrix products, arithmetic and copies ran while one was open for 0% -> 0% of each run, Pallas kernels for 12% -> 16%
where the time goes in v4:
time: 117 us
  blocking collectives  27.4 us (23%)
  waiting for transfers between devices  27.2 us (23%)
  Pallas kernels  26.6 us (23%)
  starting transfers between devices  26.1 us (22%)
  local copies, waits for them, and re-layouts  8.55 us (7%)
    all_to_all x1, blocking collectives, shards(): lax.all_to_all(plane.reshape(8, 2, SLAB, HEAD_DIM), ('zh', 'c'), 0, 0)  18 us
    all_to_all x1, waiting for transfers between devices, shards(): last = lax.all_to_all(last, target, 0, 0)  13 us
    ppermute x1, waiting for transfers between devices, shards(): lax.ppermute(dkv_sent, ring, [(i + 2, i) for i in range(count - 2)])  11.7 us
    all_to_all x1, starting transfers between devices, shards(): pieces = lax.all_to_all(pieces, target, 0, 0)  10.3 us
    all_to_all x1, blocking collectives, shards(): blocks = lax.all_to_all(blocks, ('x', 'yh'), 0, 0)  9.43 us
    unnamed x28, local copies, waits for them, and re-layouts  8.55 us
    all_to_all x1, starting transfers between devices, shards(): last = lax.all_to_all(last, target, 0, 0)  8.08 us
    pallas_call x1, Pallas kernels, attend_wide(): pl.pallas_call(attend_wide_body, in_specs=[VM] * 8, out_specs=[VM] * 3, o...  5.02 us
  transfers between devices with their start and end apart: 9, of which 5 were waited for; matrix products, arithmetic and copies ran while one was open for 0% of the time, Pallas kernels for 16%

profile of v4, /device:TPU:1, one launch (start us, length us, event | category | flops | bytes accessed | tf_op | source)
XLA Modules:
  0.0 116.6 jit_solution(17958206072568397492)
XLA Ops:
  0.6 3.3 %collective-permute-start = (bf16[256,1536]{1,0:T(8,128)(2,1)}, bf16[256,1536]{1,0:T(8,128)(2,1)S(1)}, u32[]{:S(2)}, u32[]{:S(2)}) collective-permute-start(bf16[256,1536]{1,0:T(8,128)(2,1)} %bitcast.14), channel_id=1, source_target_pairs={{0,1},{1,0},{2,3},{3,2},{4,5},{5,4},{6,7},{7,6},{8,9},{9,8},{10,11... | collective-permute-start | bytes 2359304 | tf_op jit(solution)/shard_map/ppermute | solution.py:565
  4.0 0.1 collective-permute-start.1
  4.1 3.4 %project_own.1 = (bf16[256,1536]{1,0:T(8,128)(2,1)S(1)}, bf16[1536,512]{1,0:T(8,128)(2,1)S(1)}, bf16[1536,768]{1,0:T(8,128)(2,1)S(1)}, bf16[256,768]{1,0:T(8,128)(2,1)S(1)}, bf16[256,256]{1,0:T(8,128)(2,1)S(1)}) custom-call(bf16[256,1536]{1,0:T(8,128)(2,1)} %bitcast.15, bf16[1536,512]{1,0:T(8,128)(2,1)} %wkv.3, bf16[1536,1536]{1,0:T(8,128)(2,1)} %wq.3), custom_call_target="tpu_custom_call" | custom-call | flops 805306368 | bytes 5242880 | tf_op jit(solution)/shard_map/project_own/pallas_call | solution.py:108
  7.5 0.0 collective-permute-done.x_oth
  7.5 0.4 project_kv.1
  7.9 0.0 copy-start.5
  7.9 1.5 %collective-permute-start.2 = (bf16[384,256]{1,0:T(8,128)(2,1)S(1)}, bf16[384,256]{1,0:T(8,128)(2,1)S(1)}, u32[]{:S(2)}, u32[]{:S(2)}) collective-permute-start(bf16[384,256]{1,0:T(8,128)(2,1)S(1)} %get-tuple-element.40), channel_id=1, source_target_pairs={{0,2},{1,3},{2,4},{3,5},{4,6},{5,7},{6,8},{7,9},{8,10},{9,11},{10,... | collective-permute-start | bytes 589832 | tf_op jit(solution)/shard_map/ppermute | solution.py:577
  9.4 0.0 copy-start.2
  9.4 0.0 copy-start.12
  9.4 0.8 project_q.1.q
  10.2 0.0 collective-permute-done.1.do_oth
  10.2 0.0 copy-start.3
  10.3 0.3 copy-done.2
  10.6 0.0 copy-done.12
  10.6 2.0 %attend_last.1 = (bf16[128,1024]{1,0:T(8,128)(2,1)S(1)}, bf16[128,512]{1,0:T(8,128)(2,1)S(1)}, f32[512,256]{1,0:T(8,128)S(1)}, s32[8,128]{1,0:T(8,128)S(1)}) custom-call(bf16[512,768]{1,0:T(8,128)(2,1)S(1)} %project_q.1.q, bf16[256,1536]{1,0:T(8,128)(2,1)S(1)} %bitcast.8, bf16[256,1536]{1,0:T(8,128)(2,1)S(1)} %collective-permute-done.1.do_oth, ...), custom_call_target="tpu_custom_call" | custom-call | flops 603979776 | bytes 3145728 | tf_op jit(solution)/shard_map/attend_last/pallas_call | solution.py:267
  12.5 0.7 collective-permute-done.2.halo
  13.3 0.0 copy-start.10
  13.3 0.0 copy-done.5
  13.3 5.0 %attend_wide.1 = (bf16[256,1024]{1,0:T(8,128)(2,1)S(1)}, bf16[256,1024]{1,0:T(8,128)(2,1)S(1)}, f32[896,256]{1,0:T(8,128)S(1)}) custom-call(bf16[512,768]{1,0:T(8,128)(2,1)S(1)} %project_q.1.q, bf16[256,1536]{1,0:T(8,128)(2,1)S(1)} %bitcast.9, bf16[256,1536]{1,0:T(8,128)(2,1)S(1)} %collective-permute-done.1.do_oth, ...), custom_call_target="tpu_custom_call" | custom-call | flops 1207959552 | bytes 5242880 | tf_op jit(solution)/shard_map/attend_wide/pallas_call | solution.py:323
  18.3 0.0 copy-done.3
  18.3 0.0 copy-done.10
  18.3 2.2 %weight_q.2 = (bf16[32,4,2,24,128]{4,3,2,1,0:T(8,128)(2,1)}, bf16[256,1024]{1,0:T(8,128)(2,1)}, bf16[256,1024]{1,0:T(8,128)(2,1)}, f32[896,256]{1,0:T(8,128)}) custom-call(bf16[256,1536]{1,0:T(8,128)(2,1)S(1)} %get-tuple-element.34.x_own, bf16[256,1536]{1,0:T(8,128)(2,1)S(1)} %collective-permute-done.x_oth, bf16[256,1024]{1,0:T(8,128)(2,1)S(1)} %get-tuple-element.44.mix_own, ...), custom_call_target="tpu_custom_call" | custom-call | flops 805306368 | bytes 4194304 | tf_op jit(solution)/shard_map/weight_q/pallas_call | solution.py:403
  20.5 10.3 %all-to-all-start.1 = ((bf16[32,4,2,24,128]{4,3,2,1,0:T(8,128)(2,1)}), bf16[32,4,2,24,128]{4,3,2,1,0:T(8,128)(2,1)}, u32[]{:S(2)}, u32[]{:S(2)}) async-start(bf16[32,4,2,24,128]{4,3,2,1,0:T(8,128)(2,1)} %get-tuple-element.60), calls=%async_computation.1 | async-start | bytes 3145728 | tf_op jit(solution)/shard_map/all_to_all | solution.py:584
  30.8 0.0 copy-start.4
  30.9 1.1 copy-done.4
  32.0 0.0 copy-start.6
  32.0 0.9 copy-done.6
  32.9 0.0 copy-start.7
  32.9 1.2 %copy-done.7 = f32[896,256]{1,0:T(8,128)S(1)} copy-done((f32[896,256]{1,0:T(8,128)S(1)}, f32[896,256]{1,0:T(8,128)}, u32[]{:S(2)}) %copy-start.7) | copy-done | bytes 917528
  34.1 0.0 copy-start.11
  34.1 0.9 copy-done.11
  35.0 4.1 %attend_slim.1 = (bf16[256,512]{1,0:T(8,128)(2,1)S(1)}, bf16[256,512]{1,0:T(8,128)(2,1)S(1)}, f32[512,256]{1,0:T(8,128)S(1)}, bf16[384,256]{1,0:T(8,128)(2,1)S(1)}) custom-call(bf16[512,768]{1,0:T(8,128)(2,1)S(1)} %project_q.1.q, bf16[256,1536]{1,0:T(8,128)(2,1)S(1)} %bitcast.10, bf16[256,1536]{1,0:T(8,128)(2,1)S(1)} %copy-done.4, ...), custom_call_target="tpu_custom_call" | custom-call | flops 603979776 | bytes 5242880 | tf_op jit(solution)/shard_map/attend_slim/pallas_call | solution.py:350
  39.2 0.0 copy-start.9
  39.2 1.3 %collective-permute-start.3 = (bf16[384,256]{1,0:T(8,128)(2,1)S(1)}, bf16[384,256]{1,0:T(8,128)(2,1)S(1)}, u32[]{:S(2)}, u32[]{:S(2)}) collective-permute-start(bf16[384,256]{1,0:T(8,128)(2,1)S(1)} %get-tuple-element.52), channel_id=1, source_target_pairs={{2,0},{3,1},{4,2},{5,3},{6,4},{7,5},{8,6},{9,7},{10,8},{11,9},{12,... | collective-permute-start | bytes 589832 | tf_op jit(solution)/shard_map/ppermute | solution.py:588
  40.5 1.5 %weight_q.3.before = bf16[32,4,2,24,128]{4,3,2,1,0:T(8,128)(2,1)} custom-call(bf16[256,1536]{1,0:T(8,128)(2,1)S(1)} %get-tuple-element.34.x_own, bf16[256,1536]{1,0:T(8,128)(2,1)S(1)} %collective-permute-done.x_oth, bf16[256,512]{1,0:T(8,128)(2,1)S(1)} %get-tuple-element.50.mix_own.slim, bf16[256,512]{1,0:T(8,128)(2,1)S(1)} %get-tuple-element.53.mix_oth), custom_call_target="tpu_custom_call" | custom-call | flops 402653184 | bytes 4194304 | tf_op jit(solution)/shard_map/weight_q/pallas_call | solution.py:403
  42.0 0.0 copy-done.9
  42.0 11.7 %collective-permute-done.3.arrived = bf16[384,256]{1,0:T(8,128)(2,1)S(1)} collective-permute-done((bf16[384,256]{1,0:T(8,128)(2,1)S(1)}, bf16[384,256]{1,0:T(8,128)(2,1)S(1)}, u32[]{:S(2)}, u32[]{:S(2)}) %collective-permute-start.3) | collective-permute-done | bytes 196640 | tf_op jit(solution)/shard_map/ppermute | solution.py:588
  53.7 1.5 %weight_kv.1 = (bf16[32,4,2,24,128]{4,3,2,1,0:T(8,128)(2,1)}, bf16[256,256]{1,0:T(8,128)(2,1)S(1)}, bf16[256,256]{1,0:T(8,128)(2,1)S(1)}) custom-call(bf16[256,1536]{1,0:T(8,128)(2,1)S(1)} %get-tuple-element.34.x_own, bf16[256,1536]{1,0:T(8,128)(2,1)S(1)} %collective-permute-done.x_oth, ...), custom_call_target="tpu_custom_call", output_to_operand_aliasing={{0}: (4, {})} | custom-call | flops 402653184 | bytes 3145728 | tf_op jit(solution)/shard_map/weight_kv/pallas_call | solution.py:437
  55.2 0.0 copy-start.13
  55.2 0.6 copy-done.13
  55.9 0.0 all-to-all-done.1.pieces
  55.9 0.0 copy-start.1
  55.9 8.1 %all-to-all-start = ((bf16[32,4,2,24,128]{4,3,2,1,0:T(8,128)(2,1)}), bf16[32,4,2,24,128]{4,3,2,1,0:T(8,128)(2,1)S(1)}, u32[]{:S(2)}, u32[]{:S(2)}) async-start(bf16[32,4,2,24,128]{4,3,2,1,0:T(8,128)(2,1)} %get-tuple-element.59), calls=%async_computation | async-start | bytes 3145728 | tf_op jit(solution)/shard_map/all_to_all | solution.py:591
  64.0 1.0 collective-permute-start.4
  64.9 0.1 collective-permute-start.5
  65.0 0.4 collective-permute-start.6
  65.5 1.6 %collective-permute-done.5.slim_in = bf16[256,512]{1,0:T(8,128)(2,1)S(1)} collective-permute-done((bf16[256,512]{1,0:T(8,128)(2,1)}, bf16[256,512]{1,0:T(8,128)(2,1)S(1)}, u32[]{:S(2)}, u32[]{:S(2)}) %collective-permute-start.5) | collective-permute-done | bytes 262176 | tf_op jit(solution)/shard_map/ppermute | solution.py:565
  67.1 0.2 collective-permute-done.6.dkv_in
  67.3 0.0 collective-permute-done.4.wide_in
  67.3 0.0 copy-done.1
  67.3 0.0 copy-start
  67.3 2.3 %copy-done = bf16[1536,1536]{1,0:T(8,128)(2,1)S(1)} copy-done((bf16[1536,1536]{1,0:T(8,128)(2,1)S(1)}, bf16[1536,1536]{1,0:T(8,128)(2,1)}, u32[]{:S(2)}) %copy-start) | copy-done | bytes 4718616
  69.6 0.0 copy-start.8
  69.6 1.0 copy-done.8
  70.6 3.0 %grad_tokens.1 = (bf16[256,1536]{1,0:T(8,128)(2,1)}, bf16[256,1536]{1,0:T(8,128)(2,1)}, f32[8,128]{1,0:T(8,128)S(1)}) custom-call(bf16[256,1024]{1,0:T(8,128)(2,1)S(1)} %copy-done.8, bf16[256,512]{1,0:T(8,128)(2,1)S(1)} %get-tuple-element.50.mix_own.slim, bf16[256,256]{1,0:T(8,128)(2,1)S(1)} %get-tuple-element.54.dkv, ...), custom_call_target="tpu_custom_call" | custom-call | flops 1610612736 | bytes 8388608 | tf_op jit(solution)/shard_map/grad_tokens/pallas_call | solution.py:476
  73.7 1.6 %sum_first.1.plane = bf16[4,2,24,128]{3,2,1,0:T(8,128)(2,1)S(1)} custom-call(bf16[32,4,2,24,128]{4,3,2,1,0:T(8,128)(2,1)} %all-to-all-done.1.pieces, f32[8,128]{1,0:T(8,128)S(1)} %get-tuple-element.61.after), custom_call_target="tpu_custom_call" | custom-call | flops 786432 | bytes 2097152 | tf_op jit(solution)/shard_map/sum_first/pallas_call | solution.py:492
  75.3 13.0 %all-to-all-done.pieces = bf16[32,4,2,24,128]{4,3,2,1,0:T(8,128)(2,1)S(1)} async-done(((bf16[32,4,2,24,128]{4,3,2,1,0:T(8,128)(2,1)}), bf16[32,4,2,24,128]{4,3,2,1,0:T(8,128)(2,1)S(1)}, u32[]{:S(2)}, u32[]{:S(2)}) %all-to-all-start) | async-done | bytes 1572896 | tf_op jit(solution)/shard_map/all_to_all | solution.py:591
  88.3 0.2 sum_last.1
  88.5 18.0 %all_to_all.20 = bf16[8,2,24,128]{3,2,1,0:T(8,128)(2,1)S(1)} all-to-all(bf16[8,2,24,128]{3,2,1,0:T(8,128)(2,1)S(1)} %bitcast.12), channel_id=1, replica_groups=mesh['x'=4,'yh'=2,'zh'=4,'zl'=2,'yl'=2,'c'=2] {'zh','c'}, dimensions={0} | all-to-all | bytes 196608 | tf_op jit(solution)/shard_map/all_to_all | solution.py:599
  106.5 9.4 %all_to_all.21.blocks = bf16[8,2,2,24,128]{4,3,2,1,0:T(8,128)(2,1)S(1)} all-to-all(bf16[8,2,2,24,128]{4,3,2,1,0:T(8,128)(2,1)S(1)} %sum_line.1), channel_id=1, replica_groups=mesh['x'=4,'yh'=2,'zh'=4,'zl'=2,'yl'=2,'c'=2] {'x','yh'}, dimensions={0} | all-to-all | bytes 393216 | tf_op jit(solution)/shard_map/all_to_all | solution.py:601
  115.9 0.7 finish.1
  (1 shorter events, 0.0 us)
Async XLA Ops:
  0.6 6.9 %collective-permute-start = (bf16[256,1536]{1,0:T(8,128)(2,1)}, bf16[256,1536]{1,0:T(8,128)(2,1)S(1)}, u32[]{:S(2)}, u32[]{:S(2)}) collective-permute-start(bf16[256,1536]{1,0:T(8,128)(2,1)} %bitcast.14), channel_id=1, source_target_pairs={{0,1},{1,0},{2,3},{3,2},{4,5},{5,4},{6,7},{7,6},{8,9},{9,8},{10,11... | collective-permute-start | bytes 2359304 | tf_op jit(solution)/shard_map/ppermute | solution.py:565
  4.0 6.3 %collective-permute-start.1 = (bf16[256,1536]{1,0:T(8,128)(2,1)}, bf16[256,1536]{1,0:T(8,128)(2,1)S(1)}, u32[]{:S(2)}, u32[]{:S(2)}) collective-permute-start(bf16[256,1536]{1,0:T(8,128)(2,1)} %bitcast.7), channel_id=1, source_target_pairs={{0,1},{1,0},{2,3},{3,2},{4,5},{5,4},{6,7},{7,6},{8,9},{9,8},{10,11... | collective-permute-start | bytes 2359304 | tf_op jit(solution)/shard_map/ppermute | solution.py:565
  7.9 5.4 %copy-start.5 = (bf16[512,256]{1,0:T(8,128)(2,1)}, bf16[512,256]{1,0:T(8,128)(2,1)S(1)}, u32[]{:S(2)}) copy-start(bf16[512,256]{1,0:T(8,128)(2,1)S(1)} %get-tuple-element.39.kv) | copy-start | bytes 786436
  7.9 5.3 %collective-permute-start.2 = (bf16[384,256]{1,0:T(8,128)(2,1)S(1)}, bf16[384,256]{1,0:T(8,128)(2,1)S(1)}, u32[]{:S(2)}, u32[]{:S(2)}) collective-permute-start(bf16[384,256]{1,0:T(8,128)(2,1)S(1)} %get-tuple-element.40), channel_id=1, source_target_pairs={{0,2},{1,3},{2,4},{3,5},{4,6},{5,7},{6,8},{7,9},{8,10},{9,11},{10,... | collective-permute-start | bytes 589832 | tf_op jit(solution)/shard_map/ppermute | solution.py:577
  9.4 1.1 copy-start.2
  9.4 1.1 copy-start.12
  10.2 8.1 %copy-start.3 = (bf16[256,1536]{1,0:T(8,128)(2,1)}, bf16[256,1536]{1,0:T(8,128)(2,1)S(1)}, u32[]{:S(2)}) copy-start(bf16[256,1536]{1,0:T(8,128)(2,1)S(1)} %collective-permute-done.1.do_oth) | copy-start | bytes 2359300
  13.3 5.0 %copy-start.10 = (bf16[384,256]{1,0:T(8,128)(2,1)}, bf16[384,256]{1,0:T(8,128)(2,1)S(1)}, u32[]{:S(2)}) copy-start(bf16[384,256]{1,0:T(8,128)(2,1)S(1)} %collective-permute-done.2.halo) | copy-start | bytes 589828
  20.5 35.3 %all-to-all-start.1 = ((bf16[32,4,2,24,128]{4,3,2,1,0:T(8,128)(2,1)}), bf16[32,4,2,24,128]{4,3,2,1,0:T(8,128)(2,1)}, u32[]{:S(2)}, u32[]{:S(2)}) async-start(bf16[32,4,2,24,128]{4,3,2,1,0:T(8,128)(2,1)} %get-tuple-element.60), calls=%async_computation.1 | async-start | bytes 3145728 | tf_op jit(solution)/shard_map/all_to_all | solution.py:584
  30.8 1.1 copy-start.4
  32.0 0.9 copy-start.6
  32.9 1.2 %copy-start.7 = (f32[896,256]{1,0:T(8,128)S(1)}, f32[896,256]{1,0:T(8,128)}, u32[]{:S(2)}) copy-start(f32[896,256]{1,0:T(8,128)} %get-tuple-element.49.dkv_in) | copy-start | bytes 2752516
  34.1 0.9 copy-start.11
  39.2 2.8 %copy-start.9 = (bf16[256,512]{1,0:T(8,128)(2,1)}, bf16[256,512]{1,0:T(8,128)(2,1)S(1)}, u32[]{:S(2)}) copy-start(bf16[256,512]{1,0:T(8,128)(2,1)S(1)} %get-tuple-element.53.mix_oth) | copy-start | bytes 786436
  39.2 14.5 %collective-permute-start.3 = (bf16[384,256]{1,0:T(8,128)(2,1)S(1)}, bf16[384,256]{1,0:T(8,128)(2,1)S(1)}, u32[]{:S(2)}, u32[]{:S(2)}) collective-permute-start(bf16[384,256]{1,0:T(8,128)(2,1)S(1)} %get-tuple-element.52), channel_id=1, source_target_pairs={{2,0},{3,1},{4,2},{5,3},{6,4},{7,5},{8,6},{9,7},{10,8},{11,9},{12,... | collective-permute-start | bytes 589832 | tf_op jit(solution)/shard_map/ppermute | solution.py:588
  55.2 0.7 copy-start.13
  55.9 11.4 %copy-start.1 = (bf16[1536,512]{1,0:T(8,128)(2,1)S(1)}, bf16[1536,512]{1,0:T(8,128)(2,1)}, u32[]{:S(2)}) copy-start(bf16[1536,512]{1,0:T(8,128)(2,1)} %wkv.3) | copy-start | bytes 4718596
  55.9 32.4 %all-to-all-start = ((bf16[32,4,2,24,128]{4,3,2,1,0:T(8,128)(2,1)}), bf16[32,4,2,24,128]{4,3,2,1,0:T(8,128)(2,1)S(1)}, u32[]{:S(2)}, u32[]{:S(2)}) async-start(bf16[32,4,2,24,128]{4,3,2,1,0:T(8,128)(2,1)} %get-tuple-element.59), calls=%async_computation | async-start | bytes 3145728 | tf_op jit(solution)/shard_map/all_to_all | solution.py:591
  64.0 3.3 %collective-permute-start.4 = (bf16[256,1024]{1,0:T(8,128)(2,1)}, bf16[256,1024]{1,0:T(8,128)(2,1)S(1)}, u32[]{:S(2)}, u32[]{:S(2)}) collective-permute-start(bf16[256,1024]{1,0:T(8,128)(2,1)} %get-tuple-element.55), channel_id=1, source_target_pairs={{0,1},{1,0},{2,3},{3,2},{4,5},{5,4},{6,7},{7,6},{8,9},{9,8},{10,11... | collective-permute-start | bytes 1572872 | tf_op jit(solution)/shard_map/ppermute | solution.py:565
  64.9 2.1 %collective-permute-start.5 = (bf16[256,512]{1,0:T(8,128)(2,1)}, bf16[256,512]{1,0:T(8,128)(2,1)S(1)}, u32[]{:S(2)}, u32[]{:S(2)}) collective-permute-start(bf16[256,512]{1,0:T(8,128)(2,1)} %copy-done.9), channel_id=1, source_target_pairs={{0,1},{1,0},{2,3},{3,2},{4,5},{5,4},{6,7},{7,6},{8,9},{9,8},{10,11... | collective-permute-start | bytes 786440 | tf_op jit(solution)/shard_map/ppermute | solution.py:565
  65.0 2.2 %collective-permute-start.6 = (bf16[256,256]{1,0:T(8,128)(2,1)}, bf16[256,256]{1,0:T(8,128)(2,1)S(1)}, u32[]{:S(2)}, u32[]{:S(2)}) collective-permute-start(bf16[256,256]{1,0:T(8,128)(2,1)} %copy-done.13), channel_id=1, source_target_pairs={{0,1},{1,0},{2,3},{3,2},{4,5},{5,4},{6,7},{7,6},{8,9},{9,8},{10,11... | collective-permute-start | bytes 393224 | tf_op jit(solution)/shard_map/ppermute | solution.py:565
  67.3 2.3 %copy-start = (bf16[1536,1536]{1,0:T(8,128)(2,1)S(1)}, bf16[1536,1536]{1,0:T(8,128)(2,1)}, u32[]{:S(2)}) copy-start(bf16[1536,1536]{1,0:T(8,128)(2,1)} %wq.3) | copy-start | bytes 14155780
  69.6 1.0 copy-start.8

commit v5 on v3

--- a/solution.py
+++ b/solution.py
@@ -163,7 +163,7 @@
     )(x_oth, q_own, w_query)
 
 
-def attend_block(b, c, chip, q, do_own, do_oth, keys, keys_t, vals_t, starts, segs, ones):
+def attend_block(b, pairs, c, q, do_own, do_oth, keys, keys_t, vals_t, low, ones):
     half, inner = b // 2, (b % 2) * BLOCK
     own = half == c
     here = slice(inner, inner + BLOCK)
@@ -174,42 +174,47 @@
     v_more = jnp.concatenate([v_win, ones[:HEAD_DIM, :HEAD_DIM]], axis=0)
     kt_win = keys_t[:, win]
     vt_win = vals_t[:, win]
-    line = segs[pl.ds(chip * (PAIR // BLOCK) + b, 1), :]
-    lowest = jnp.zeros_like(line)
-    for d in range(DOCS):
-        lowest = jnp.where(line == d, starts[d], lowest)
     j_pos = lax.broadcasted_iota(jnp.int32, (WINDOW, BLOCK), 0)
     i_pos = lax.broadcasted_iota(jnp.int32, (WINDOW, BLOCK), 1)
-    seen = (j_pos + b * BLOCK >= lowest) & (j_pos <= i_pos + HALO)
+    seen = (j_pos + b * BLOCK >= low[b : b + 1, :]) & (j_pos <= i_pos + HALO)
     bias = jnp.where(seen, 0.0, -1e30)
     bias = jnp.concatenate([bias, bias], axis=1)
-    dk = jnp.zeros((WINDOW, HEAD_DIM), F32)
-    dv = jnp.zeros((WINDOW, HEAD_DIM), F32)
-    ctx_parts = []
-    dq_parts = []
-    for pair in range(GROUP // 2):
+    q2s, do2s = [], []
+    for pair in pairs:
         at = pair * 256
         q_two = q[q_rows, at : at + 256]
         do_cols = columns(c * QCOLS + at, 256)
         do_two = jnp.where(own, do_own[here, do_cols], do_oth[here, do_cols])
-        q2 = jnp.concatenate([q_two[:, :HEAD_DIM], q_two[:, HEAD_DIM:]], axis=0)
-        do2 = jnp.concatenate([do_two[:, :HEAD_DIM], do_two[:, HEAD_DIM:]], axis=0)
-        scores = nt(k_win, q2) + bias
+        q2s.append(jnp.concatenate([q_two[:, :HEAD_DIM], q_two[:, HEAD_DIM:]], axis=0))
+        do2s.append(jnp.concatenate([do_two[:, :HEAD_DIM], do_two[:, HEAD_DIM:]], axis=0))
+    raw = [nt(k_win, q2) for q2 in q2s]
+    probs = []
+    for scores in raw:
+        scores = scores + bias
         top = jnp.max(scores, axis=0, keepdims=True)
         expo = jnp.exp2((scores - top) * (SCALE * LOG2E))
-        probs = expo * (1.0 / jnp.sum(expo, axis=0, keepdims=True))
-        probs_low = probs.astype(BF16)
-        ctx_t = nn(vt_win, probs_low).astype(BF16)
-        dp = nt(v_more, do2)
-        delta = jnp.sum(dp[WINDOW:] * ctx_t.astype(F32), axis=0, keepdims=True)
-        ds = (probs * (dp[:WINDOW] - delta) * SCALE).astype(BF16)
-        dv = dv + nn(probs_low, do2)
-        dk = dk + nn(ds, q2)
-        dq_t = nn(kt_win, ds).astype(BF16)
+        probs.append(expo * (1.0 / jnp.sum(expo, axis=0, keepdims=True)))
+    lows = [p.astype(BF16) for p in probs]
+    dps = [nt(v_more, do2) for do2 in do2s]
+    ctx_ts = [nn(vt_win, p).astype(BF16) for p in lows]
+    deltas = [
+        jnp.sum(dp[WINDOW:] * ctx_t.astype(F32), axis=0, keepdims=True)
+        for dp, ctx_t in zip(dps, ctx_ts)
+    ]
+    dvs = [nn(p, do2) for p, do2 in zip(lows, do2s)]
+    dss = [
+        (p * (dp[:WINDOW] - delta) * SCALE).astype(BF16)
+        for p, dp, delta in zip(probs, dps, deltas)
+    ]
+    dks = [nn(ds, q2) for ds, q2 in zip(dss, q2s)]
+    dq_ts = [nn(kt_win, ds).astype(BF16) for ds in dss]
+    ctx_parts, dq_parts = [], []
+    for ctx_t, dq_t in zip(ctx_ts, dq_ts):
         turned = nt(ones, jnp.concatenate([ctx_t, dq_t], axis=0)).astype(BF16)
         ctx_parts += [turned[:BLOCK, :HEAD_DIM], turned[BLOCK:, :HEAD_DIM]]
         dq_parts += [turned[:BLOCK, HEAD_DIM:], turned[BLOCK:, HEAD_DIM:]]
-    return jnp.concatenate(ctx_parts + dq_parts, axis=1), jnp.concatenate([dk, dv], axis=1)
+    grads = jnp.concatenate([sum(dks[1:], dks[0]), sum(dvs[1:], dvs[0])], axis=1)
+    return ctx_parts, dq_parts, grads
 
 
 def turn_keys(ones, keys, keys_t, vals_t, rows):
@@ -218,98 +223,91 @@
     vals_t[:, rows] = nt(small, keys[rows, HEAD_DIM:]).astype(BF16)
 
 
-def document_starts(chip, segs):
+def lowest_keys(chip, segs, low):
     lines = []
     for t in range(KEYS // BLOCK):
         row = chip * (PAIR // BLOCK) - HALO // BLOCK + t
         line = segs[pl.ds(jnp.maximum(row, 0), 1), :]
         lines.append(jnp.where(row >= 0, line, -1))
+    own = jnp.concatenate(lines[HALO // BLOCK :], axis=0)
     lines = jnp.concatenate(lines, axis=0)
-    return [jnp.sum(jnp.where(lines < d, 1, 0)) for d in range(DOCS)]
-
-
-def attend_last_body(q, do_own, do_oth, kv, segs, mix, dkv, keys, keys_t, vals_t):
+    first = jnp.zeros_like(own)
+    for d in range(DOCS):
+        first = jnp.where(own == d, jnp.sum(jnp.where(lines < d, 1, 0)), first)
+    low[: PAIR // BLOCK, :] = first
+
+
+KEY_SCRATCH = [
+    pltpu.VMEM((KEYS, KVCOLS), BF16),
+    pltpu.VMEM((HEAD_DIM, KEYS), BF16),
+    pltpu.VMEM((HEAD_DIM, KEYS), BF16),
+]
+
+
+def attend_last_body(q, do_own, do_oth, kv, segs, mix, dkv, low, keys, keys_t, vals_t):
     c = lax.axis_index("c")
     chip = lax.axis_index(("zh", "zl", "yl"))
     ones = eye(256)
     keys[HALO:] = kv[...]
     turn_keys(ones, keys, keys_t, vals_t, slice(HALO, KEYS))
-    starts = document_starts(chip, segs)
-    mix_block, dkv[...] = attend_block(
-        3, c, chip, q, do_own, do_oth, keys, keys_t, vals_t, starts, segs, ones
+    lowest_keys(chip, segs, low)
+    ctx, dq, dkv[...] = attend_block(
+        3, range(3), c, q, do_own, do_oth, keys, keys_t, vals_t, low, ones
     )
-    mix[...] = mix_block
+    mix[...] = jnp.concatenate(ctx + dq, axis=1)
 
 
 def attend_last(q, do_own, do_oth, kv, segs):
     return pl.pallas_call(
         attend_last_body,
         in_specs=[VM] * 5,
-        out_specs=[VM] * 2,
-        out_shape=[shape((BLOCK, 2 * QCOLS)), shape((WINDOW, KVCOLS), F32)],
-        scratch_shapes=[
-            pltpu.VMEM((KEYS, KVCOLS), BF16),
-            pltpu.VMEM((HEAD_DIM, KEYS), BF16),
-            pltpu.VMEM((HEAD_DIM, KEYS), BF16),
+        out_specs=[VM] * 3,
+        out_shape=[
+            shape((BLOCK, 2 * QCOLS)),
+            shape((WINDOW, KVCOLS), F32),
+            shape((8, BLOCK), jnp.int32),
         ],
+        scratch_shapes=KEY_SCRATCH,
         compiler_params=params(),
         cost_estimate=cost(2 * BLOCK * WINDOW * QCOLS * 6, 3 << 20, BLOCK * WINDOW * GROUP),
         name="attend_last",
     )(q, do_own, do_oth, kv, segs)
 
 
-def attend_body(
-    q,
-    do_own,
-    do_oth,
-    kv,
-    halo,
-    segs,
-    mix_last,
-    dkv_last,
-    mix_own,
-    mix_oth,
-    dkv_out,
-    sent_out,
-    keys,
-    keys_t,
-    vals_t,
-    dkv,
-):
+def put(c, b, mix_own, mix_oth, value):
+    own = b // 2 == c
+    here = slice((b % 2) * BLOCK, (b % 2 + 1) * BLOCK)
+
+    @pl.when(own)
+    def _():
+        mix_own[here, :] = value
+
+    @pl.when(jnp.logical_not(own))
+    def _():
+        mix_oth[here, :] = value
+
+
+def attend_body(q, do_own, do_oth, kv, halo, low, mix_last, dkv_last, *rest):
+    mix_own, mix_oth, dkv_out, sent, keys, keys_t, vals_t, dkv = rest
     c = lax.axis_index("c")
-    chip = lax.axis_index(("zh", "zl", "yl"))
     ones = eye(256)
     keys[:HALO] = halo[...]
     keys[HALO:] = kv[...]
     turn_keys(ones, keys, keys_t, vals_t, slice(0, KEYS))
-    starts = document_starts(chip, segs)
     dkv[:HALO] = jnp.zeros((HALO, KVCOLS), F32)
     dkv[HALO:] = dkv_last[...]
-
-    def put(b, value):
-        own = b // 2 == c
-        here = slice((b % 2) * BLOCK, (b % 2 + 1) * BLOCK)
-
-        @pl.when(own)
-        def _():
-            mix_own[here, :] = value
-
-        @pl.when(jnp.logical_not(own))
-        def _():
-            mix_oth[here, :] = value
-
+    put(c, 3, mix_own, mix_oth, mix_last[...])
     for b in range(3):
-        mix, grads = attend_block(
-            b, c, chip, q, do_own, do_oth, keys, keys_t, vals_t, starts, segs, ones
+        ctx, dq, grads = attend_block(
+            b, range(3), c, q, do_own, do_oth, keys, keys_t, vals_t, low, ones
         )
         dkv[b * BLOCK : b * BLOCK + WINDOW, :] += grads
-        put(b, mix)
-    put(3, mix_last[...])
-    sent_out[...] = dkv[:HALO, :].astype(BF16)
+        put(c, b, mix_own, mix_oth, jnp.concatenate(ctx + dq, axis=1))
+    sent[...] = dkv[:HALO, :].astype(BF16)
     dkv_out[...] = dkv[HALO:, :]
 
 
-def attend(q, do_own, do_oth, kv, halo, segs, mix_last, dkv_last):
+def attend(q, do_own, do_oth, kv, halo, low, mix_last, dkv_last):
     return pl.pallas_call(
         attend_body,
         in_specs=[VM] * 8,
@@ -320,16 +318,11 @@
             shape((PAIR, KVCOLS), F32),
             shape((HALO, KVCOLS)),
         ],
-        scratch_shapes=[
-            pltpu.VMEM((KEYS, KVCOLS), BF16),
-            pltpu.VMEM((HEAD_DIM, KEYS), BF16),
-            pltpu.VMEM((HEAD_DIM, KEYS), BF16),
-            pltpu.VMEM((KEYS, KVCOLS), F32),
-        ],
+        scratch_shapes=KEY_SCRATCH + [pltpu.VMEM((KEYS, KVCOLS), F32)],
         compiler_params=params(),
         cost_estimate=cost(3 * 2 * BLOCK * WINDOW * QCOLS * 6, 5 << 20, 3 * BLOCK * WINDOW * 6),
         name="attend",
-    )(q, do_own, do_oth, kv, halo, segs, mix_last, dkv_last)
+    )(q, do_own, do_oth, kv, halo, low, mix_last, dkv_last)
 
 
 def spread(value, held):
@@ -508,8 +501,8 @@
     halo = lax.ppermute(kv_sent, ring, [(i, i + 2) for i in range(count - 2)])
     q = project_q(x_oth, q_own, wq_here)
     segs = segments.reshape(-1, BLOCK)
-    mix_last, dkv_last = attend_last(q, do_own, do_oth, kv, segs)
-    mix, mix_oth, dkv, dkv_sent = attend(q, do_own, do_oth, kv, halo, segs, mix_last, dkv_last)
+    mix_last, dkv_last, low = attend_last(q, do_own, do_oth, kv, segs)
+    mix, mix_oth, dkv, dkv_sent = attend(q, do_own, do_oth, kv, halo, low, mix_last, dkv_last)
     arrived = lax.ppermute(dkv_sent, ring, [(i + 2, i) for i in range(count - 2)])
     pieces = weight_q(x_own, x_oth, mix, mix_oth)
     pieces, dkv_own, dkv_oth = weight_kv(x_own, x_oth, dkv, arrived, pieces)

time: 117 us -> 113 us (0.966)
  Pallas kernels: 26.2 us -> 21.1 us
    pallas_call x1, Pallas kernels: 10.1 us -> 6.18 us  [attend(): pl.pallas_call(attend_body, in_specs=[VM] * 8, out_specs=[VM] * 4, out_sh...]
    pallas_call x1, Pallas kernels: 3.26 us -> 1.98 us  [attend_last(): pl.pallas_call(attend_last_body, in_specs=[VM] * 5, out_specs=[VM] * 3, o...]
  transfers between devices with their start and end apart: 7 -> 7, of which waited for: 4 -> 5; matrix products, arithmetic and copies ran while one was open for 0% -> 0% of each run, Pallas kernels for 12% -> 11%
where the time goes in v5:
time: 113 us
  waiting for transfers between devices  39.1 us (35%)
  blocking collectives  28.7 us (25%)
  Pallas kernels  21.1 us (19%)
  starting transfers between devices  18.4 us (16%)
  local copies, waits for them, and re-layouts  4.9 us (4%)
    all_to_all x1, waiting for transfers between devices, shards(): pieces = lax.all_to_all(pieces, ('x', 'yh', 'yl', 'zl'), 0, 0)  32 us
    all_to_all x1, blocking collectives, shards(): lines = lax.all_to_all(plane.reshape(8, ROWS, HEAD_DIM), ('zh', 'c'), 0, 0)  19.3 us
    all_to_all x1, starting transfers between devices, shards(): pieces = lax.all_to_all(pieces, ('x', 'yh', 'yl', 'zl'), 0, 0)  9.66 us
    all_to_all x1, blocking collectives, shards(): blocks = lax.all_to_all(blocks, ('x', 'yh'), 0, 0)  9.43 us
    pallas_call x1, Pallas kernels, attend(): pl.pallas_call(attend_body, in_specs=[VM] * 8, out_specs=[VM] * 4, out_sh...  6.18 us
    ppermute x4, starting transfers between devices, swap(): return lax.ppermute(value, 'c', [(0, 1), (1, 0)])  5.77 us
    unnamed x14, local copies, waits for them, and re-layouts  4.9 us
    ppermute x1, waiting for transfers between devices, shards(): lax.ppermute(dkv_sent, ring, [(i + 2, i) for i in range(count - 2)])  3.93 us
  transfers between devices with their start and end apart: 7, of which 5 were waited for; matrix products, arithmetic and copies ran while one was open for 0% of the time, Pallas kernels for 11%

profile of v5, /device:TPU:1, one launch (start us, length us, event | category | flops | bytes accessed | tf_op | source)
XLA Modules:
  0.0 113.0 jit_solution(16653371147830842402)
XLA Ops:
  0.6 3.3 %collective-permute-start = (bf16[256,1536]{1,0:T(8,128)(2,1)}, bf16[256,1536]{1,0:T(8,128)(2,1)S(1)}, u32[]{:S(2)}, u32[]{:S(2)}) collective-permute-start(bf16[256,1536]{1,0:T(8,128)(2,1)} %bitcast.13), channel_id=1, source_target_pairs={{0,1},{1,0},{2,3},{3,2},{4,5},{5,4},{6,7},{7,6},{8,9},{9,8},{10,11... | collective-permute-start | bytes 2359304 | tf_op jit(solution)/shard_map/ppermute | solution.py:489
  4.0 0.1 collective-permute-start.1
  4.1 3.5 %project_own.1 = (bf16[256,1536]{1,0:T(8,128)(2,1)S(1)}, bf16[1536,512]{1,0:T(8,128)(2,1)S(1)}, bf16[1536,768]{1,0:T(8,128)(2,1)S(1)}, bf16[256,768]{1,0:T(8,128)(2,1)S(1)}, bf16[256,256]{1,0:T(8,128)(2,1)S(1)}) custom-call(bf16[256,1536]{1,0:T(8,128)(2,1)} %bitcast.14, bf16[1536,512]{1,0:T(8,128)(2,1)} %wkv.3, bf16[1536,1536]{1,0:T(8,128)(2,1)} %wq.3), custom_call_target="tpu_custom_call" | custom-call | flops 805306368 | bytes 5242880 | tf_op jit(solution)/shard_map/project_own/pallas_call | solution.py:105
  7.5 0.0 collective-permute-done.x_oth
  7.5 0.0 copy-start.5
  7.5 0.0 copy-start.6
  7.6 0.4 project_kv.1
  8.0 1.5 %collective-permute-start.2 = (bf16[384,256]{1,0:T(8,128)(2,1)S(1)}, bf16[384,256]{1,0:T(8,128)(2,1)S(1)}, u32[]{:S(2)}, u32[]{:S(2)}) collective-permute-start(bf16[384,256]{1,0:T(8,128)(2,1)S(1)} %get-tuple-element.31), channel_id=1, source_target_pairs={{0,2},{1,3},{2,4},{3,5},{4,6},{5,7},{6,8},{7,9},{8,10},{9,11},{10,... | collective-permute-start | bytes 589832 | tf_op jit(solution)/shard_map/ppermute | solution.py:501
  9.4 0.8 project_q.1.q
  10.2 0.0 collective-permute-done.1.do_oth
  10.2 0.0 copy-done.5
  10.3 0.0 copy-done.6
  10.3 2.0 %attend_last.1 = (bf16[128,1536]{1,0:T(8,128)(2,1)S(1)}, f32[512,256]{1,0:T(8,128)S(1)}, s32[8,128]{1,0:T(8,128)S(1)}) custom-call(bf16[512,768]{1,0:T(8,128)(2,1)S(1)} %project_q.1.q, bf16[256,1536]{1,0:T(8,128)(2,1)S(1)} %bitcast.8, bf16[256,1536]{1,0:T(8,128)(2,1)S(1)} %collective-permute-done.1.do_oth, bf16[512,256]{1,0:T(8,128)(2,1)S(1)} %get-tuple-element.30.kv, ...), custom_call_target="tpu_custom_call" | custom-call | flops 603979776 | bytes 3145728 | tf_op jit(solution)/shard_map/attend_last/pallas_call | solution.py:261
  12.3 1.1 collective-permute-done.2.halo
  13.3 6.2 %attend.1 = (bf16[256,1536]{1,0:T(8,128)(2,1)S(1)}, bf16[256,1536]{1,0:T(8,128)(2,1)S(1)}, f32[512,256]{1,0:T(8,128)S(1)}, bf16[384,256]{1,0:T(8,128)(2,1)S(1)}) custom-call(bf16[512,768]{1,0:T(8,128)(2,1)S(1)} %project_q.1.q, bf16[256,1536]{1,0:T(8,128)(2,1)S(1)} %bitcast.9, bf16[256,1536]{1,0:T(8,128)(2,1)S(1)} %collective-permute-done.1.do_oth, ...), custom_call_target="tpu_custom_call" | custom-call | flops 1811939328 | bytes 5242880 | tf_op jit(solution)/shard_map/attend/pallas_call | solution.py:311
  19.5 0.0 copy-start.2
  19.5 0.0 copy-start.4
  19.5 1.5 %collective-permute-start.3 = (bf16[384,256]{1,0:T(8,128)(2,1)S(1)}, bf16[384,256]{1,0:T(8,128)(2,1)S(1)}, u32[]{:S(2)}, u32[]{:S(2)}) collective-permute-start(bf16[384,256]{1,0:T(8,128)(2,1)S(1)} %get-tuple-element.38), channel_id=1, source_target_pairs={{2,0},{3,1},{4,2},{5,3},{6,4},{7,5},{8,6},{9,7},{10,8},{11,9},{12,... | collective-permute-start | bytes 589832 | tf_op jit(solution)/shard_map/ppermute | solution.py:506
  21.0 2.6 %weight_q.1.before = bf16[32,4,2,48,128]{4,3,2,1,0:T(8,128)(2,1)} custom-call(bf16[256,1536]{1,0:T(8,128)(2,1)S(1)} %get-tuple-element.36.x_own, bf16[256,1536]{1,0:T(8,128)(2,1)S(1)} %collective-permute-done.x_oth, bf16[256,1536]{1,0:T(8,128)(2,1)S(1)} %get-tuple-element.35.mix_own.mix, bf16[256,1536]{1,0:T(8,128)(2,1)S(1)} %get-tuple-element.39.mix_oth), custom_call_target="tpu_custom_call" | custom-call | flops 1207959552 | bytes 4194304 | tf_op jit(solution)/shard_map/weight_q/pallas_call | solution.py:353
  23.6 0.0 copy-done.2
  23.7 3.9 %collective-permute-done.3.arrived = bf16[384,256]{1,0:T(8,128)(2,1)S(1)} collective-permute-done((bf16[384,256]{1,0:T(8,128)(2,1)S(1)}, bf16[384,256]{1,0:T(8,128)(2,1)S(1)}, u32[]{:S(2)}, u32[]{:S(2)}) %collective-permute-start.3) | collective-permute-done | bytes 196640 | tf_op jit(solution)/shard_map/ppermute | solution.py:506
  27.6 1.5 %weight_kv.1 = (bf16[32,4,2,48,128]{4,3,2,1,0:T(8,128)(2,1)}, bf16[256,256]{1,0:T(8,128)(2,1)S(1)}, bf16[256,256]{1,0:T(8,128)(2,1)S(1)}) custom-call(bf16[256,1536]{1,0:T(8,128)(2,1)S(1)} %get-tuple-element.36.x_own, bf16[256,1536]{1,0:T(8,128)(2,1)S(1)} %collective-permute-done.x_oth, ...), custom_call_target="tpu_custom_call", output_to_operand_aliasing={{0}: (4, {})} | custom-call | flops 402653184 | bytes 3145728 | tf_op jit(solution)/shard_map/weight_kv/pallas_call | solution.py:387
  29.1 0.0 copy-done.4
  29.1 9.7 %all-to-all-start = ((bf16[32,4,2,48,128]{4,3,2,1,0:T(8,128)(2,1)}), bf16[32,4,2,48,128]{4,3,2,1,0:T(8,128)(2,1)S(1)}, u32[]{:S(2)}, u32[]{:S(2)}) async-start(bf16[32,4,2,48,128]{4,3,2,1,0:T(8,128)(2,1)} %get-tuple-element.44), calls=%async_computation | async-start | bytes 6291456 | tf_op jit(solution)/shard_map/all_to_all | solution.py:509
  38.8 2.2 %collective-permute-start.4 = (bf16[256,1536]{1,0:T(8,128)(2,1)}, bf16[256,1536]{1,0:T(8,128)(2,1)S(1)}, u32[]{:S(2)}, u32[]{:S(2)}) collective-permute-start(bf16[256,1536]{1,0:T(8,128)(2,1)} %copy-done.4), channel_id=1, source_target_pairs={{0,1},{1,0},{2,3},{3,2},{4,5},{5,4},{6,7},{7,6},{8,9},{9,8},{10,11... | collective-permute-start | bytes 2359304 | tf_op jit(solution)/shard_map/ppermute | solution.py:489
  41.0 0.1 collective-permute-start.5
  41.1 2.0 %collective-permute-done.5.dkv_in = bf16[256,256]{1,0:T(8,128)(2,1)S(1)} collective-permute-done((bf16[256,256]{1,0:T(8,128)(2,1)S(1)}, bf16[256,256]{1,0:T(8,128)(2,1)S(1)}, u32[]{:S(2)}, u32[]{:S(2)}) %collective-permute-start.5) | collective-permute-done | bytes 131104 | tf_op jit(solution)/shard_map/ppermute | solution.py:489
  43.1 0.1 collective-permute-done.4.mix_in
  43.3 0.0 copy-start
  43.3 2.3 %copy-done = bf16[1536,1536]{1,0:T(8,128)(2,1)S(1)} copy-done((bf16[1536,1536]{1,0:T(8,128)(2,1)S(1)}, bf16[1536,1536]{1,0:T(8,128)(2,1)}, u32[]{:S(2)}) %copy-start) | copy-done | bytes 4718616
  45.6 0.0 copy-start.1
  45.6 1.4 %copy-done.1 = bf16[1536,512]{1,0:T(8,128)(2,1)S(1)} copy-done((bf16[1536,512]{1,0:T(8,128)(2,1)S(1)}, bf16[1536,512]{1,0:T(8,128)(2,1)}, u32[]{:S(2)}) %copy-start.1) | copy-done | bytes 1572888
  47.0 0.0 copy-start.3
  47.0 1.1 %copy-done.3 = bf16[256,1536]{1,0:T(8,128)(2,1)S(1)} copy-done((bf16[256,1536]{1,0:T(8,128)(2,1)S(1)}, bf16[256,1536]{1,0:T(8,128)(2,1)}, u32[]{:S(2)}) %copy-start.3) | copy-done | bytes 786456
  48.2 3.0 %grad_tokens.1 = (bf16[256,1536]{1,0:T(8,128)(2,1)}, bf16[256,1536]{1,0:T(8,128)(2,1)}, f32[8,128]{1,0:T(8,128)S(1)}) custom-call(bf16[256,1536]{1,0:T(8,128)(2,1)S(1)} %copy-done.3, bf16[256,256]{1,0:T(8,128)(2,1)S(1)} %get-tuple-element.40.dkv, bf16[256,1536]{1,0:T(8,128)(2,1)S(1)} %collective-permute-done.4.mix_in, ...), custom_call_target="tpu_custom_call" | custom-call | flops 1610612736 | bytes 8388608 | tf_op jit(solution)/shard_map/grad_tokens/pallas_call | solution.py:422
  51.2 32.0 %all-to-all-done.pieces = bf16[32,4,2,48,128]{4,3,2,1,0:T(8,128)(2,1)S(1)} async-done(((bf16[32,4,2,48,128]{4,3,2,1,0:T(8,128)(2,1)}), bf16[32,4,2,48,128]{4,3,2,1,0:T(8,128)(2,1)S(1)}, u32[]{:S(2)}, u32[]{:S(2)}) %all-to-all-start) | async-done | bytes 3145760 | tf_op jit(solution)/shard_map/all_to_all | solution.py:509
  83.2 0.4 sum_plane.1
  83.6 19.3 %all_to_all.15 = bf16[8,48,128]{2,1,0:T(8,128)(2,1)S(1)} all-to-all(bf16[8,48,128]{2,1,0:T(8,128)(2,1)S(1)} %bitcast.10), channel_id=1, replica_groups=mesh['x'=4,'yh'=2,'zh'=4,'zl'=2,'yl'=2,'c'=2] {'zh','c'}, dimensions={0} | all-to-all | bytes 196608 | tf_op jit(solution)/shard_map/all_to_all | solution.py:514
  102.9 9.4 %all_to_all.16.blocks = bf16[8,2,48,128]{3,2,1,0:T(8,128)(2,1)S(1)} all-to-all(bf16[8,2,48,128]{3,2,1,0:T(8,128)(2,1)S(1)} %sum_line.1), channel_id=1, replica_groups=mesh['x'=4,'yh'=2,'zh'=4,'zl'=2,'yl'=2,'c'=2] {'x','yh'}, dimensions={0} | all-to-all | bytes 393216 | tf_op jit(solution)/shard_map/all_to_all | solution.py:516
  112.3 0.7 finish.1
  (1 shorter events, 0.0 us)
Async XLA Ops:
  0.6 6.9 %collective-permute-start = (bf16[256,1536]{1,0:T(8,128)(2,1)}, bf16[256,1536]{1,0:T(8,128)(2,1)S(1)}, u32[]{:S(2)}, u32[]{:S(2)}) collective-permute-start(bf16[256,1536]{1,0:T(8,128)(2,1)} %bitcast.13), channel_id=1, source_target_pairs={{0,1},{1,0},{2,3},{3,2},{4,5},{5,4},{6,7},{7,6},{8,9},{9,8},{10,11... | collective-permute-start | bytes 2359304 | tf_op jit(solution)/shard_map/ppermute | solution.py:489
  4.0 6.3 %collective-permute-start.1 = (bf16[256,1536]{1,0:T(8,128)(2,1)}, bf16[256,1536]{1,0:T(8,128)(2,1)S(1)}, u32[]{:S(2)}, u32[]{:S(2)}) collective-permute-start(bf16[256,1536]{1,0:T(8,128)(2,1)} %bitcast.7), channel_id=1, source_target_pairs={{0,1},{1,0},{2,3},{3,2},{4,5},{5,4},{6,7},{7,6},{8,9},{9,8},{10,11... | collective-permute-start | bytes 2359304 | tf_op jit(solution)/shard_map/ppermute | solution.py:489
  7.5 2.7 %copy-start.5 = (bf16[1,256,1536]{2,1,0:T(8,128)(2,1)S(1)}, bf16[1,256,1536]{2,1,0:T(8,128)(2,1)}, u32[]{:S(2)}) copy-start(bf16[1,256,1536]{2,1,0:T(8,128)(2,1)} %param.9) | copy-start | bytes 2359300
  7.5 2.7 %copy-start.6 = (s32[1,8192]{1,0:T(1,128)S(1)}, s32[1,8192]{1,0:T(1,128)}, u32[]{:S(2)}) copy-start(s32[1,8192]{1,0:T(1,128)} %param.6) | copy-start | bytes 98308
  8.0 5.3 %collective-permute-start.2 = (bf16[384,256]{1,0:T(8,128)(2,1)S(1)}, bf16[384,256]{1,0:T(8,128)(2,1)S(1)}, u32[]{:S(2)}, u32[]{:S(2)}) collective-permute-start(bf16[384,256]{1,0:T(8,128)(2,1)S(1)} %get-tuple-element.31), channel_id=1, source_target_pairs={{0,2},{1,3},{2,4},{3,5},{4,6},{5,7},{6,8},{7,9},{8,10},{9,11},{10,... | collective-permute-start | bytes 589832 | tf_op jit(solution)/shard_map/ppermute | solution.py:501
  19.5 4.2 %copy-start.2 = (bf16[256,1536]{1,0:T(8,128)(2,1)}, bf16[256,1536]{1,0:T(8,128)(2,1)S(1)}, u32[]{:S(2)}) copy-start(bf16[256,1536]{1,0:T(8,128)(2,1)S(1)} %get-tuple-element.35.mix_own.mix) | copy-start | bytes 2359300
  19.5 9.6 %copy-start.4 = (bf16[256,1536]{1,0:T(8,128)(2,1)}, bf16[256,1536]{1,0:T(8,128)(2,1)S(1)}, u32[]{:S(2)}) copy-start(bf16[256,1536]{1,0:T(8,128)(2,1)S(1)} %get-tuple-element.39.mix_oth) | copy-start | bytes 2359300
  19.5 8.1 %collective-permute-start.3 = (bf16[384,256]{1,0:T(8,128)(2,1)S(1)}, bf16[384,256]{1,0:T(8,128)(2,1)S(1)}, u32[]{:S(2)}, u32[]{:S(2)}) collective-permute-start(bf16[384,256]{1,0:T(8,128)(2,1)S(1)} %get-tuple-element.38), channel_id=1, source_target_pairs={{2,0},{3,1},{4,2},{5,3},{6,4},{7,5},{8,6},{9,7},{10,8},{11,9},{12,... | collective-permute-start | bytes 589832 | tf_op jit(solution)/shard_map/ppermute | solution.py:506
  29.1 54.0 %all-to-all-start = ((bf16[32,4,2,48,128]{4,3,2,1,0:T(8,128)(2,1)}), bf16[32,4,2,48,128]{4,3,2,1,0:T(8,128)(2,1)S(1)}, u32[]{:S(2)}, u32[]{:S(2)}) async-start(bf16[32,4,2,48,128]{4,3,2,1,0:T(8,128)(2,1)} %get-tuple-element.44), calls=%async_computation | async-start | bytes 6291456 | tf_op jit(solution)/shard_map/all_to_all | solution.py:509
  38.8 4.5 %collective-permute-start.4 = (bf16[256,1536]{1,0:T(8,128)(2,1)}, bf16[256,1536]{1,0:T(8,128)(2,1)S(1)}, u32[]{:S(2)}, u32[]{:S(2)}) collective-permute-start(bf16[256,1536]{1,0:T(8,128)(2,1)} %copy-done.4), channel_id=1, source_target_pairs={{0,1},{1,0},{2,3},{3,2},{4,5},{5,4},{6,7},{7,6},{8,9},{9,8},{10,11... | collective-permute-start | bytes 2359304 | tf_op jit(solution)/shard_map/ppermute | solution.py:489
  41.0 2.1 %collective-permute-start.5 = (bf16[256,256]{1,0:T(8,128)(2,1)S(1)}, bf16[256,256]{1,0:T(8,128)(2,1)S(1)}, u32[]{:S(2)}, u32[]{:S(2)}) collective-permute-start(bf16[256,256]{1,0:T(8,128)(2,1)S(1)} %get-tuple-element.41), channel_id=1, source_target_pairs={{0,1},{1,0},{2,3},{3,2},{4,5},{5,4},{6,7},{7,6},{8,9},{9,8},{10,11... | collective-permute-start | bytes 393224 | tf_op jit(solution)/shard_map/ppermute | solution.py:489
  43.3 2.3 %copy-start = (bf16[1536,1536]{1,0:T(8,128)(2,1)S(1)}, bf16[1536,1536]{1,0:T(8,128)(2,1)}, u32[]{:S(2)}) copy-start(bf16[1536,1536]{1,0:T(8,128)(2,1)} %wq.3) | copy-start | bytes 14155780
  45.6 1.4 %copy-start.1 = (bf16[1536,512]{1,0:T(8,128)(2,1)S(1)}, bf16[1536,512]{1,0:T(8,128)(2,1)}, u32[]{:S(2)}) copy-start(bf16[1536,512]{1,0:T(8,128)(2,1)} %wkv.3) | copy-start | bytes 4718596
  47.0 1.1 %copy-start.3 = (bf16[256,1536]{1,0:T(8,128)(2,1)S(1)}, bf16[256,1536]{1,0:T(8,128)(2,1)}, u32[]{:S(2)}) copy-start(bf16[256,1536]{1,0:T(8,128)(2,1)} %copy-done.2) | copy-start | bytes 2359300

commit v6 on v5

--- a/solution.py
+++ b/solution.py
@@ -28,7 +28,8 @@
 NT = (((1,), (1,)), ((), ()))
 TN = (((0,), (0,)), ((), ()))
 ROWS = 48
-PIECES = (32, 4, 2, ROWS, HEAD_DIM)
+KEEP = 384
+PIECES = (16, 4, 2, ROWS, HEAD_DIM)
 LIMIT = 24 * 1024 * 1024
 VM = pl.BlockSpec(memory_space=pltpu.VMEM)
 ANY = pl.BlockSpec(memory_space=pl.ANY)
@@ -274,8 +275,9 @@
     )(q, do_own, do_oth, kv, segs)
 
 
-def put(c, b, mix_own, mix_oth, value):
-    own = b // 2 == c
+def put(b, outs, value):
+    mix_own, mix_oth, kept, sent = outs
+    own = b // 2 == lax.axis_index("c")
     here = slice((b % 2) * BLOCK, (b % 2 + 1) * BLOCK)
 
     @pl.when(own)
@@ -286,9 +288,16 @@
     def _():
         mix_oth[here, :] = value
 
+    first = lax.axis_index("xl") == 0
+    rows = pl.ds(pl.multiple_of(jnp.where(own, 0, OWN) + (b % 2) * BLOCK, BLOCK), BLOCK)
+    one = value[:, QCOLS : QCOLS + KEEP]
+    two = value[:, QCOLS + KEEP :]
+    kept[rows, :] = jnp.where(first, one, two)
+    sent[rows, :] = jnp.where(first, two, one)
+
 
 def attend_body(q, do_own, do_oth, kv, halo, low, mix_last, dkv_last, *rest):
-    mix_own, mix_oth, dkv_out, sent, keys, keys_t, vals_t, dkv = rest
+    *outs, dkv_out, dkv_sent, keys, keys_t, vals_t, dkv = rest
     c = lax.axis_index("c")
     ones = eye(256)
     keys[:HALO] = halo[...]
@@ -296,14 +305,14 @@
     turn_keys(ones, keys, keys_t, vals_t, slice(0, KEYS))
     dkv[:HALO] = jnp.zeros((HALO, KVCOLS), F32)
     dkv[HALO:] = dkv_last[...]
-    put(c, 3, mix_own, mix_oth, mix_last[...])
+    put(3, outs, mix_last[...])
     for b in range(3):
         ctx, dq, grads = attend_block(
             b, range(3), c, q, do_own, do_oth, keys, keys_t, vals_t, low, ones
         )
         dkv[b * BLOCK : b * BLOCK + WINDOW, :] += grads
-        put(c, b, mix_own, mix_oth, jnp.concatenate(ctx + dq, axis=1))
-    sent[...] = dkv[:HALO, :].astype(BF16)
+        put(b, outs, jnp.concatenate(ctx + dq, axis=1))
+    dkv_sent[...] = dkv[:HALO, :].astype(BF16)
     dkv_out[...] = dkv[HALO:, :]
 
 
@@ -311,10 +320,12 @@
     return pl.pallas_call(
         attend_body,
         in_specs=[VM] * 8,
-        out_specs=[VM] * 4,
+        out_specs=[VM] * 6,
         out_shape=[
             shape((OWN, 2 * QCOLS)),
             shape((OWN, 2 * QCOLS)),
+            shape((PAIR, KEEP)),
+            shape((PAIR, KEEP)),
             shape((PAIR, KVCOLS), F32),
             shape((HALO, KVCOLS)),
         ],
@@ -325,47 +336,7 @@
     )(q, do_own, do_oth, kv, halo, low, mix_last, dkv_last)
 
 
-def spread(value, held):
-    for s in range(2):
-        for y in range(2):
-            for zl in range(2):
-                for zh in range(4):
-                    for core in range(2):
-                        row = (zh * 2 + zl) * 192 + y * 96 + core * ROWS
-                        piece = value[row : row + ROWS, s * HEAD_DIM : (s + 1) * HEAD_DIM]
-                        held[s * 4 + y * 2 + zl, zh, core] = piece.astype(BF16)
-
-
-def weight_q_body(x_own, x_oth, mix_own, mix_oth, out, held, sems):
-    copies = []
-    for j in range(3):
-        cols = slice(QCOLS + j * 256, QCOLS + (j + 1) * 256)
-        value = tn(x_own[...], mix_own[:, cols]) + tn(x_oth[...], mix_oth[:, cols])
-        spread(value, held.at[j])
-        copy = pltpu.make_async_copy(held.at[j], out.at[pl.ds(8 * j, 8)], sems.at[j])
-        copy.start()
-        copies.append(copy)
-    for copy in copies:
-        copy.wait()
-
-
-def weight_q(x_own, x_oth, mix_own, mix_oth):
-    return pl.pallas_call(
-        weight_q_body,
-        in_specs=[VM] * 4,
-        out_specs=ANY,
-        out_shape=pltpu.HBM(PIECES, BF16),
-        scratch_shapes=[
-            pltpu.VMEM((3, 8) + PIECES[1:], BF16),
-            pltpu.SemaphoreType.DMA((3,)),
-        ],
-        compiler_params=params(),
-        cost_estimate=cost(2 * PAIR * D * QCOLS, 4 << 20),
-        name="weight_q",
-    )(x_own, x_oth, mix_own, mix_oth)
-
-
-def weight_kv_body(x_own, x_oth, dkv, arrived, before, out, own_out, oth_out, held, sem):
+def total_kv_body(dkv, arrived, own_out, oth_out, kept, sent):
     c = lax.axis_index("c")
     low = dkv[:OWN]
     skip = PAIR - HALO
@@ -377,24 +348,108 @@
     oth = jnp.where(c == 0, high, low)
     own_out[...] = own
     oth_out[...] = oth
-    spread(tn(x_own[...], own) + tn(x_oth[...], oth), held)
-    copy = pltpu.make_async_copy(held, out.at[pl.ds(24, 8)], sem)
-    copy.start()
-    copy.wait()
-
-
-def weight_kv(x_own, x_oth, dkv, arrived, before):
-    return pl.pallas_call(
-        weight_kv_body,
-        in_specs=[VM] * 4 + [ANY],
-        out_specs=[ANY, VM, VM],
-        out_shape=[pltpu.HBM(PIECES, BF16), shape((OWN, KVCOLS)), shape((OWN, KVCOLS))],
-        scratch_shapes=[pltpu.VMEM((8,) + PIECES[1:], BF16), pltpu.SemaphoreType.DMA],
-        input_output_aliases={4: 0},
-        compiler_params=params(),
-        cost_estimate=cost(2 * PAIR * D * KVCOLS, 3 << 20),
-        name="weight_kv",
-    )(x_own, x_oth, dkv, arrived, before)
+    first = lax.axis_index("xl") == 0
+    for rows, value in ((slice(0, OWN), own), (slice(OWN, PAIR), oth)):
+        kept[rows, :] = jnp.where(first, value[:, :HEAD_DIM], value[:, HEAD_DIM:])
+        sent[rows, :] = jnp.where(first, value[:, HEAD_DIM:], value[:, :HEAD_DIM])
+
+
+def total_kv(dkv, arrived):
+    return pl.pallas_call(
+        total_kv_body,
+        in_specs=[VM] * 2,
+        out_specs=[VM] * 4,
+        out_shape=[shape((OWN, KVCOLS))] * 2 + [shape((PAIR, HEAD_DIM))] * 2,
+        compiler_params=params(),
+        cost_estimate=cost(1, 1),
+        name="total_kv",
+    )(dkv, arrived)
+
+
+def chunks(width):
+    return [slice(at, min(at + 256, width)) for at in range(0, width, 256)]
+
+
+def weight_near_body(x_own, x_oth, g, out):
+    for cols in chunks(g.shape[1]):
+        out[:, cols] = tn(x_own[...], g[:OWN, cols]) + tn(x_oth[...], g[OWN:, cols])
+
+
+def weight_near(x_own, x_oth, g):
+    width = g.shape[1]
+    return pl.pallas_call(
+        weight_near_body,
+        in_specs=[VM] * 3,
+        out_specs=VM,
+        out_shape=shape((D, width), F32),
+        compiler_params=params(),
+        cost_estimate=cost(20 * PAIR * D * width, 30 << 20),
+        name="weight_near",
+    )(x_own, x_oth, g)
+
+
+def relay_body(value, after, out):
+    del value, after, out
+
+
+def relay(value, after):
+    return pl.pallas_call(
+        relay_body,
+        in_specs=[VM] * 2,
+        out_specs=VM,
+        out_shape=shape(value.shape),
+        input_output_aliases={0: 0},
+        compiler_params=params(),
+        cost_estimate=cost(1, 1),
+        name="relay",
+    )(value, after)
+
+
+def spread(value, held, block):
+    for s in range(value.shape[1] // HEAD_DIM):
+        for y in range(2):
+            for zl in range(2):
+                for zh in range(4):
+                    for core in range(2):
+                        row = (zh * 2 + zl) * 192 + y * 96 + core * ROWS
+                        piece = value[row : row + ROWS, s * HEAD_DIM : (s + 1) * HEAD_DIM]
+                        held[(block + s) * 4 + y * 2 + zl, zh, core] = piece.astype(BF16)
+
+
+def weight_far_body(start, x_own, x_oth, near, g, *rest):
+    out, held, sems = rest[-3:]
+    copies = []
+    for i, cols in enumerate(chunks(g.shape[1])):
+        value = near[:, cols] + tn(x_own[...], g[:OWN, cols]) + tn(x_oth[...], g[OWN:, cols])
+        spread(value, held, 2 * i)
+        count = (cols.stop - cols.start) // 32
+        copies.append(
+            pltpu.make_async_copy(
+                held.at[pl.ds(8 * i, count)], out.at[pl.ds(start + 8 * i, count)], sems.at[i]
+            )
+        )
+        copies[-1].start()
+    for copy in copies:
+        copy.wait()
+
+
+def weight_far(x_own, x_oth, near, g, before=None):
+    width = g.shape[1]
+    extra = [] if before is None else [before]
+    return pl.pallas_call(
+        functools.partial(weight_far_body, 0 if before is None else 12),
+        in_specs=[VM] * 4 + [ANY] * len(extra),
+        out_specs=ANY,
+        out_shape=pltpu.HBM(PIECES, BF16),
+        scratch_shapes=[
+            pltpu.VMEM((width // 32,) + PIECES[1:], BF16),
+            pltpu.SemaphoreType.DMA((2,)),
+        ],
+        input_output_aliases={4: 0} if extra else {},
+        compiler_params=params(),
+        cost_estimate=cost(2 * PAIR * D * width, 4 << 20),
+        name="weight_far",
+    )(x_own, x_oth, near, g, *extra)
 
 
 def ordered(first, own, oth):
@@ -441,7 +496,7 @@
         out_specs=VM,
         out_shape=shape(PIECES[1:]),
         compiler_params=params(),
-        cost_estimate=cost(32 * 8 * ROWS * HEAD_DIM, 3 << 20),
+        cost_estimate=cost(16 * 8 * ROWS * HEAD_DIM, 2 << 20),
         name="sum_plane",
     )(pieces, after)
 
@@ -464,14 +519,18 @@
 
 
 def finish_body(blocks, query_w, keyval_w):
-    for s in range(8):
-        for core in range(2):
-            if s < GROUP:
-                at = (core * GROUP + s) * HEAD_DIM
-                query_w[:, at : at + HEAD_DIM] = blocks[s, core]
-            else:
-                at = ((s - GROUP) * KV_HEADS + core) * HEAD_DIM
-                keyval_w[:, at : at + HEAD_DIM] = blocks[s, core]
+    for xh in range(2):
+        for xl in range(2):
+            for yh in range(2):
+                for core in range(2):
+                    rows = blocks[(xh * 2 + xl) * 2 + yh, core]
+                    block = xh * 2 + yh
+                    if block < 3:
+                        at = (core * GROUP + xl * 3 + block) * HEAD_DIM
+                        query_w[:, at : at + HEAD_DIM] = rows
+                    else:
+                        at = (xl * KV_HEADS + core) * HEAD_DIM
+                        keyval_w[:, at : at + HEAD_DIM] = rows
 
 
 def finish(blocks):
@@ -485,8 +544,8 @@
     )(blocks)
 
 
-def swap(value):
-    return lax.ppermute(value, "c", [(0, 1), (1, 0)])
+def swap(value, axis="c"):
+    return lax.ppermute(value, axis, [(0, 1), (1, 0)])
 
 
 def shards(tokens, segments, w_query, w_keyval, grad_context):
@@ -494,6 +553,7 @@
     do_own = grad_context[0]
     x_oth = swap(x_own)
     do_oth = swap(do_own)
+    far_own = swap(x_own, "xl")
     count = 32
     ring = ("zh", "zl", "yl", "c")
     x_own, wkv_here, wq_here, q_own, kv_own = project_own(x_own, w_keyval, w_query)
@@ -502,26 +562,35 @@
     q = project_q(x_oth, q_own, wq_here)
     segs = segments.reshape(-1, BLOCK)
     mix_last, dkv_last, low = attend_last(q, do_own, do_oth, kv, segs)
-    mix, mix_oth, dkv, dkv_sent = attend(q, do_own, do_oth, kv, halo, low, mix_last, dkv_last)
+    mix, mix_oth, kept, sent, dkv, dkv_sent = attend(
+        q, do_own, do_oth, kv, halo, low, mix_last, dkv_last
+    )
     arrived = lax.ppermute(dkv_sent, ring, [(i + 2, i) for i in range(count - 2)])
-    pieces = weight_q(x_own, x_oth, mix, mix_oth)
-    pieces, dkv_own, dkv_oth = weight_kv(x_own, x_oth, dkv, arrived, pieces)
-    pieces = lax.all_to_all(pieces, ("x", "yh", "yl", "zl"), 0, 0)
+    far = swap(sent, "xl")
+    far_own = relay(far_own, kept)
+    far_oth = swap(far_own)
+    near = weight_near(x_own, x_oth, kept)
+    dkv_own, dkv_oth, kept_kv, sent_kv = total_kv(dkv, arrived)
+    far_kv = swap(sent_kv, "xl")
+    near_kv = weight_near(x_own, x_oth, kept_kv)
+    pieces = weight_far(far_own, far_oth, near, far)
+    pieces = weight_far(far_own, far_oth, near_kv, far_kv, pieces)
+    pieces = lax.all_to_all(pieces, ("xh", "yh", "yl", "zl"), 0, 0)
     mix_in = swap(mix_oth)
     dkv_in = swap(dkv_oth)
     grad_in, context, done = grad_tokens(mix, dkv_own, mix_in, dkv_in, w_query, w_keyval)
     plane = sum_plane(pieces, done)
     lines = lax.all_to_all(plane.reshape(8, ROWS, HEAD_DIM), ("zh", "c"), 0, 0)
     blocks = sum_line(lines.reshape(4, 2, ROWS, HEAD_DIM))
-    blocks = lax.all_to_all(blocks, ("x", "yh"), 0, 0)
+    blocks = lax.all_to_all(blocks, ("xh", "xl", "yh"), 0, 0)
     query_w, keyval_w = finish(blocks)
     return context[None], grad_in[None], query_w, keyval_w
 
 
 def solution(mesh):
-    fine = Mesh(mesh.devices.reshape(4, 2, 4, 2, 2, 2), ("x", "yh", "zh", "zl", "yl", "c"))
-    dp = ("x", "yh")
-    ctx = ("zh", "zl", "yl", "c")
+    names = ("xh", "xl", "yh", "zh", "zl", "yl", "c")
+    fine = Mesh(mesh.devices.reshape(2, 2, 2, 4, 2, 2, 2), names)
+    dp, ctx = names[:3], names[3:]
     return jax.shard_map(
         shards,
         mesh=fine,

time: 113 us -> 102 us (0.903); the launches traced: 113 us -> 100 us
  waiting for transfers between devices: 39.1 us -> 25.7 us
    all_to_all x1, waiting for transfers between devices: 32 us -> 11.8 us  [shards(): pieces = lax.all_to_all(pieces, ('xh', 'yh', 'yl', 'zl'), 0, 0)]
    ppermute x4 -> x8, waiting for transfers between devices: 2.15 us -> 7.66 us  [swap(): return lax.ppermute(value, axis, [(0, 1), (1, 0)])]
    ppermute x1, waiting for transfers between devices: 3.93 us -> 5.82 us  [shards(): lax.ppermute(dkv_sent, ring, [(i + 2, i) for i in range(count - 2)])]
    all_to_all x1, blocking collectives: 19.3 us -> 18 us  [shards(): lines = lax.all_to_all(plane.reshape(8, ROWS, HEAD_DIM), ('zh', 'c'), 0, 0)]
    ppermute x1, starting transfers between devices: 1.48 us -> 2.69 us  [shards(): halo = lax.ppermute(kv_sent, ring, [(i, i + 2) for i in range(count - 2)])]
    pallas_call x3 -> x7, Pallas kernels: 10.3 us -> 11.4 us  [the longest x1 6.21 us: attend(): pl.pallas_call(attend_body, in_specs=[VM] * 8, out_specs=[VM] * 6, out_sh...]
    ppermute x4 -> x8, starting transfers between devices: 5.77 us -> 6.58 us  [swap(): return lax.ppermute(value, axis, [(0, 1), (1, 0)])]
  transfers between devices with their start and end apart: 7 -> 11, of which waited for: 5 -> 8; matrix products, arithmetic and copies ran while one was open for 0% -> 0% of each run, Pallas kernels for 11% -> 19%
where the time goes in v6:
time: 102 us; the launch traced here: 100 us
  blocking collectives  27.9 us (27%)
  waiting for transfers between devices  25.7 us (25%)
  Pallas kernels  21.9 us (21%)
  starting transfers between devices  19.5 us (19%)
  local copies, waits for them, and re-layouts  4.69 us (5%)
    all_to_all x1, blocking collectives, shards(): lines = lax.all_to_all(plane.reshape(8, ROWS, HEAD_DIM), ('zh', 'c'), 0, 0)  18 us
    all_to_all x1, waiting for transfers between devices, shards(): pieces = lax.all_to_all(pieces, ('xh', 'yh', 'yl', 'zl'), 0, 0)  11.8 us
    all_to_all x1, blocking collectives, shards(): blocks = lax.all_to_all(blocks, ('xh', 'xl', 'yh'), 0, 0)  9.9 us
    all_to_all x1, starting transfers between devices, shards(): pieces = lax.all_to_all(pieces, ('xh', 'yh', 'yl', 'zl'), 0, 0)  8.96 us
    ppermute x8, waiting for transfers between devices, swap(): return lax.ppermute(value, axis, [(0, 1), (1, 0)])  7.66 us
    ppermute x8, starting transfers between devices, swap(): return lax.ppermute(value, axis, [(0, 1), (1, 0)])  6.58 us
    pallas_call x1, Pallas kernels, attend(): pl.pallas_call(attend_body, in_specs=[VM] * 8, out_specs=[VM] * 6, out_sh...  6.21 us
    ppermute x1, waiting for transfers between devices, shards(): lax.ppermute(dkv_sent, ring, [(i + 2, i) for i in range(count - 2)])  5.82 us
  transfers between devices with their start and end apart: 11, of which 8 were waited for; matrix products, arithmetic and copies ran while one was open for 0% of the time, Pallas kernels for 19%

profile of v6, /device:TPU:1, one launch (start us, length us, event | category | flops | bytes accessed | tf_op | source)
XLA Modules:
  0.0 100.5 jit_solution(4250883379358497481)
XLA Ops:
  0.6 3.3 %collective-permute-start = (bf16[256,1536]{1,0:T(8,128)(2,1)}, bf16[256,1536]{1,0:T(8,128)(2,1)S(1)}, u32[]{:S(2)}, u32[]{:S(2)}) collective-permute-start(bf16[256,1536]{1,0:T(8,128)(2,1)} %bitcast.13), channel_id=1, source_target_pairs={{0,1},{1,0},{2,3},{3,2},{4,5},{5,4},{6,7},{7,6},{8,9},{9,8},{10,11... | collective-permute-start | bytes 2359304 | tf_op jit(solution)/shard_map/ppermute | solution.py:548
  4.0 0.1 collective-permute-start.1
  4.1 0.0 collective-permute-start.6
  4.1 3.4 %project_own.1 = (bf16[256,1536]{1,0:T(8,128)(2,1)S(1)}, bf16[1536,512]{1,0:T(8,128)(2,1)S(1)}, bf16[1536,768]{1,0:T(8,128)(2,1)S(1)}, bf16[256,768]{1,0:T(8,128)(2,1)S(1)}, bf16[256,256]{1,0:T(8,128)(2,1)S(1)}) custom-call(bf16[256,1536]{1,0:T(8,128)(2,1)} %bitcast.15, bf16[1536,512]{1,0:T(8,128)(2,1)} %wkv.3, bf16[1536,1536]{1,0:T(8,128)(2,1)} %wq.3), custom_call_target="tpu_custom_call" | custom-call | flops 805306368 | bytes 5242880 | tf_op jit(solution)/shard_map/project_own/pallas_call | solution.py:106
  7.5 0.0 collective-permute-done.x_oth
  7.5 0.4 project_kv.1
  7.9 2.7 %collective-permute-start.2 = (bf16[384,256]{1,0:T(8,128)(2,1)S(1)}, bf16[384,256]{1,0:T(8,128)(2,1)S(1)}, u32[]{:S(2)}, u32[]{:S(2)}) collective-permute-start(bf16[384,256]{1,0:T(8,128)(2,1)S(1)} %get-tuple-element.34), channel_id=1, source_target_pairs={{0,2},{1,3},{2,4},{3,5},{4,6},{5,7},{6,8},{7,9},{8,10},{9,11},{10,... | collective-permute-start | bytes 589832 | tf_op jit(solution)/shard_map/ppermute | solution.py:561
  10.6 0.0 copy-start.2
  10.6 0.0 copy-start.5
  10.6 0.8 project_q.1.q
  11.4 0.0 collective-permute-done.1.do_oth
  11.4 0.3 copy-done.2
  11.8 0.0 copy-done.5
  11.8 2.0 %attend_last.1 = (bf16[128,1536]{1,0:T(8,128)(2,1)S(1)}, f32[512,256]{1,0:T(8,128)S(1)}, s32[8,128]{1,0:T(8,128)S(1)}) custom-call(bf16[512,768]{1,0:T(8,128)(2,1)S(1)} %project_q.1.q, bf16[256,1536]{1,0:T(8,128)(2,1)S(1)} %bitcast.8, bf16[256,1536]{1,0:T(8,128)(2,1)S(1)} %collective-permute-done.1.do_oth, bf16[512,256]{1,0:T(8,128)(2,1)S(1)} %get-tuple-element.33.kv, ...), custom_call_target="tpu_custom_call" | custom-call | flops 603979776 | bytes 3145728 | tf_op jit(solution)/shard_map/attend_last/pallas_call | solution.py:262
  13.7 0.4 collective-permute-done.2.halo
  14.2 6.2 %attend.1 = (bf16[256,1536]{1,0:T(8,128)(2,1)S(1)}, bf16[256,1536]{1,0:T(8,128)(2,1)S(1)}, bf16[512,384]{1,0:T(8,128)(2,1)S(1)}, bf16[512,384]{1,0:T(8,128)(2,1)...) custom-call(bf16[512,768]{1,0:T(8,128)(2,1)S(1)} %project_q.1.q, bf16[256,1536]{1,0:T(8,128)(2,1)S(1)} %bitcast.9, ...), custom_call_target="tpu_custom_call" | custom-call | flops 1811939328 | bytes 5242880 | tf_op jit(solution)/shard_map/attend/pallas_call | solution.py:320
  20.4 0.0 copy-start.3
  20.4 0.9 copy-done.3
  21.3 0.0 copy-start.6
  21.3 1.7 %collective-permute-done.6.value = bf16[256,1536]{1,0:T(8,128)(2,1)S(1)} collective-permute-done((bf16[256,1536]{1,0:T(8,128)(2,1)}, bf16[256,1536]{1,0:T(8,128)(2,1)S(1)}, u32[]{:S(2)}, u32[]{:S(2)}) %collective-permute-start.6) | collective-permute-done | bytes 786464 | tf_op jit(solution)/shard_map/ppermute | solution.py:548
  23.0 1.2 %collective-permute-start.7 = (bf16[256,1536]{1,0:T(8,128)(2,1)S(1)}, bf16[256,1536]{1,0:T(8,128)(2,1)S(1)}, u32[]{:S(2)}, u32[]{:S(2)}) collective-permute-start(bf16[256,1536]{1,0:T(8,128)(2,1)S(1)} %relay.1.x_own), channel_id=1, source_target_pairs={{0,1},{1,0},{2,3},{3,2},{4,5},{5,4},{6,7},{7,6},{8,9},{9,8},{10,11... | collective-permute-start | bytes 2359304 | tf_op jit(solution)/shard_map/ppermute | solution.py:548
  24.2 1.3 %collective-permute-start.3 = (bf16[384,256]{1,0:T(8,128)(2,1)S(1)}, bf16[384,256]{1,0:T(8,128)(2,1)S(1)}, u32[]{:S(2)}, u32[]{:S(2)}) collective-permute-start(bf16[384,256]{1,0:T(8,128)(2,1)S(1)} %get-tuple-element.40), channel_id=1, source_target_pairs={{2,0},{3,1},{4,2},{5,3},{6,4},{7,5},{8,6},{9,7},{10,8},{11,9},{12,... | collective-permute-start | bytes 589832 | tf_op jit(solution)/shard_map/ppermute | solution.py:568
  25.5 0.3 collective-permute-start.9
  25.8 0.0 copy-done.6
  25.8 1.0 %weight_near.3.near = f32[1536,384]{1,0:T(8,128)S(1)} custom-call(bf16[256,1536]{1,0:T(8,128)(2,1)S(1)} %get-tuple-element.47.x_own, bf16[256,1536]{1,0:T(8,128)(2,1)S(1)} %collective-permute-done.x_oth, bf16[512,384]{1,0:T(8,128)(2,1)S(1)} %get-tuple-element.46.after.g), custom_call_target="tpu_custom_call" | custom-call | flops 6039797760 | bytes 31457280 | tf_op jit(solution)/shard_map/weight_near/pallas_call | solution.py:380
  26.8 5.8 %collective-permute-done.3.arrived = bf16[384,256]{1,0:T(8,128)(2,1)S(1)} collective-permute-done((bf16[384,256]{1,0:T(8,128)(2,1)S(1)}, bf16[384,256]{1,0:T(8,128)(2,1)S(1)}, u32[]{:S(2)}, u32[]{:S(2)}) %collective-permute-start.3) | collective-permute-done | bytes 196640 | tf_op jit(solution)/shard_map/ppermute | solution.py:568
  32.6 0.1 total_kv.1
  32.7 0.1 collective-permute-start.8
  32.8 0.6 weight_near.2.near
  33.5 3.1 %collective-permute-done.9.g = bf16[512,384]{1,0:T(8,128)(2,1)S(1)} collective-permute-done((bf16[512,384]{1,0:T(8,128)(2,1)S(1)}, bf16[512,384]{1,0:T(8,128)(2,1)S(1)}, u32[]{:S(2)}, u32[]{:S(2)}) %collective-permute-start.9) | collective-permute-done | bytes 393248 | tf_op jit(solution)/shard_map/ppermute | solution.py:548
  36.5 0.0 collective-permute-done.7.x_oth
  36.5 2.1 %weight_far.2.rest_0_ = bf16[16,4,2,48,128]{4,3,2,1,0:T(8,128)(2,1)} custom-call(bf16[256,1536]{1,0:T(8,128)(2,1)S(1)} %relay.1.x_own, bf16[256,1536]{1,0:T(8,128)(2,1)S(1)} %collective-permute-done.7.x_oth, f32[1536,384]{1,0:T(8,128)S(1)} %weight_near.3.near, bf16[512,384]{1,0:T(8,128)(2,1)S(1)} %collective-permute-done.9.g), custom_call_target="tpu_custom_call" | custom-call | flops 603979776 | bytes 4194304 | tf_op jit(solution)/shard_map/weight_far/pallas_call | solution.py:439
  38.6 0.7 collective-permute-done.8.g
  39.3 1.4 %weight_far.3 = bf16[16,4,2,48,128]{4,3,2,1,0:T(8,128)(2,1)} custom-call(bf16[256,1536]{1,0:T(8,128)(2,1)S(1)} %relay.1.x_own, bf16[256,1536]{1,0:T(8,128)(2,1)S(1)} %collective-permute-done.7.x_oth, f32[1536,128]{1,0:T(8,128)S(1)} %weight_near.2.near, bf16[512,128]{1,0:T(8,128)(2,1)S(1)} %collective-permute-done.8.g, ...), custom_call_target="tpu_custom_call", output_to_operand_aliasing={{}: (4, {})} | custom-call | flops 201326592 | bytes 4194304 | tf_op jit(solution)/shard_map/weight_far/pallas_call | solution.py:439
  40.7 0.0 copy-start.1
  40.7 9.0 %all-to-all-start = ((bf16[16,4,2,48,128]{4,3,2,1,0:T(8,128)(2,1)}), bf16[16,4,2,48,128]{4,3,2,1,0:T(8,128)(2,1)S(1)}, u32[]{:S(2)}, u32[]{:S(2)}) async-start(bf16[16,4,2,48,128]{4,3,2,1,0:T(8,128)(2,1)} %weight_far.3), calls=%async_computation | async-start | bytes 3145728 | tf_op jit(solution)/shard_map/all_to_all | solution.py:578
  49.7 1.4 %collective-permute-start.4 = (bf16[256,1536]{1,0:T(8,128)(2,1)}, bf16[256,1536]{1,0:T(8,128)(2,1)S(1)}, u32[]{:S(2)}, u32[]{:S(2)}) collective-permute-start(bf16[256,1536]{1,0:T(8,128)(2,1)} %copy-done.6), channel_id=1, source_target_pairs={{0,1},{1,0},{2,3},{3,2},{4,5},{5,4},{6,7},{7,6},{8,9},{9,8},{10,11... | collective-permute-start | bytes 2359304 | tf_op jit(solution)/shard_map/ppermute | solution.py:548
  51.1 0.1 collective-permute-start.5
  51.2 2.0 %collective-permute-done.5.dkv_in = bf16[256,256]{1,0:T(8,128)(2,1)S(1)} collective-permute-done((bf16[256,256]{1,0:T(8,128)(2,1)S(1)}, bf16[256,256]{1,0:T(8,128)(2,1)S(1)}, u32[]{:S(2)}, u32[]{:S(2)}) %collective-permute-start.5) | collective-permute-done | bytes 131104 | tf_op jit(solution)/shard_map/ppermute | solution.py:548
  53.2 0.1 collective-permute-done.4.mix_in
  53.4 0.0 copy-done.1
  53.4 0.0 copy-start
  53.4 2.3 %copy-done = bf16[1536,1536]{1,0:T(8,128)(2,1)S(1)} copy-done((bf16[1536,1536]{1,0:T(8,128)(2,1)S(1)}, bf16[1536,1536]{1,0:T(8,128)(2,1)}, u32[]{:S(2)}) %copy-start) | copy-done | bytes 4718616
  55.7 0.0 copy-start.4
  55.7 1.1 %copy-done.4 = bf16[256,1536]{1,0:T(8,128)(2,1)S(1)} copy-done((bf16[256,1536]{1,0:T(8,128)(2,1)S(1)}, bf16[256,1536]{1,0:T(8,128)(2,1)}, u32[]{:S(2)}) %copy-start.4) | copy-done | bytes 786456
  56.9 3.0 %grad_tokens.1 = (bf16[256,1536]{1,0:T(8,128)(2,1)}, bf16[256,1536]{1,0:T(8,128)(2,1)}, f32[8,128]{1,0:T(8,128)S(1)}) custom-call(bf16[256,1536]{1,0:T(8,128)(2,1)S(1)} %copy-done.4, bf16[256,256]{1,0:T(8,128)(2,1)S(1)} %get-tuple-element.41.dkv, bf16[256,1536]{1,0:T(8,128)(2,1)S(1)} %collective-permute-done.4.mix_in, ...), custom_call_target="tpu_custom_call" | custom-call | flops 1610612736 | bytes 8388608 | tf_op jit(solution)/shard_map/grad_tokens/pallas_call | solution.py:477
  59.9 11.8 %all-to-all-done.pieces = bf16[16,4,2,48,128]{4,3,2,1,0:T(8,128)(2,1)S(1)} async-done(((bf16[16,4,2,48,128]{4,3,2,1,0:T(8,128)(2,1)}), bf16[16,4,2,48,128]{4,3,2,1,0:T(8,128)(2,1)S(1)}, u32[]{:S(2)}, u32[]{:S(2)}) %all-to-all-start) | async-done | bytes 1572896 | tf_op jit(solution)/shard_map/all_to_all | solution.py:578
  71.6 0.2 sum_plane.1
  71.8 18.0 %all_to_all.15 = bf16[8,48,128]{2,1,0:T(8,128)(2,1)S(1)} all-to-all(bf16[8,48,128]{2,1,0:T(8,128)(2,1)S(1)} %bitcast.10), channel_id=1, replica_groups=mesh['xh'=2,'xl'=2,'yh'=2,'zh'=4,'zl'=2,'yl'=2,'c'=2] {'zh','c'}, dimensions={0} | all-to-all | bytes 196608 | tf_op jit(solution)/shard_map/all_to_all | solution.py:583
  89.9 9.9 %all_to_all.16.blocks = bf16[8,2,48,128]{3,2,1,0:T(8,128)(2,1)S(1)} all-to-all(bf16[8,2,48,128]{3,2,1,0:T(8,128)(2,1)S(1)} %sum_line.1), channel_id=1, replica_groups=mesh['xh'=2,'xl'=2,'yh'=2,'zh'=4,'zl'=2,'yl'=2,'c'=2] {'xh','xl','yh'}, dimensions={0} | all-to-all | bytes 393216 | tf_op jit(solution)/shard_map/all_to_all | solution.py:585
  99.8 0.7 finish.1
  (2 shorter events, 0.0 us)
Async XLA Ops:
  0.6 6.9 %collective-permute-start = (bf16[256,1536]{1,0:T(8,128)(2,1)}, bf16[256,1536]{1,0:T(8,128)(2,1)S(1)}, u32[]{:S(2)}, u32[]{:S(2)}) collective-permute-start(bf16[256,1536]{1,0:T(8,128)(2,1)} %bitcast.13), channel_id=1, source_target_pairs={{0,1},{1,0},{2,3},{3,2},{4,5},{5,4},{6,7},{7,6},{8,9},{9,8},{10,11... | collective-permute-start | bytes 2359304 | tf_op jit(solution)/shard_map/ppermute | solution.py:548
  4.0 7.5 %collective-permute-start.1 = (bf16[256,1536]{1,0:T(8,128)(2,1)}, bf16[256,1536]{1,0:T(8,128)(2,1)S(1)}, u32[]{:S(2)}, u32[]{:S(2)}) collective-permute-start(bf16[256,1536]{1,0:T(8,128)(2,1)} %bitcast.7), channel_id=1, source_target_pairs={{0,1},{1,0},{2,3},{3,2},{4,5},{5,4},{6,7},{7,6},{8,9},{9,8},{10,11... | collective-permute-start | bytes 2359304 | tf_op jit(solution)/shard_map/ppermute | solution.py:548
  4.1 18.9 %collective-permute-start.6 = (bf16[256,1536]{1,0:T(8,128)(2,1)}, bf16[256,1536]{1,0:T(8,128)(2,1)S(1)}, u32[]{:S(2)}, u32[]{:S(2)}) collective-permute-start(bf16[256,1536]{1,0:T(8,128)(2,1)} %bitcast.14), channel_id=1, source_target_pairs={{0,64},{64,0},{1,65},{65,1},{2,66},{66,2},{3,67},{67,3},{4,68},{68... | collective-permute-start | bytes 2359304 | tf_op jit(solution)/shard_map/ppermute | solution.py:548
  7.9 6.2 %collective-permute-start.2 = (bf16[384,256]{1,0:T(8,128)(2,1)S(1)}, bf16[384,256]{1,0:T(8,128)(2,1)S(1)}, u32[]{:S(2)}, u32[]{:S(2)}) collective-permute-start(bf16[384,256]{1,0:T(8,128)(2,1)S(1)} %get-tuple-element.34), channel_id=1, source_target_pairs={{0,2},{1,3},{2,4},{3,5},{4,6},{5,7},{6,8},{7,9},{8,10},{9,11},{10,... | collective-permute-start | bytes 589832 | tf_op jit(solution)/shard_map/ppermute | solution.py:561
  10.6 1.1 %copy-start.2 = (bf16[1,256,1536]{2,1,0:T(8,128)(2,1)S(1)}, bf16[1,256,1536]{2,1,0:T(8,128)(2,1)}, u32[]{:S(2)}) copy-start(bf16[1,256,1536]{2,1,0:T(8,128)(2,1)} %param.9) | copy-start | bytes 2359300
  10.6 1.1 %copy-start.5 = (s32[1,8192]{1,0:T(1,128)S(1)}, s32[1,8192]{1,0:T(1,128)}, u32[]{:S(2)}) copy-start(s32[1,8192]{1,0:T(1,128)} %param.6) | copy-start | bytes 98308
  20.4 0.9 copy-start.3
  21.3 4.5 %copy-start.6 = (bf16[256,1536]{1,0:T(8,128)(2,1)}, bf16[256,1536]{1,0:T(8,128)(2,1)S(1)}, u32[]{:S(2)}) copy-start(bf16[256,1536]{1,0:T(8,128)(2,1)S(1)} %get-tuple-element.42) | copy-start | bytes 2359300
  23.0 13.5 %collective-permute-start.7 = (bf16[256,1536]{1,0:T(8,128)(2,1)S(1)}, bf16[256,1536]{1,0:T(8,128)(2,1)S(1)}, u32[]{:S(2)}, u32[]{:S(2)}) collective-permute-start(bf16[256,1536]{1,0:T(8,128)(2,1)S(1)} %relay.1.x_own), channel_id=1, source_target_pairs={{0,1},{1,0},{2,3},{3,2},{4,5},{5,4},{6,7},{7,6},{8,9},{9,8},{10,11... | collective-permute-start | bytes 2359304 | tf_op jit(solution)/shard_map/ppermute | solution.py:548
  24.2 8.4 %collective-permute-start.3 = (bf16[384,256]{1,0:T(8,128)(2,1)S(1)}, bf16[384,256]{1,0:T(8,128)(2,1)S(1)}, u32[]{:S(2)}, u32[]{:S(2)}) collective-permute-start(bf16[384,256]{1,0:T(8,128)(2,1)S(1)} %get-tuple-element.40), channel_id=1, source_target_pairs={{2,0},{3,1},{4,2},{5,3},{6,4},{7,5},{8,6},{9,7},{10,8},{11,9},{12,... | collective-permute-start | bytes 589832 | tf_op jit(solution)/shard_map/ppermute | solution.py:568
  25.5 11.0 %collective-permute-start.9 = (bf16[512,384]{1,0:T(8,128)(2,1)S(1)}, bf16[512,384]{1,0:T(8,128)(2,1)S(1)}, u32[]{:S(2)}, u32[]{:S(2)}) collective-permute-start(bf16[512,384]{1,0:T(8,128)(2,1)S(1)} %get-tuple-element.50), channel_id=1, source_target_pairs={{0,64},{64,0},{1,65},{65,1},{2,66},{66,2},{3,67},{67,3},{4,68},{68... | collective-permute-start | bytes 1179656 | tf_op jit(solution)/shard_map/ppermute | solution.py:548
  32.7 6.6 %collective-permute-start.8 = (bf16[512,128]{1,0:T(8,128)(2,1)S(1)}, bf16[512,128]{1,0:T(8,128)(2,1)S(1)}, u32[]{:S(2)}, u32[]{:S(2)}) collective-permute-start(bf16[512,128]{1,0:T(8,128)(2,1)S(1)} %get-tuple-element.49), channel_id=1, source_target_pairs={{0,64},{64,0},{1,65},{65,1},{2,66},{66,2},{3,67},{67,3},{4,68},{68... | collective-permute-start | bytes 393224 | tf_op jit(solution)/shard_map/ppermute | solution.py:548
  40.7 12.7 %copy-start.1 = (bf16[1536,512]{1,0:T(8,128)(2,1)S(1)}, bf16[1536,512]{1,0:T(8,128)(2,1)}, u32[]{:S(2)}) copy-start(bf16[1536,512]{1,0:T(8,128)(2,1)} %wkv.3) | copy-start | bytes 4718596
  40.7 30.9 %all-to-all-start = ((bf16[16,4,2,48,128]{4,3,2,1,0:T(8,128)(2,1)}), bf16[16,4,2,48,128]{4,3,2,1,0:T(8,128)(2,1)S(1)}, u32[]{:S(2)}, u32[]{:S(2)}) async-start(bf16[16,4,2,48,128]{4,3,2,1,0:T(8,128)(2,1)} %weight_far.3), calls=%async_computation | async-start | bytes 3145728 | tf_op jit(solution)/shard_map/all_to_all | solution.py:578
  49.7 3.7 %collective-permute-start.4 = (bf16[256,1536]{1,0:T(8,128)(2,1)}, bf16[256,1536]{1,0:T(8,128)(2,1)S(1)}, u32[]{:S(2)}, u32[]{:S(2)}) collective-permute-start(bf16[256,1536]{1,0:T(8,128)(2,1)} %copy-done.6), channel_id=1, source_target_pairs={{0,1},{1,0},{2,3},{3,2},{4,5},{5,4},{6,7},{7,6},{8,9},{9,8},{10,11... | collective-permute-start | bytes 2359304 | tf_op jit(solution)/shard_map/ppermute | solution.py:548
  51.1 2.1 %collective-permute-start.5 = (bf16[256,256]{1,0:T(8,128)(2,1)S(1)}, bf16[256,256]{1,0:T(8,128)(2,1)S(1)}, u32[]{:S(2)}, u32[]{:S(2)}) collective-permute-start(bf16[256,256]{1,0:T(8,128)(2,1)S(1)} %get-tuple-element.43), channel_id=1, source_target_pairs={{0,1},{1,0},{2,3},{3,2},{4,5},{5,4},{6,7},{7,6},{8,9},{9,8},{10,11... | collective-permute-start | bytes 393224 | tf_op jit(solution)/shard_map/ppermute | solution.py:548
  53.4 2.3 %copy-start = (bf16[1536,1536]{1,0:T(8,128)(2,1)S(1)}, bf16[1536,1536]{1,0:T(8,128)(2,1)}, u32[]{:S(2)}) copy-start(bf16[1536,1536]{1,0:T(8,128)(2,1)} %wq.3) | copy-start | bytes 14155780
  55.7 1.1 %copy-start.4 = (bf16[256,1536]{1,0:T(8,128)(2,1)S(1)}, bf16[256,1536]{1,0:T(8,128)(2,1)}, u32[]{:S(2)}) copy-start(bf16[256,1536]{1,0:T(8,128)(2,1)} %copy-done.3) | copy-start | bytes 2359300

commit v7 on v6

--- a/solution.py
+++ b/solution.py
@@ -275,18 +275,18 @@
     )(q, do_own, do_oth, kv, segs)
 
 
-def put(b, outs, value):
-    mix_own, mix_oth, kept, sent = outs
+def put(b, value, held, mix_own, mix_oth, kept, sent, sem):
     own = b // 2 == lax.axis_index("c")
-    here = slice((b % 2) * BLOCK, (b % 2 + 1) * BLOCK)
+    rows = pl.ds((b % 2) * BLOCK, BLOCK)
+    held[b] = value
 
     @pl.when(own)
     def _():
-        mix_own[here, :] = value
+        pltpu.make_async_copy(held.at[b], mix_own.at[rows], sem).start()
 
     @pl.when(jnp.logical_not(own))
     def _():
-        mix_oth[here, :] = value
+        pltpu.make_async_copy(held.at[b], mix_oth.at[rows], sem).start()
 
     first = lax.axis_index("xl") == 0
     rows = pl.ds(pl.multiple_of(jnp.where(own, 0, OWN) + (b % 2) * BLOCK, BLOCK), BLOCK)
@@ -297,7 +297,7 @@
 
 
 def attend_body(q, do_own, do_oth, kv, halo, low, mix_last, dkv_last, *rest):
-    *outs, dkv_out, dkv_sent, keys, keys_t, vals_t, dkv = rest
+    mix_own, mix_oth, kept, sent, dkv_out, dkv_sent, keys, keys_t, vals_t, dkv, held, sems = rest
     c = lax.axis_index("c")
     ones = eye(256)
     keys[:HALO] = halo[...]
@@ -305,31 +305,38 @@
     turn_keys(ones, keys, keys_t, vals_t, slice(0, KEYS))
     dkv[:HALO] = jnp.zeros((HALO, KVCOLS), F32)
     dkv[HALO:] = dkv_last[...]
-    put(3, outs, mix_last[...])
+    put(3, mix_last[...], held, mix_own, mix_oth, kept, sent, sems.at[3])
     for b in range(3):
         ctx, dq, grads = attend_block(
             b, range(3), c, q, do_own, do_oth, keys, keys_t, vals_t, low, ones
         )
         dkv[b * BLOCK : b * BLOCK + WINDOW, :] += grads
-        put(b, outs, jnp.concatenate(ctx + dq, axis=1))
+        put(b, jnp.concatenate(ctx + dq, axis=1), held, mix_own, mix_oth, kept, sent, sems.at[b])
     dkv_sent[...] = dkv[:HALO, :].astype(BF16)
     dkv_out[...] = dkv[HALO:, :]
+    for b in range(4):
+        pltpu.make_async_copy(held.at[b], mix_own.at[pl.ds(0, BLOCK)], sems.at[b]).wait()
 
 
 def attend(q, do_own, do_oth, kv, halo, low, mix_last, dkv_last):
     return pl.pallas_call(
         attend_body,
         in_specs=[VM] * 8,
-        out_specs=[VM] * 6,
+        out_specs=[ANY] * 2 + [VM] * 4,
         out_shape=[
-            shape((OWN, 2 * QCOLS)),
-            shape((OWN, 2 * QCOLS)),
+            pltpu.HBM((OWN, 2 * QCOLS), BF16),
+            pltpu.HBM((OWN, 2 * QCOLS), BF16),
             shape((PAIR, KEEP)),
             shape((PAIR, KEEP)),
             shape((PAIR, KVCOLS), F32),
             shape((HALO, KVCOLS)),
         ],
-        scratch_shapes=KEY_SCRATCH + [pltpu.VMEM((KEYS, KVCOLS), F32)],
+        scratch_shapes=KEY_SCRATCH
+        + [
+            pltpu.VMEM((KEYS, KVCOLS), F32),
+            pltpu.VMEM((4, BLOCK, 2 * QCOLS), BF16),
+            pltpu.SemaphoreType.DMA((4,)),
+        ],
         compiler_params=params(),
         cost_estimate=cost(3 * 2 * BLOCK * WINDOW * QCOLS * 6, 5 << 20, 3 * BLOCK * WINDOW * 6),
         name="attend",
@@ -553,11 +560,11 @@
     do_own = grad_context[0]
     x_oth = swap(x_own)
     do_oth = swap(do_own)
-    far_own = swap(x_own, "xl")
     count = 32
     ring = ("zh", "zl", "yl", "c")
     x_own, wkv_here, wq_here, q_own, kv_own = project_own(x_own, w_keyval, w_query)
     kv, kv_sent = project_kv(x_oth, kv_own, wkv_here)
+    far_own = swap(x_own, "xl")
     halo = lax.ppermute(kv_sent, ring, [(i, i + 2) for i in range(count - 2)])
     q = project_q(x_oth, q_own, wq_here)
     segs = segments.reshape(-1, BLOCK)
@@ -567,9 +574,9 @@
     )
     arrived = lax.ppermute(dkv_sent, ring, [(i + 2, i) for i in range(count - 2)])
     far = swap(sent, "xl")
+    near = weight_near(x_own, x_oth, kept)
     far_own = relay(far_own, kept)
     far_oth = swap(far_own)
-    near = weight_near(x_own, x_oth, kept)
     dkv_own, dkv_oth, kept_kv, sent_kv = total_kv(dkv, arrived)
     far_kv = swap(sent_kv, "xl")
     near_kv = weight_near(x_own, x_oth, kept_kv)

time: 102 us -> 104 us (1.020)
  waiting for transfers between devices: 25.7 us -> 29.6 us
  starting transfers between devices: 19.5 us -> 18 us
    ppermute x8, waiting for transfers between devices: 7.66 us -> 11.7 us  [swap(): return lax.ppermute(value, axis, [(0, 1), (1, 0)])]
    all_to_all x1, starting transfers between devices: 8.96 us -> 7.36 us  [shards(): pieces = lax.all_to_all(pieces, ('xh', 'yh', 'yl', 'zl'), 0, 0)]
    unnamed x14 -> x10, local copies, waits for them, and re-layouts: 4.69 us -> 3.8 us
where the time goes in v7:
time: 104 us; the launch traced here: 102 us
  waiting for transfers between devices  29.6 us (28%)
  blocking collectives  28.1 us (27%)
  Pallas kernels  22.1 us (21%)
  starting transfers between devices  18 us (17%)
  local copies, waits for them, and re-layouts  3.8 us (4%)
    all_to_all x1, blocking collectives, shards(): lines = lax.all_to_all(plane.reshape(8, ROWS, HEAD_DIM), ('zh', 'c'), 0, 0)  18.2 us
    all_to_all x1, waiting for transfers between devices, shards(): pieces = lax.all_to_all(pieces, ('xh', 'yh', 'yl', 'zl'), 0, 0)  11.7 us
    ppermute x8, waiting for transfers between devices, swap(): return lax.ppermute(value, axis, [(0, 1), (1, 0)])  11.7 us
    all_to_all x1, blocking collectives, shards(): blocks = lax.all_to_all(blocks, ('xh', 'xl', 'yh'), 0, 0)  9.93 us
    all_to_all x1, starting transfers between devices, shards(): pieces = lax.all_to_all(pieces, ('xh', 'yh', 'yl', 'zl'), 0, 0)  7.36 us
    ppermute x8, starting transfers between devices, swap(): return lax.ppermute(value, axis, [(0, 1), (1, 0)])  6.71 us
    pallas_call x1, Pallas kernels, attend(): pl.pallas_call(attend_body, in_specs=[VM] * 8, out_specs=[ANY] * 2 + [VM]...  6.33 us
    ppermute x1, waiting for transfers between devices, shards(): lax.ppermute(dkv_sent, ring, [(i + 2, i) for i in range(count - 2)])  5.82 us
  transfers between devices with their start and end apart: 11, of which 8 were waited for; matrix products, arithmetic and copies ran while one was open for 0% of the time, Pallas kernels for 19%

profile of v7, /device:TPU:1, one launch (start us, length us, event | category | flops | bytes accessed | tf_op | source)
XLA Modules:
  0.0 102.4 jit_solution(17851739652304731406)
XLA Ops:
  0.6 3.3 %collective-permute-start = (bf16[256,1536]{1,0:T(8,128)(2,1)}, bf16[256,1536]{1,0:T(8,128)(2,1)S(1)}, u32[]{:S(2)}, u32[]{:S(2)}) collective-permute-start(bf16[256,1536]{1,0:T(8,128)(2,1)} %bitcast.13), channel_id=1, source_target_pairs={{0,1},{1,0},{2,3},{3,2},{4,5},{5,4},{6,7},{7,6},{8,9},{9,8},{10,11... | collective-permute-start | bytes 2359304 | tf_op jit(solution)/shard_map/ppermute | solution.py:555
  4.0 0.1 collective-permute-start.1
  4.1 3.5 %project_own.1 = (bf16[256,1536]{1,0:T(8,128)(2,1)S(1)}, bf16[1536,512]{1,0:T(8,128)(2,1)S(1)}, bf16[1536,768]{1,0:T(8,128)(2,1)S(1)}, bf16[256,768]{1,0:T(8,128)(2,1)S(1)}, bf16[256,256]{1,0:T(8,128)(2,1)S(1)}) custom-call(bf16[256,1536]{1,0:T(8,128)(2,1)} %bitcast.14, bf16[1536,512]{1,0:T(8,128)(2,1)} %wkv.3, bf16[1536,1536]{1,0:T(8,128)(2,1)} %wq.3), custom_call_target="tpu_custom_call" | custom-call | flops 805306368 | bytes 5242880 | tf_op jit(solution)/shard_map/project_own/pallas_call | solution.py:106
  7.5 0.1 collective-permute-start.6
  7.6 0.0 collective-permute-done.x_oth
  7.6 0.4 project_kv.1
  8.0 2.7 %collective-permute-start.2 = (bf16[384,256]{1,0:T(8,128)(2,1)S(1)}, bf16[384,256]{1,0:T(8,128)(2,1)S(1)}, u32[]{:S(2)}, u32[]{:S(2)}) collective-permute-start(bf16[384,256]{1,0:T(8,128)(2,1)S(1)} %get-tuple-element.34), channel_id=1, source_target_pairs={{0,2},{1,3},{2,4},{3,5},{4,6},{5,7},{6,8},{7,9},{8,10},{9,11},{10,... | collective-permute-start | bytes 589832 | tf_op jit(solution)/shard_map/ppermute | solution.py:568
  10.7 0.0 copy-start.2
  10.7 0.0 copy-start.4
  10.7 0.8 project_q.1.q
  11.5 0.0 collective-permute-done.1.do_oth
  11.5 0.3 copy-done.2
  11.8 0.0 copy-done.4
  11.8 2.0 %attend_last.1 = (bf16[128,1536]{1,0:T(8,128)(2,1)S(1)}, f32[512,256]{1,0:T(8,128)S(1)}, s32[8,128]{1,0:T(8,128)S(1)}) custom-call(bf16[512,768]{1,0:T(8,128)(2,1)S(1)} %project_q.1.q, bf16[256,1536]{1,0:T(8,128)(2,1)S(1)} %bitcast.8, bf16[256,1536]{1,0:T(8,128)(2,1)S(1)} %collective-permute-done.1.do_oth, bf16[512,256]{1,0:T(8,128)(2,1)S(1)} %get-tuple-element.33.kv, ...), custom_call_target="tpu_custom_call" | custom-call | flops 603979776 | bytes 3145728 | tf_op jit(solution)/shard_map/attend_last/pallas_call | solution.py:262
  13.8 0.4 collective-permute-done.2.halo
  14.2 6.3 %attend.1 = (bf16[256,1536]{1,0:T(8,128)(2,1)}, bf16[256,1536]{1,0:T(8,128)(2,1)}, bf16[512,384]{1,0:T(8,128)(2,1)S(1)}, bf16[512,384]{1,0:T(8,128)(2,1)S(1)}, f...) custom-call(bf16[512,768]{1,0:T(8,128)(2,1)S(1)} %project_q.1.q, bf16[256,1536]{1,0:T(8,128)(2,1)S(1)} %bitcast.9, ...), custom_call_target="tpu_custom_call" | custom-call | flops 1811939328 | bytes 5242880 | tf_op jit(solution)/shard_map/attend/pallas_call | solution.py:322
  20.6 5.7 %collective-permute-done.6.value = bf16[256,1536]{1,0:T(8,128)(2,1)S(1)} collective-permute-done((bf16[256,1536]{1,0:T(8,128)(2,1)S(1)}, bf16[256,1536]{1,0:T(8,128)(2,1)S(1)}, u32[]{:S(2)}, u32[]{:S(2)}) %collective-permute-start.6) | collective-permute-done | bytes 786464 | tf_op jit(solution)/shard_map/ppermute | solution.py:555
  26.3 1.2 %collective-permute-start.7 = (bf16[256,1536]{1,0:T(8,128)(2,1)S(1)}, bf16[256,1536]{1,0:T(8,128)(2,1)S(1)}, u32[]{:S(2)}, u32[]{:S(2)}) collective-permute-start(bf16[256,1536]{1,0:T(8,128)(2,1)S(1)} %relay.1.x_own), channel_id=1, source_target_pairs={{0,1},{1,0},{2,3},{3,2},{4,5},{5,4},{6,7},{7,6},{8,9},{9,8},{10,11... | collective-permute-start | bytes 2359304 | tf_op jit(solution)/shard_map/ppermute | solution.py:555
  27.6 1.3 %collective-permute-start.3 = (bf16[384,256]{1,0:T(8,128)(2,1)S(1)}, bf16[384,256]{1,0:T(8,128)(2,1)S(1)}, u32[]{:S(2)}, u32[]{:S(2)}) collective-permute-start(bf16[384,256]{1,0:T(8,128)(2,1)S(1)} %get-tuple-element.40), channel_id=1, source_target_pairs={{2,0},{3,1},{4,2},{5,3},{6,4},{7,5},{8,6},{9,7},{10,8},{11,9},{12,... | collective-permute-start | bytes 589832 | tf_op jit(solution)/shard_map/ppermute | solution.py:575
  28.9 0.3 collective-permute-start.9
  29.1 1.0 weight_near.3.near
  30.2 5.8 %collective-permute-done.3.arrived = bf16[384,256]{1,0:T(8,128)(2,1)S(1)} collective-permute-done((bf16[384,256]{1,0:T(8,128)(2,1)S(1)}, bf16[384,256]{1,0:T(8,128)(2,1)S(1)}, u32[]{:S(2)}, u32[]{:S(2)}) %collective-permute-start.3) | collective-permute-done | bytes 196640 | tf_op jit(solution)/shard_map/ppermute | solution.py:575
  36.0 0.1 total_kv.1
  36.1 0.1 collective-permute-start.8
  36.2 0.6 weight_near.2.near
  36.8 3.1 %collective-permute-done.9.g = bf16[512,384]{1,0:T(8,128)(2,1)S(1)} collective-permute-done((bf16[512,384]{1,0:T(8,128)(2,1)S(1)}, bf16[512,384]{1,0:T(8,128)(2,1)S(1)}, u32[]{:S(2)}, u32[]{:S(2)}) %collective-permute-start.9) | collective-permute-done | bytes 393248 | tf_op jit(solution)/shard_map/ppermute | solution.py:555
  39.9 0.0 collective-permute-done.7.x_oth
  39.9 2.1 %weight_far.2.rest_0_ = bf16[16,4,2,48,128]{4,3,2,1,0:T(8,128)(2,1)} custom-call(bf16[256,1536]{1,0:T(8,128)(2,1)S(1)} %relay.1.x_own, bf16[256,1536]{1,0:T(8,128)(2,1)S(1)} %collective-permute-done.7.x_oth, f32[1536,384]{1,0:T(8,128)S(1)} %weight_near.3.near, bf16[512,384]{1,0:T(8,128)(2,1)S(1)} %collective-permute-done.9.g), custom_call_target="tpu_custom_call" | custom-call | flops 603979776 | bytes 4194304 | tf_op jit(solution)/shard_map/weight_far/pallas_call | solution.py:446
  42.0 0.7 collective-permute-done.8.g
  42.7 1.4 %weight_far.3 = bf16[16,4,2,48,128]{4,3,2,1,0:T(8,128)(2,1)} custom-call(bf16[256,1536]{1,0:T(8,128)(2,1)S(1)} %relay.1.x_own, bf16[256,1536]{1,0:T(8,128)(2,1)S(1)} %collective-permute-done.7.x_oth, f32[1536,128]{1,0:T(8,128)S(1)} %weight_near.2.near, bf16[512,128]{1,0:T(8,128)(2,1)S(1)} %collective-permute-done.8.g, ...), custom_call_target="tpu_custom_call", output_to_operand_aliasing={{}: (4, {})} | custom-call | flops 201326592 | bytes 4194304 | tf_op jit(solution)/shard_map/weight_far/pallas_call | solution.py:446
  44.1 0.0 copy-start.1
  44.1 7.4 %all-to-all-start = ((bf16[16,4,2,48,128]{4,3,2,1,0:T(8,128)(2,1)}), bf16[16,4,2,48,128]{4,3,2,1,0:T(8,128)(2,1)S(1)}, u32[]{:S(2)}, u32[]{:S(2)}) async-start(bf16[16,4,2,48,128]{4,3,2,1,0:T(8,128)(2,1)} %weight_far.3), calls=%async_computation | async-start | bytes 3145728 | tf_op jit(solution)/shard_map/all_to_all | solution.py:585
  51.4 1.5 %collective-permute-start.4 = (bf16[256,1536]{1,0:T(8,128)(2,1)}, bf16[256,1536]{1,0:T(8,128)(2,1)S(1)}, u32[]{:S(2)}, u32[]{:S(2)}) collective-permute-start(bf16[256,1536]{1,0:T(8,128)(2,1)} %get-tuple-element.42), channel_id=1, source_target_pairs={{0,1},{1,0},{2,3},{3,2},{4,5},{5,4},{6,7},{7,6},{8,9},{9,8},{10,11... | collective-permute-start | bytes 2359304 | tf_op jit(solution)/shard_map/ppermute | solution.py:555
  52.9 0.1 collective-permute-start.5
  53.0 2.0 %collective-permute-done.5.dkv_in = bf16[256,256]{1,0:T(8,128)(2,1)S(1)} collective-permute-done((bf16[256,256]{1,0:T(8,128)(2,1)S(1)}, bf16[256,256]{1,0:T(8,128)(2,1)S(1)}, u32[]{:S(2)}, u32[]{:S(2)}) %collective-permute-start.5) | collective-permute-done | bytes 131104 | tf_op jit(solution)/shard_map/ppermute | solution.py:555
  55.0 0.1 collective-permute-done.4.mix_in
  55.2 0.0 copy-done.1
  55.2 0.0 copy-start
  55.2 2.3 %copy-done = bf16[1536,1536]{1,0:T(8,128)(2,1)S(1)} copy-done((bf16[1536,1536]{1,0:T(8,128)(2,1)S(1)}, bf16[1536,1536]{1,0:T(8,128)(2,1)}, u32[]{:S(2)}) %copy-start) | copy-done | bytes 4718616
  57.5 0.0 copy-start.3
  57.5 1.1 %copy-done.3 = bf16[256,1536]{1,0:T(8,128)(2,1)S(1)} copy-done((bf16[256,1536]{1,0:T(8,128)(2,1)S(1)}, bf16[256,1536]{1,0:T(8,128)(2,1)}, u32[]{:S(2)}) %copy-start.3) | copy-done | bytes 786456
  58.6 3.0 %grad_tokens.1 = (bf16[256,1536]{1,0:T(8,128)(2,1)}, bf16[256,1536]{1,0:T(8,128)(2,1)}, f32[8,128]{1,0:T(8,128)S(1)}) custom-call(bf16[256,1536]{1,0:T(8,128)(2,1)S(1)} %copy-done.3, bf16[256,256]{1,0:T(8,128)(2,1)S(1)} %get-tuple-element.41.dkv, bf16[256,1536]{1,0:T(8,128)(2,1)S(1)} %collective-permute-done.4.mix_in, ...), custom_call_target="tpu_custom_call" | custom-call | flops 1610612736 | bytes 8388608 | tf_op jit(solution)/shard_map/grad_tokens/pallas_call | solution.py:484
  61.6 11.7 %all-to-all-done.pieces = bf16[16,4,2,48,128]{4,3,2,1,0:T(8,128)(2,1)S(1)} async-done(((bf16[16,4,2,48,128]{4,3,2,1,0:T(8,128)(2,1)}), bf16[16,4,2,48,128]{4,3,2,1,0:T(8,128)(2,1)S(1)}, u32[]{:S(2)}, u32[]{:S(2)}) %all-to-all-start) | async-done | bytes 1572896 | tf_op jit(solution)/shard_map/all_to_all | solution.py:585
  73.4 0.2 sum_plane.1
  73.6 18.2 %all_to_all.15 = bf16[8,48,128]{2,1,0:T(8,128)(2,1)S(1)} all-to-all(bf16[8,48,128]{2,1,0:T(8,128)(2,1)S(1)} %bitcast.10), channel_id=1, replica_groups=mesh['xh'=2,'xl'=2,'yh'=2,'zh'=4,'zl'=2,'yl'=2,'c'=2] {'zh','c'}, dimensions={0} | all-to-all | bytes 196608 | tf_op jit(solution)/shard_map/all_to_all | solution.py:590
  91.8 9.9 %all_to_all.16.blocks = bf16[8,2,48,128]{3,2,1,0:T(8,128)(2,1)S(1)} all-to-all(bf16[8,2,48,128]{3,2,1,0:T(8,128)(2,1)S(1)} %sum_line.1), channel_id=1, replica_groups=mesh['xh'=2,'xl'=2,'yh'=2,'zh'=4,'zl'=2,'yl'=2,'c'=2] {'xh','xl','yh'}, dimensions={0} | all-to-all | bytes 393216 | tf_op jit(solution)/shard_map/all_to_all | solution.py:592
  101.7 0.7 finish.1
  (2 shorter events, 0.0 us)
Async XLA Ops:
  0.6 7.0 %collective-permute-start = (bf16[256,1536]{1,0:T(8,128)(2,1)}, bf16[256,1536]{1,0:T(8,128)(2,1)S(1)}, u32[]{:S(2)}, u32[]{:S(2)}) collective-permute-start(bf16[256,1536]{1,0:T(8,128)(2,1)} %bitcast.13), channel_id=1, source_target_pairs={{0,1},{1,0},{2,3},{3,2},{4,5},{5,4},{6,7},{7,6},{8,9},{9,8},{10,11... | collective-permute-start | bytes 2359304 | tf_op jit(solution)/shard_map/ppermute | solution.py:555
  4.0 7.6 %collective-permute-start.1 = (bf16[256,1536]{1,0:T(8,128)(2,1)}, bf16[256,1536]{1,0:T(8,128)(2,1)S(1)}, u32[]{:S(2)}, u32[]{:S(2)}) collective-permute-start(bf16[256,1536]{1,0:T(8,128)(2,1)} %bitcast.7), channel_id=1, source_target_pairs={{0,1},{1,0},{2,3},{3,2},{4,5},{5,4},{6,7},{7,6},{8,9},{9,8},{10,11... | collective-permute-start | bytes 2359304 | tf_op jit(solution)/shard_map/ppermute | solution.py:555
  7.5 18.8 %collective-permute-start.6 = (bf16[256,1536]{1,0:T(8,128)(2,1)S(1)}, bf16[256,1536]{1,0:T(8,128)(2,1)S(1)}, u32[]{:S(2)}, u32[]{:S(2)}) collective-permute-start(bf16[256,1536]{1,0:T(8,128)(2,1)S(1)} %get-tuple-element.46.x_own), channel_id=1, source_target_pairs={{0,64},{64,0},{1,65},{65,1},{2,66},{66,2},{3,67},{67,3},{4,68},{68... | collective-permute-start | bytes 2359304 | tf_op jit(solution)/shard_map/ppermute | solution.py:555
  8.0 6.2 %collective-permute-start.2 = (bf16[384,256]{1,0:T(8,128)(2,1)S(1)}, bf16[384,256]{1,0:T(8,128)(2,1)S(1)}, u32[]{:S(2)}, u32[]{:S(2)}) collective-permute-start(bf16[384,256]{1,0:T(8,128)(2,1)S(1)} %get-tuple-element.34), channel_id=1, source_target_pairs={{0,2},{1,3},{2,4},{3,5},{4,6},{5,7},{6,8},{7,9},{8,10},{9,11},{10,... | collective-permute-start | bytes 589832 | tf_op jit(solution)/shard_map/ppermute | solution.py:568
  10.7 1.1 %copy-start.2 = (bf16[1,256,1536]{2,1,0:T(8,128)(2,1)S(1)}, bf16[1,256,1536]{2,1,0:T(8,128)(2,1)}, u32[]{:S(2)}) copy-start(bf16[1,256,1536]{2,1,0:T(8,128)(2,1)} %param.9) | copy-start | bytes 2359300
  10.7 1.1 %copy-start.4 = (s32[1,8192]{1,0:T(1,128)S(1)}, s32[1,8192]{1,0:T(1,128)}, u32[]{:S(2)}) copy-start(s32[1,8192]{1,0:T(1,128)} %param.6) | copy-start | bytes 98308
  26.3 13.5 %collective-permute-start.7 = (bf16[256,1536]{1,0:T(8,128)(2,1)S(1)}, bf16[256,1536]{1,0:T(8,128)(2,1)S(1)}, u32[]{:S(2)}, u32[]{:S(2)}) collective-permute-start(bf16[256,1536]{1,0:T(8,128)(2,1)S(1)} %relay.1.x_own), channel_id=1, source_target_pairs={{0,1},{1,0},{2,3},{3,2},{4,5},{5,4},{6,7},{7,6},{8,9},{9,8},{10,11... | collective-permute-start | bytes 2359304 | tf_op jit(solution)/shard_map/ppermute | solution.py:555
  27.6 8.4 %collective-permute-start.3 = (bf16[384,256]{1,0:T(8,128)(2,1)S(1)}, bf16[384,256]{1,0:T(8,128)(2,1)S(1)}, u32[]{:S(2)}, u32[]{:S(2)}) collective-permute-start(bf16[384,256]{1,0:T(8,128)(2,1)S(1)} %get-tuple-element.40), channel_id=1, source_target_pairs={{2,0},{3,1},{4,2},{5,3},{6,4},{7,5},{8,6},{9,7},{10,8},{11,9},{12,... | collective-permute-start | bytes 589832 | tf_op jit(solution)/shard_map/ppermute | solution.py:575
  28.9 11.0 %collective-permute-start.9 = (bf16[512,384]{1,0:T(8,128)(2,1)S(1)}, bf16[512,384]{1,0:T(8,128)(2,1)S(1)}, u32[]{:S(2)}, u32[]{:S(2)}) collective-permute-start(bf16[512,384]{1,0:T(8,128)(2,1)S(1)} %get-tuple-element.50), channel_id=1, source_target_pairs={{0,64},{64,0},{1,65},{65,1},{2,66},{66,2},{3,67},{67,3},{4,68},{68... | collective-permute-start | bytes 1179656 | tf_op jit(solution)/shard_map/ppermute | solution.py:555
  36.1 6.6 %collective-permute-start.8 = (bf16[512,128]{1,0:T(8,128)(2,1)S(1)}, bf16[512,128]{1,0:T(8,128)(2,1)S(1)}, u32[]{:S(2)}, u32[]{:S(2)}) collective-permute-start(bf16[512,128]{1,0:T(8,128)(2,1)S(1)} %get-tuple-element.49), channel_id=1, source_target_pairs={{0,64},{64,0},{1,65},{65,1},{2,66},{66,2},{3,67},{67,3},{4,68},{68... | collective-permute-start | bytes 393224 | tf_op jit(solution)/shard_map/ppermute | solution.py:555
  44.1 11.1 %copy-start.1 = (bf16[1536,512]{1,0:T(8,128)(2,1)S(1)}, bf16[1536,512]{1,0:T(8,128)(2,1)}, u32[]{:S(2)}) copy-start(bf16[1536,512]{1,0:T(8,128)(2,1)} %wkv.3) | copy-start | bytes 4718596
  44.1 29.3 %all-to-all-start = ((bf16[16,4,2,48,128]{4,3,2,1,0:T(8,128)(2,1)}), bf16[16,4,2,48,128]{4,3,2,1,0:T(8,128)(2,1)S(1)}, u32[]{:S(2)}, u32[]{:S(2)}) async-start(bf16[16,4,2,48,128]{4,3,2,1,0:T(8,128)(2,1)} %weight_far.3), calls=%async_computation | async-start | bytes 3145728 | tf_op jit(solution)/shard_map/all_to_all | solution.py:585
  51.4 3.7 %collective-permute-start.4 = (bf16[256,1536]{1,0:T(8,128)(2,1)}, bf16[256,1536]{1,0:T(8,128)(2,1)S(1)}, u32[]{:S(2)}, u32[]{:S(2)}) collective-permute-start(bf16[256,1536]{1,0:T(8,128)(2,1)} %get-tuple-element.42), channel_id=1, source_target_pairs={{0,1},{1,0},{2,3},{3,2},{4,5},{5,4},{6,7},{7,6},{8,9},{9,8},{10,11... | collective-permute-start | bytes 2359304 | tf_op jit(solution)/shard_map/ppermute | solution.py:555
  52.9 2.1 %collective-permute-start.5 = (bf16[256,256]{1,0:T(8,128)(2,1)S(1)}, bf16[256,256]{1,0:T(8,128)(2,1)S(1)}, u32[]{:S(2)}, u32[]{:S(2)}) collective-permute-start(bf16[256,256]{1,0:T(8,128)(2,1)S(1)} %get-tuple-element.43), channel_id=1, source_target_pairs={{0,1},{1,0},{2,3},{3,2},{4,5},{5,4},{6,7},{7,6},{8,9},{9,8},{10,11... | collective-permute-start | bytes 393224 | tf_op jit(solution)/shard_map/ppermute | solution.py:555
  55.2 2.3 %copy-start = (bf16[1536,1536]{1,0:T(8,128)(2,1)S(1)}, bf16[1536,1536]{1,0:T(8,128)(2,1)}, u32[]{:S(2)}) copy-start(bf16[1536,1536]{1,0:T(8,128)(2,1)} %wq.3) | copy-start | bytes 14155780
  57.5 1.1 %copy-start.3 = (bf16[256,1536]{1,0:T(8,128)(2,1)S(1)}, bf16[256,1536]{1,0:T(8,128)(2,1)}, u32[]{:S(2)}) copy-start(bf16[256,1536]{1,0:T(8,128)(2,1)} %get-tuple-element.38.mix) | copy-start | bytes 2359300

commit v8 on v7

--- a/solution.py
+++ b/solution.py
@@ -509,9 +509,7 @@
 
 
 def sum_line_body(lines, out):
-    total = jnp.sum(lines[...].astype(F32), axis=0).astype(BF16)
-    for s in range(8):
-        out[s] = total
+    out[...] = jnp.sum(lines[...].astype(F32), axis=0).astype(BF16)
 
 
 def sum_line(lines):
@@ -519,36 +517,58 @@
         sum_line_body,
         in_specs=[VM],
         out_specs=VM,
-        out_shape=shape((8, 2, ROWS, HEAD_DIM)),
+        out_shape=shape(lines.shape[1:]),
         compiler_params=params(),
         name="sum_line",
     )(lines)
 
 
-def finish_body(blocks, query_w, keyval_w):
-    for xh in range(2):
-        for xl in range(2):
-            for yh in range(2):
-                for core in range(2):
-                    rows = blocks[(xh * 2 + xl) * 2 + yh, core]
-                    block = xh * 2 + yh
-                    if block < 3:
-                        at = (core * GROUP + xl * 3 + block) * HEAD_DIM
-                        query_w[:, at : at + HEAD_DIM] = rows
-                    else:
-                        at = (xl * KV_HEADS + core) * HEAD_DIM
-                        keyval_w[:, at : at + HEAD_DIM] = rows
+def stack_body(near, far, out):
+    first = lax.axis_index("yh") == 0
+    one = near[...]
+    two = far[...]
+    out[0] = jnp.where(first, one, two)
+    out[1] = jnp.where(first, two, one)
+
+
+def stack(near, far):
+    return pl.pallas_call(
+        stack_body,
+        in_specs=[VM] * 2,
+        out_specs=VM,
+        out_shape=shape((2,) + near.shape),
+        compiler_params=params(),
+        name="stack",
+    )(near, far)
+
+
+def finish_body(one, two, three, four, query_w, keyval_w):
+    x = lax.axis_index(("xh", "xl"))
+    for source in range(4):
+        value = one[...]
+        for turn, other in enumerate((two, three, four), 1):
+            value = jnp.where((source + turn) % 4 == x, other[...], value)
+        xh, xl = source // 2, source % 2
+        for yh in range(2):
+            for core in range(2):
+                block = xh * 2 + yh
+                if block < 3:
+                    at = (core * GROUP + xl * 3 + block) * HEAD_DIM
+                    query_w[:, at : at + HEAD_DIM] = value[yh, core]
+                else:
+                    at = (xl * KV_HEADS + core) * HEAD_DIM
+                    keyval_w[:, at : at + HEAD_DIM] = value[yh, core]
 
 
 def finish(blocks):
     return pl.pallas_call(
         finish_body,
-        in_specs=[VM],
+        in_specs=[VM] * 4,
         out_specs=[VM, VM],
         out_shape=[shape((ROWS, D)), shape((ROWS, 512))],
         compiler_params=params(),
         name="finish",
-    )(blocks)
+    )(*blocks)
 
 
 def swap(value, axis="c"):
@@ -560,11 +580,11 @@
     do_own = grad_context[0]
     x_oth = swap(x_own)
     do_oth = swap(do_own)
+    far_own = swap(x_own, "xl")
     count = 32
     ring = ("zh", "zl", "yl", "c")
     x_own, wkv_here, wq_here, q_own, kv_own = project_own(x_own, w_keyval, w_query)
     kv, kv_sent = project_kv(x_oth, kv_own, wkv_here)
-    far_own = swap(x_own, "xl")
     halo = lax.ppermute(kv_sent, ring, [(i, i + 2) for i in range(count - 2)])
     q = project_q(x_oth, q_own, wq_here)
     segs = segments.reshape(-1, BLOCK)
@@ -589,8 +609,12 @@
     plane = sum_plane(pieces, done)
     lines = lax.all_to_all(plane.reshape(8, ROWS, HEAD_DIM), ("zh", "c"), 0, 0)
     blocks = sum_line(lines.reshape(4, 2, ROWS, HEAD_DIM))
-    blocks = lax.all_to_all(blocks, ("xh", "xl", "yh"), 0, 0)
-    query_w, keyval_w = finish(blocks)
+    blocks = stack(blocks, swap(blocks, "yh"))
+    around = [
+        lax.ppermute(blocks, ("xh", "xl"), [(i, (i + turn) % 4) for i in range(4)])
+        for turn in range(1, 4)
+    ]
+    query_w, keyval_w = finish([blocks] + around)
     return context[None], grad_in[None], query_w, keyval_w
 
 

time: 104 us -> 103 us (level)
  blocking collectives: 28.1 us -> 18 us
  waiting for transfers between devices: 29.6 us -> 34.7 us
  starting transfers between devices: 18 us -> 21.3 us
    all_to_all x1 -> x0, blocking collectives: 9.93 us -> none  [shards(): blocks = lax.all_to_all(blocks, ('xh', 'xl', 'yh'), 0, 0)]
    ppermute x0 -> x3, waiting for transfers between devices: none -> 4.15 us  [shards(): lax.ppermute(blocks, ('xh', 'xl'), [(i, (i + turn) % 4) for i in range(4)])]
    ppermute x0 -> x3, starting transfers between devices: none -> 2.32 us  [shards(): lax.ppermute(blocks, ('xh', 'xl'), [(i, (i + turn) % 4) for i in range(4)])]
    ppermute x8 -> x9, waiting for transfers between devices: 11.7 us -> 12.6 us  [swap(): return lax.ppermute(value, axis, [(0, 1), (1, 0)])]
    ppermute x8 -> x9, starting transfers between devices: 6.71 us -> 6.74 us  [swap(): return lax.ppermute(value, axis, [(0, 1), (1, 0)])]
  transfers between devices with their start and end apart: 11 -> 15, of which waited for: 8 -> 12; matrix products, arithmetic and copies ran while one was open for 0% -> 0% of each run, Pallas kernels for 19% -> 20%
where the time goes in v8:
time: 103 us; the launch traced here: 101 us
  waiting for transfers between devices  34.7 us (34%)
  Pallas kernels  22.1 us (21%)
  starting transfers between devices  21.3 us (21%)
  blocking collectives  18 us (17%)
  local copies, waits for them, and re-layouts  3.81 us (4%)
    all_to_all x1, blocking collectives, shards(): lines = lax.all_to_all(plane.reshape(8, ROWS, HEAD_DIM), ('zh', 'c'), 0, 0)  18 us
    ppermute x9, waiting for transfers between devices, swap(): return lax.ppermute(value, axis, [(0, 1), (1, 0)])  12.6 us
    all_to_all x1, waiting for transfers between devices, shards(): pieces = lax.all_to_all(pieces, ('xh', 'yh', 'yl', 'zl'), 0, 0)  11.7 us
    all_to_all x1, starting transfers between devices, shards(): pieces = lax.all_to_all(pieces, ('xh', 'yh', 'yl', 'zl'), 0, 0)  8.27 us
    ppermute x9, starting transfers between devices, swap(): return lax.ppermute(value, axis, [(0, 1), (1, 0)])  6.74 us
    pallas_call x1, Pallas kernels, attend(): pl.pallas_call(attend_body, in_specs=[VM] * 8, out_specs=[ANY] * 2 + [VM]...  6.31 us
    ppermute x1, waiting for transfers between devices, shards(): lax.ppermute(dkv_sent, ring, [(i + 2, i) for i in range(count - 2)])  5.83 us
    ppermute x3, waiting for transfers between devices, shards(): lax.ppermute(blocks, ('xh', 'xl'), [(i, (i + turn) % 4) for i in range(4)])  4.15 us
  transfers between devices with their start and end apart: 15, of which 12 were waited for; matrix products, arithmetic and copies ran while one was open for 0% of the time, Pallas kernels for 20%

profile of v8, /device:TPU:1, one launch (start us, length us, event | category | flops | bytes accessed | tf_op | source)
XLA Modules:
  0.0 100.7 jit_solution(15376312286897283723)
XLA Ops:
  0.6 3.3 %collective-permute-start = (bf16[256,1536]{1,0:T(8,128)(2,1)}, bf16[256,1536]{1,0:T(8,128)(2,1)S(1)}, u32[]{:S(2)}, u32[]{:S(2)}) collective-permute-start(bf16[256,1536]{1,0:T(8,128)(2,1)} %bitcast.13), channel_id=1, source_target_pairs={{0,1},{1,0},{2,3},{3,2},{4,5},{5,4},{6,7},{7,6},{8,9},{9,8},{10,11... | collective-permute-start | bytes 2359304 | tf_op jit(solution)/shard_map/ppermute | solution.py:575
  4.0 0.1 collective-permute-start.1
  4.1 0.0 collective-permute-start.6
  4.1 3.4 %project_own.1 = (bf16[256,1536]{1,0:T(8,128)(2,1)S(1)}, bf16[1536,512]{1,0:T(8,128)(2,1)S(1)}, bf16[1536,768]{1,0:T(8,128)(2,1)S(1)}, bf16[256,768]{1,0:T(8,128)(2,1)S(1)}, bf16[256,256]{1,0:T(8,128)(2,1)S(1)}) custom-call(bf16[256,1536]{1,0:T(8,128)(2,1)} %bitcast.15, bf16[1536,512]{1,0:T(8,128)(2,1)} %wkv.3, bf16[1536,1536]{1,0:T(8,128)(2,1)} %wq.3), custom_call_target="tpu_custom_call" | custom-call | flops 805306368 | bytes 5242880 | tf_op jit(solution)/shard_map/project_own/pallas_call | solution.py:106
  7.5 0.0 collective-permute-done.x_oth
  7.5 0.4 project_kv.1
  7.9 2.7 %collective-permute-start.2 = (bf16[384,256]{1,0:T(8,128)(2,1)S(1)}, bf16[384,256]{1,0:T(8,128)(2,1)S(1)}, u32[]{:S(2)}, u32[]{:S(2)}) collective-permute-start(bf16[384,256]{1,0:T(8,128)(2,1)S(1)} %get-tuple-element.34), channel_id=1, source_target_pairs={{0,2},{1,3},{2,4},{3,5},{4,6},{5,7},{6,8},{7,9},{8,10},{9,11},{10,... | collective-permute-start | bytes 589832 | tf_op jit(solution)/shard_map/ppermute | solution.py:588
  10.6 0.0 copy-start.2
  10.6 0.0 copy-start.4
  10.6 0.8 project_q.1.q
  11.4 0.0 collective-permute-done.1.do_oth
  11.4 0.3 copy-done.2
  11.8 0.0 copy-done.4
  11.8 2.0 %attend_last.1 = (bf16[128,1536]{1,0:T(8,128)(2,1)S(1)}, f32[512,256]{1,0:T(8,128)S(1)}, s32[8,128]{1,0:T(8,128)S(1)}) custom-call(bf16[512,768]{1,0:T(8,128)(2,1)S(1)} %project_q.1.q, bf16[256,1536]{1,0:T(8,128)(2,1)S(1)} %bitcast.8, bf16[256,1536]{1,0:T(8,128)(2,1)S(1)} %collective-permute-done.1.do_oth, bf16[512,256]{1,0:T(8,128)(2,1)S(1)} %get-tuple-element.33.kv, ...), custom_call_target="tpu_custom_call" | custom-call | flops 603979776 | bytes 3145728 | tf_op jit(solution)/shard_map/attend_last/pallas_call | solution.py:262
  13.7 0.4 collective-permute-done.2.halo
  14.2 6.3 %attend.1 = (bf16[256,1536]{1,0:T(8,128)(2,1)}, bf16[256,1536]{1,0:T(8,128)(2,1)}, bf16[512,384]{1,0:T(8,128)(2,1)S(1)}, bf16[512,384]{1,0:T(8,128)(2,1)S(1)}, f...) custom-call(bf16[512,768]{1,0:T(8,128)(2,1)S(1)} %project_q.1.q, bf16[256,1536]{1,0:T(8,128)(2,1)S(1)} %bitcast.9, ...), custom_call_target="tpu_custom_call" | custom-call | flops 1811939328 | bytes 5242880 | tf_op jit(solution)/shard_map/attend/pallas_call | solution.py:322
  20.5 2.5 %collective-permute-done.6.value = bf16[256,1536]{1,0:T(8,128)(2,1)S(1)} collective-permute-done((bf16[256,1536]{1,0:T(8,128)(2,1)}, bf16[256,1536]{1,0:T(8,128)(2,1)S(1)}, u32[]{:S(2)}, u32[]{:S(2)}) %collective-permute-start.6) | collective-permute-done | bytes 786464 | tf_op jit(solution)/shard_map/ppermute | solution.py:575
  23.0 1.2 %collective-permute-start.7 = (bf16[256,1536]{1,0:T(8,128)(2,1)S(1)}, bf16[256,1536]{1,0:T(8,128)(2,1)S(1)}, u32[]{:S(2)}, u32[]{:S(2)}) collective-permute-start(bf16[256,1536]{1,0:T(8,128)(2,1)S(1)} %relay.1.x_own), channel_id=1, source_target_pairs={{0,1},{1,0},{2,3},{3,2},{4,5},{5,4},{6,7},{7,6},{8,9},{9,8},{10,11... | collective-permute-start | bytes 2359304 | tf_op jit(solution)/shard_map/ppermute | solution.py:575
  24.2 1.3 %collective-permute-start.3 = (bf16[384,256]{1,0:T(8,128)(2,1)S(1)}, bf16[384,256]{1,0:T(8,128)(2,1)S(1)}, u32[]{:S(2)}, u32[]{:S(2)}) collective-permute-start(bf16[384,256]{1,0:T(8,128)(2,1)S(1)} %get-tuple-element.40), channel_id=1, source_target_pairs={{2,0},{3,1},{4,2},{5,3},{6,4},{7,5},{8,6},{9,7},{10,8},{11,9},{12,... | collective-permute-start | bytes 589832 | tf_op jit(solution)/shard_map/ppermute | solution.py:595
  25.5 0.3 collective-permute-start.9
  25.8 1.0 %weight_near.3.near = f32[1536,384]{1,0:T(8,128)S(1)} custom-call(bf16[256,1536]{1,0:T(8,128)(2,1)S(1)} %get-tuple-element.47.x_own, bf16[256,1536]{1,0:T(8,128)(2,1)S(1)} %collective-permute-done.x_oth, bf16[512,384]{1,0:T(8,128)(2,1)S(1)} %get-tuple-element.46.after.g), custom_call_target="tpu_custom_call" | custom-call | flops 6039797760 | bytes 31457280 | tf_op jit(solution)/shard_map/weight_near/pallas_call | solution.py:387
  26.8 5.8 %collective-permute-done.3.arrived = bf16[384,256]{1,0:T(8,128)(2,1)S(1)} collective-permute-done((bf16[384,256]{1,0:T(8,128)(2,1)S(1)}, bf16[384,256]{1,0:T(8,128)(2,1)S(1)}, u32[]{:S(2)}, u32[]{:S(2)}) %collective-permute-start.3) | collective-permute-done | bytes 196640 | tf_op jit(solution)/shard_map/ppermute | solution.py:595
  32.6 0.1 total_kv.1
  32.7 0.1 collective-permute-start.8
  32.8 0.6 weight_near.2.near
  33.5 3.1 %collective-permute-done.9.g = bf16[512,384]{1,0:T(8,128)(2,1)S(1)} collective-permute-done((bf16[512,384]{1,0:T(8,128)(2,1)S(1)}, bf16[512,384]{1,0:T(8,128)(2,1)S(1)}, u32[]{:S(2)}, u32[]{:S(2)}) %collective-permute-start.9) | collective-permute-done | bytes 393248 | tf_op jit(solution)/shard_map/ppermute | solution.py:575
  36.5 0.0 collective-permute-done.7.x_oth
  36.5 2.1 %weight_far.2.rest_0_ = bf16[16,4,2,48,128]{4,3,2,1,0:T(8,128)(2,1)} custom-call(bf16[256,1536]{1,0:T(8,128)(2,1)S(1)} %relay.1.x_own, bf16[256,1536]{1,0:T(8,128)(2,1)S(1)} %collective-permute-done.7.x_oth, f32[1536,384]{1,0:T(8,128)S(1)} %weight_near.3.near, bf16[512,384]{1,0:T(8,128)(2,1)S(1)} %collective-permute-done.9.g), custom_call_target="tpu_custom_call" | custom-call | flops 603979776 | bytes 4194304 | tf_op jit(solution)/shard_map/weight_far/pallas_call | solution.py:446
  38.6 0.7 collective-permute-done.8.g
  39.3 1.4 %weight_far.3 = bf16[16,4,2,48,128]{4,3,2,1,0:T(8,128)(2,1)} custom-call(bf16[256,1536]{1,0:T(8,128)(2,1)S(1)} %relay.1.x_own, bf16[256,1536]{1,0:T(8,128)(2,1)S(1)} %collective-permute-done.7.x_oth, f32[1536,128]{1,0:T(8,128)S(1)} %weight_near.2.near, bf16[512,128]{1,0:T(8,128)(2,1)S(1)} %collective-permute-done.8.g, ...), custom_call_target="tpu_custom_call", output_to_operand_aliasing={{}: (4, {})} | custom-call | flops 201326592 | bytes 4194304 | tf_op jit(solution)/shard_map/weight_far/pallas_call | solution.py:446
  40.7 0.0 copy-start.1
  40.7 8.3 %all-to-all-start = ((bf16[16,4,2,48,128]{4,3,2,1,0:T(8,128)(2,1)}), bf16[16,4,2,48,128]{4,3,2,1,0:T(8,128)(2,1)S(1)}, u32[]{:S(2)}, u32[]{:S(2)}) async-start(bf16[16,4,2,48,128]{4,3,2,1,0:T(8,128)(2,1)} %weight_far.3), calls=%async_computation | async-start | bytes 3145728 | tf_op jit(solution)/shard_map/all_to_all | solution.py:605
  49.0 1.5 %collective-permute-start.4 = (bf16[256,1536]{1,0:T(8,128)(2,1)}, bf16[256,1536]{1,0:T(8,128)(2,1)S(1)}, u32[]{:S(2)}, u32[]{:S(2)}) collective-permute-start(bf16[256,1536]{1,0:T(8,128)(2,1)} %get-tuple-element.42), channel_id=1, source_target_pairs={{0,1},{1,0},{2,3},{3,2},{4,5},{5,4},{6,7},{7,6},{8,9},{9,8},{10,11... | collective-permute-start | bytes 2359304 | tf_op jit(solution)/shard_map/ppermute | solution.py:575
  50.5 0.1 collective-permute-start.5
  50.6 2.0 %collective-permute-done.5.dkv_in = bf16[256,256]{1,0:T(8,128)(2,1)S(1)} collective-permute-done((bf16[256,256]{1,0:T(8,128)(2,1)S(1)}, bf16[256,256]{1,0:T(8,128)(2,1)S(1)}, u32[]{:S(2)}, u32[]{:S(2)}) %collective-permute-start.5) | collective-permute-done | bytes 131104 | tf_op jit(solution)/shard_map/ppermute | solution.py:575
  52.6 0.1 collective-permute-done.4.mix_in
  52.7 0.0 copy-done.1
  52.7 0.0 copy-start
  52.7 2.3 %copy-done = bf16[1536,1536]{1,0:T(8,128)(2,1)S(1)} copy-done((bf16[1536,1536]{1,0:T(8,128)(2,1)S(1)}, bf16[1536,1536]{1,0:T(8,128)(2,1)}, u32[]{:S(2)}) %copy-start) | copy-done | bytes 4718616
  55.1 0.0 copy-start.3
  55.1 1.1 %copy-done.3 = bf16[256,1536]{1,0:T(8,128)(2,1)S(1)} copy-done((bf16[256,1536]{1,0:T(8,128)(2,1)S(1)}, bf16[256,1536]{1,0:T(8,128)(2,1)}, u32[]{:S(2)}) %copy-start.3) | copy-done | bytes 786456
  56.2 3.0 %grad_tokens.1 = (bf16[256,1536]{1,0:T(8,128)(2,1)}, bf16[256,1536]{1,0:T(8,128)(2,1)}, f32[8,128]{1,0:T(8,128)S(1)}) custom-call(bf16[256,1536]{1,0:T(8,128)(2,1)S(1)} %copy-done.3, bf16[256,256]{1,0:T(8,128)(2,1)S(1)} %get-tuple-element.41.dkv, bf16[256,1536]{1,0:T(8,128)(2,1)S(1)} %collective-permute-done.4.mix_in, ...), custom_call_target="tpu_custom_call" | custom-call | flops 1610612736 | bytes 8388608 | tf_op jit(solution)/shard_map/grad_tokens/pallas_call | solution.py:484
  59.2 11.7 %all-to-all-done.pieces = bf16[16,4,2,48,128]{4,3,2,1,0:T(8,128)(2,1)S(1)} async-done(((bf16[16,4,2,48,128]{4,3,2,1,0:T(8,128)(2,1)}), bf16[16,4,2,48,128]{4,3,2,1,0:T(8,128)(2,1)S(1)}, u32[]{:S(2)}, u32[]{:S(2)}) %all-to-all-start) | async-done | bytes 1572896 | tf_op jit(solution)/shard_map/all_to_all | solution.py:605
  70.9 0.2 sum_plane.1
  71.1 18.0 %all_to_all.10 = bf16[8,48,128]{2,1,0:T(8,128)(2,1)S(1)} all-to-all(bf16[8,48,128]{2,1,0:T(8,128)(2,1)S(1)} %bitcast.10), channel_id=1, replica_groups=mesh['xh'=2,'xl'=2,'yh'=2,'zh'=4,'zl'=2,'yl'=2,'c'=2] {'zh','c'}, dimensions={0} | all-to-all | bytes 196608 | tf_op jit(solution)/shard_map/all_to_all | solution.py:610
  89.2 0.1 collective-permute-start.10
  89.3 4.1 %collective-permute-done.10.far = bf16[2,48,128]{2,1,0:T(8,128)(2,1)S(1)} collective-permute-done((bf16[2,48,128]{2,1,0:T(8,128)(2,1)S(1)}, bf16[2,48,128]{2,1,0:T(8,128)(2,1)S(1)}, u32[]{:S(2)}, u32[]{:S(2)}) %collective-permute-start.10) | collective-permute-done | bytes 24608 | tf_op jit(solution)/shard_map/ppermute | solution.py:575
  93.5 0.2 collective-permute-start.13
  93.6 2.2 %collective-permute-start.12 = (bf16[2,2,48,128]{3,2,1,0:T(8,128)(2,1)S(1)}, bf16[2,2,48,128]{3,2,1,0:T(8,128)(2,1)S(1)}, u32[]{:S(2)}, u32[]{:S(2)}) collective-permute-start(bf16[2,2,48,128]{3,2,1,0:T(8,128)(2,1)S(1)} %stack.1.one), channel_id=1, source_target_pairs={{0,128},{64,192},{128,0},{192,64},{1,129},{65,193},{129,1},{193,65... | collective-permute-start | bytes 147464 | tf_op jit(solution)/shard_map/ppermute | solution.py:614
  95.8 0.0 collective-permute-start.11
  95.8 0.7 collective-permute-done.13.four
  96.5 1.6 %collective-permute-done.12.three = bf16[2,2,48,128]{3,2,1,0:T(8,128)(2,1)S(1)} collective-permute-done((bf16[2,2,48,128]{3,2,1,0:T(8,128)(2,1)S(1)}, bf16[2,2,48,128]{3,2,1,0:T(8,128)(2,1)S(1)}, u32[]{:S(2)}, u32[]{:S(2)}) %collective-permute-start.12) | collective-permute-done | bytes 49184 | tf_op jit(solution)/shard_map/ppermute | solution.py:614
  98.1 1.8 %collective-permute-done.11.two = bf16[2,2,48,128]{3,2,1,0:T(8,128)(2,1)S(1)} collective-permute-done((bf16[2,2,48,128]{3,2,1,0:T(8,128)(2,1)S(1)}, bf16[2,2,48,128]{3,2,1,0:T(8,128)(2,1)S(1)}, u32[]{:S(2)}, u32[]{:S(2)}) %collective-permute-start.11) | collective-permute-done | bytes 49184 | tf_op jit(solution)/shard_map/ppermute | solution.py:614
  99.9 0.7 finish.1
  (3 shorter events, 0.0 us)
Async XLA Ops:
  0.6 6.9 %collective-permute-start = (bf16[256,1536]{1,0:T(8,128)(2,1)}, bf16[256,1536]{1,0:T(8,128)(2,1)S(1)}, u32[]{:S(2)}, u32[]{:S(2)}) collective-permute-start(bf16[256,1536]{1,0:T(8,128)(2,1)} %bitcast.13), channel_id=1, source_target_pairs={{0,1},{1,0},{2,3},{3,2},{4,5},{5,4},{6,7},{7,6},{8,9},{9,8},{10,11... | collective-permute-start | bytes 2359304 | tf_op jit(solution)/shard_map/ppermute | solution.py:575
  4.0 7.5 %collective-permute-start.1 = (bf16[256,1536]{1,0:T(8,128)(2,1)}, bf16[256,1536]{1,0:T(8,128)(2,1)S(1)}, u32[]{:S(2)}, u32[]{:S(2)}) collective-permute-start(bf16[256,1536]{1,0:T(8,128)(2,1)} %bitcast.7), channel_id=1, source_target_pairs={{0,1},{1,0},{2,3},{3,2},{4,5},{5,4},{6,7},{7,6},{8,9},{9,8},{10,11... | collective-permute-start | bytes 2359304 | tf_op jit(solution)/shard_map/ppermute | solution.py:575
  4.1 18.9 %collective-permute-start.6 = (bf16[256,1536]{1,0:T(8,128)(2,1)}, bf16[256,1536]{1,0:T(8,128)(2,1)S(1)}, u32[]{:S(2)}, u32[]{:S(2)}) collective-permute-start(bf16[256,1536]{1,0:T(8,128)(2,1)} %bitcast.14), channel_id=1, source_target_pairs={{0,64},{64,0},{1,65},{65,1},{2,66},{66,2},{3,67},{67,3},{4,68},{68... | collective-permute-start | bytes 2359304 | tf_op jit(solution)/shard_map/ppermute | solution.py:575
  7.9 6.2 %collective-permute-start.2 = (bf16[384,256]{1,0:T(8,128)(2,1)S(1)}, bf16[384,256]{1,0:T(8,128)(2,1)S(1)}, u32[]{:S(2)}, u32[]{:S(2)}) collective-permute-start(bf16[384,256]{1,0:T(8,128)(2,1)S(1)} %get-tuple-element.34), channel_id=1, source_target_pairs={{0,2},{1,3},{2,4},{3,5},{4,6},{5,7},{6,8},{7,9},{8,10},{9,11},{10,... | collective-permute-start | bytes 589832 | tf_op jit(solution)/shard_map/ppermute | solution.py:588
  10.6 1.1 %copy-start.2 = (bf16[1,256,1536]{2,1,0:T(8,128)(2,1)S(1)}, bf16[1,256,1536]{2,1,0:T(8,128)(2,1)}, u32[]{:S(2)}) copy-start(bf16[1,256,1536]{2,1,0:T(8,128)(2,1)} %param.9) | copy-start | bytes 2359300
  10.6 1.1 %copy-start.4 = (s32[1,8192]{1,0:T(1,128)S(1)}, s32[1,8192]{1,0:T(1,128)}, u32[]{:S(2)}) copy-start(s32[1,8192]{1,0:T(1,128)} %param.6) | copy-start | bytes 98308
  23.0 13.5 %collective-permute-start.7 = (bf16[256,1536]{1,0:T(8,128)(2,1)S(1)}, bf16[256,1536]{1,0:T(8,128)(2,1)S(1)}, u32[]{:S(2)}, u32[]{:S(2)}) collective-permute-start(bf16[256,1536]{1,0:T(8,128)(2,1)S(1)} %relay.1.x_own), channel_id=1, source_target_pairs={{0,1},{1,0},{2,3},{3,2},{4,5},{5,4},{6,7},{7,6},{8,9},{9,8},{10,11... | collective-permute-start | bytes 2359304 | tf_op jit(solution)/shard_map/ppermute | solution.py:575
  24.2 8.4 %collective-permute-start.3 = (bf16[384,256]{1,0:T(8,128)(2,1)S(1)}, bf16[384,256]{1,0:T(8,128)(2,1)S(1)}, u32[]{:S(2)}, u32[]{:S(2)}) collective-permute-start(bf16[384,256]{1,0:T(8,128)(2,1)S(1)} %get-tuple-element.40), channel_id=1, source_target_pairs={{2,0},{3,1},{4,2},{5,3},{6,4},{7,5},{8,6},{9,7},{10,8},{11,9},{12,... | collective-permute-start | bytes 589832 | tf_op jit(solution)/shard_map/ppermute | solution.py:595
  25.5 11.0 %collective-permute-start.9 = (bf16[512,384]{1,0:T(8,128)(2,1)S(1)}, bf16[512,384]{1,0:T(8,128)(2,1)S(1)}, u32[]{:S(2)}, u32[]{:S(2)}) collective-permute-start(bf16[512,384]{1,0:T(8,128)(2,1)S(1)} %get-tuple-element.50), channel_id=1, source_target_pairs={{0,64},{64,0},{1,65},{65,1},{2,66},{66,2},{3,67},{67,3},{4,68},{68... | collective-permute-start | bytes 1179656 | tf_op jit(solution)/shard_map/ppermute | solution.py:575
  32.7 6.6 %collective-permute-start.8 = (bf16[512,128]{1,0:T(8,128)(2,1)S(1)}, bf16[512,128]{1,0:T(8,128)(2,1)S(1)}, u32[]{:S(2)}, u32[]{:S(2)}) collective-permute-start(bf16[512,128]{1,0:T(8,128)(2,1)S(1)} %get-tuple-element.49), channel_id=1, source_target_pairs={{0,64},{64,0},{1,65},{65,1},{2,66},{66,2},{3,67},{67,3},{4,68},{68... | collective-permute-start | bytes 393224 | tf_op jit(solution)/shard_map/ppermute | solution.py:575
  40.7 12.0 %copy-start.1 = (bf16[1536,512]{1,0:T(8,128)(2,1)S(1)}, bf16[1536,512]{1,0:T(8,128)(2,1)}, u32[]{:S(2)}) copy-start(bf16[1536,512]{1,0:T(8,128)(2,1)} %wkv.3) | copy-start | bytes 4718596
  40.7 30.2 %all-to-all-start = ((bf16[16,4,2,48,128]{4,3,2,1,0:T(8,128)(2,1)}), bf16[16,4,2,48,128]{4,3,2,1,0:T(8,128)(2,1)S(1)}, u32[]{:S(2)}, u32[]{:S(2)}) async-start(bf16[16,4,2,48,128]{4,3,2,1,0:T(8,128)(2,1)} %weight_far.3), calls=%async_computation | async-start | bytes 3145728 | tf_op jit(solution)/shard_map/all_to_all | solution.py:605
  49.0 3.7 %collective-permute-start.4 = (bf16[256,1536]{1,0:T(8,128)(2,1)}, bf16[256,1536]{1,0:T(8,128)(2,1)S(1)}, u32[]{:S(2)}, u32[]{:S(2)}) collective-permute-start(bf16[256,1536]{1,0:T(8,128)(2,1)} %get-tuple-element.42), channel_id=1, source_target_pairs={{0,1},{1,0},{2,3},{3,2},{4,5},{5,4},{6,7},{7,6},{8,9},{9,8},{10,11... | collective-permute-start | bytes 2359304 | tf_op jit(solution)/shard_map/ppermute | solution.py:575
  50.5 2.1 %collective-permute-start.5 = (bf16[256,256]{1,0:T(8,128)(2,1)S(1)}, bf16[256,256]{1,0:T(8,128)(2,1)S(1)}, u32[]{:S(2)}, u32[]{:S(2)}) collective-permute-start(bf16[256,256]{1,0:T(8,128)(2,1)S(1)} %get-tuple-element.43), channel_id=1, source_target_pairs={{0,1},{1,0},{2,3},{3,2},{4,5},{5,4},{6,7},{7,6},{8,9},{9,8},{10,11... | collective-permute-start | bytes 393224 | tf_op jit(solution)/shard_map/ppermute | solution.py:575
  52.7 2.3 %copy-start = (bf16[1536,1536]{1,0:T(8,128)(2,1)S(1)}, bf16[1536,1536]{1,0:T(8,128)(2,1)}, u32[]{:S(2)}) copy-start(bf16[1536,1536]{1,0:T(8,128)(2,1)} %wq.3) | copy-start | bytes 14155780
  55.1 1.1 %copy-start.3 = (bf16[256,1536]{1,0:T(8,128)(2,1)S(1)}, bf16[256,1536]{1,0:T(8,128)(2,1)}, u32[]{:S(2)}) copy-start(bf16[256,1536]{1,0:T(8,128)(2,1)} %get-tuple-element.38.mix) | copy-start | bytes 2359300
  89.2 4.3 %collective-permute-start.10 = (bf16[2,48,128]{2,1,0:T(8,128)(2,1)S(1)}, bf16[2,48,128]{2,1,0:T(8,128)(2,1)S(1)}, u32[]{:S(2)}, u32[]{:S(2)}) collective-permute-start(bf16[2,48,128]{2,1,0:T(8,128)(2,1)S(1)} %sum_line.1.near), channel_id=1, source_target_pairs={{0,32},{32,0},{1,33},{33,1},{2,34},{34,2},{3,35},{35,3},{4,36},{36... | collective-permute-start | bytes 73736 | tf_op jit(solution)/shard_map/ppermute | solution.py:575
  93.5 3.0 %collective-permute-start.13 = (bf16[2,2,48,128]{3,2,1,0:T(8,128)(2,1)S(1)}, bf16[2,2,48,128]{3,2,1,0:T(8,128)(2,1)S(1)}, u32[]{:S(2)}, u32[]{:S(2)}) collective-permute-start(bf16[2,2,48,128]{3,2,1,0:T(8,128)(2,1)S(1)} %stack.1.one), channel_id=1, source_target_pairs={{0,192},{64,0},{128,64},{192,128},{1,193},{65,1},{129,65},{193,129... | collective-permute-start | bytes 147464 | tf_op jit(solution)/shard_map/ppermute | solution.py:614
  93.6 4.5 %collective-permute-start.12 = (bf16[2,2,48,128]{3,2,1,0:T(8,128)(2,1)S(1)}, bf16[2,2,48,128]{3,2,1,0:T(8,128)(2,1)S(1)}, u32[]{:S(2)}, u32[]{:S(2)}) collective-permute-start(bf16[2,2,48,128]{3,2,1,0:T(8,128)(2,1)S(1)} %stack.1.one), channel_id=1, source_target_pairs={{0,128},{64,192},{128,0},{192,64},{1,129},{65,193},{129,1},{193,65... | collective-permute-start | bytes 147464 | tf_op jit(solution)/shard_map/ppermute | solution.py:614
  95.8 4.2 %collective-permute-start.11 = (bf16[2,2,48,128]{3,2,1,0:T(8,128)(2,1)S(1)}, bf16[2,2,48,128]{3,2,1,0:T(8,128)(2,1)S(1)}, u32[]{:S(2)}, u32[]{:S(2)}) collective-permute-start(bf16[2,2,48,128]{3,2,1,0:T(8,128)(2,1)S(1)} %stack.1.one), channel_id=1, source_target_pairs={{0,64},{64,128},{128,192},{192,0},{1,65},{65,129},{129,193},{193,1... | collective-permute-start | bytes 147464 | tf_op jit(solution)/shard_map/ppermute | solution.py:614

commit v9 on v7

--- a/solution.py
+++ b/solution.py
@@ -390,7 +390,7 @@
         out_specs=VM,
         out_shape=shape((D, width), F32),
         compiler_params=params(),
-        cost_estimate=cost(20 * PAIR * D * width, 30 << 20),
+        cost_estimate=cost(200 * PAIR * D * width, 300 << 20),
         name="weight_near",
     )(x_own, x_oth, g)
 
@@ -560,11 +560,11 @@
     do_own = grad_context[0]
     x_oth = swap(x_own)
     do_oth = swap(do_own)
+    far_own = swap(x_own, "xl")
     count = 32
     ring = ("zh", "zl", "yl", "c")
     x_own, wkv_here, wq_here, q_own, kv_own = project_own(x_own, w_keyval, w_query)
     kv, kv_sent = project_kv(x_oth, kv_own, wkv_here)
-    far_own = swap(x_own, "xl")
     halo = lax.ppermute(kv_sent, ring, [(i, i + 2) for i in range(count - 2)])
     q = project_q(x_oth, q_own, wq_here)
     segs = segments.reshape(-1, BLOCK)

time: 104 us -> 98.1 us (0.943)
  waiting for transfers between devices: 29.6 us -> 18.8 us
  starting transfers between devices: 18 us -> 23.3 us
    ppermute x8, waiting for transfers between devices: 11.7 us -> 5.63 us  [swap(): return lax.ppermute(value, axis, [(0, 1), (1, 0)])]
    ppermute x1, waiting for transfers between devices: 5.82 us -> 3.02 us  [shards(): lax.ppermute(dkv_sent, ring, [(i + 2, i) for i in range(count - 2)])]
    all_to_all x1, starting transfers between devices: 7.36 us -> 10.1 us  [shards(): pieces = lax.all_to_all(pieces, ('xh', 'yh', 'yl', 'zl'), 0, 0)]
    ppermute x8, starting transfers between devices: 6.71 us -> 9.24 us  [swap(): return lax.ppermute(value, axis, [(0, 1), (1, 0)])]
    all_to_all x1, waiting for transfers between devices: 11.7 us -> 9.74 us  [shards(): pieces = lax.all_to_all(pieces, ('xh', 'yh', 'yl', 'zl'), 0, 0)]
  transfers between devices with their start and end apart: 11 -> 11, of which waited for: 8 -> 8; matrix products, arithmetic and copies ran while one was open for 0% -> 0% of each run, Pallas kernels for 19% -> 20%
where the time goes in v9:
time: 98.1 us; the launch traced here: 96.8 us
  blocking collectives  28 us (29%)
  starting transfers between devices  23.3 us (24%)
  Pallas kernels  22.1 us (23%)
  waiting for transfers between devices  18.8 us (19%)
  local copies, waits for them, and re-layouts  3.8 us (4%)
    all_to_all x1, blocking collectives, shards(): lines = lax.all_to_all(plane.reshape(8, ROWS, HEAD_DIM), ('zh', 'c'), 0, 0)  17.6 us
    all_to_all x1, blocking collectives, shards(): blocks = lax.all_to_all(blocks, ('xh', 'xl', 'yh'), 0, 0)  10.4 us
    all_to_all x1, starting transfers between devices, shards(): pieces = lax.all_to_all(pieces, ('xh', 'yh', 'yl', 'zl'), 0, 0)  10.1 us
    all_to_all x1, waiting for transfers between devices, shards(): pieces = lax.all_to_all(pieces, ('xh', 'yh', 'yl', 'zl'), 0, 0)  9.74 us
    ppermute x8, starting transfers between devices, swap(): return lax.ppermute(value, axis, [(0, 1), (1, 0)])  9.24 us
    pallas_call x1, Pallas kernels, attend(): pl.pallas_call(attend_body, in_specs=[VM] * 8, out_specs=[ANY] * 2 + [VM]...  6.33 us
    ppermute x8, waiting for transfers between devices, swap(): return lax.ppermute(value, axis, [(0, 1), (1, 0)])  5.63 us
    unnamed x10, local copies, waits for them, and re-layouts  3.8 us
  transfers between devices with their start and end apart: 11, of which 8 were waited for; matrix products, arithmetic and copies ran while one was open for 0% of the time, Pallas kernels for 20%

profile of v9, /device:TPU:1, one launch (start us, length us, event | category | flops | bytes accessed | tf_op | source)
XLA Modules:
  0.0 96.8 jit_solution(1484398874174330147)
XLA Ops:
  0.6 3.3 %collective-permute-start = (bf16[256,1536]{1,0:T(8,128)(2,1)}, bf16[256,1536]{1,0:T(8,128)(2,1)S(1)}, u32[]{:S(2)}, u32[]{:S(2)}) collective-permute-start(bf16[256,1536]{1,0:T(8,128)(2,1)} %bitcast.13), channel_id=1, source_target_pairs={{0,1},{1,0},{2,3},{3,2},{4,5},{5,4},{6,7},{7,6},{8,9},{9,8},{10,11... | collective-permute-start | bytes 2359304 | tf_op jit(solution)/shard_map/ppermute | solution.py:555
  4.0 0.1 collective-permute-start.1
  4.1 0.0 collective-permute-start.6
  4.1 3.4 %project_own.1 = (bf16[256,1536]{1,0:T(8,128)(2,1)S(1)}, bf16[1536,512]{1,0:T(8,128)(2,1)S(1)}, bf16[1536,768]{1,0:T(8,128)(2,1)S(1)}, bf16[256,768]{1,0:T(8,128)(2,1)S(1)}, bf16[256,256]{1,0:T(8,128)(2,1)S(1)}) custom-call(bf16[256,1536]{1,0:T(8,128)(2,1)} %bitcast.15, bf16[1536,512]{1,0:T(8,128)(2,1)} %wkv.3, bf16[1536,1536]{1,0:T(8,128)(2,1)} %wq.3), custom_call_target="tpu_custom_call" | custom-call | flops 805306368 | bytes 5242880 | tf_op jit(solution)/shard_map/project_own/pallas_call | solution.py:106
  7.5 0.0 collective-permute-done.x_oth
  7.5 0.4 project_kv.1
  7.9 2.7 %collective-permute-start.2 = (bf16[384,256]{1,0:T(8,128)(2,1)S(1)}, bf16[384,256]{1,0:T(8,128)(2,1)S(1)}, u32[]{:S(2)}, u32[]{:S(2)}) collective-permute-start(bf16[384,256]{1,0:T(8,128)(2,1)S(1)} %get-tuple-element.34), channel_id=1, source_target_pairs={{0,2},{1,3},{2,4},{3,5},{4,6},{5,7},{6,8},{7,9},{8,10},{9,11},{10,... | collective-permute-start | bytes 589832 | tf_op jit(solution)/shard_map/ppermute | solution.py:568
  10.6 0.0 copy-start.2
  10.6 0.0 copy-start.4
  10.7 0.8 project_q.1.q
  11.4 0.0 collective-permute-done.1.do_oth
  11.4 0.3 copy-done.2
  11.8 0.0 copy-done.4
  11.8 2.0 %attend_last.1 = (bf16[128,1536]{1,0:T(8,128)(2,1)S(1)}, f32[512,256]{1,0:T(8,128)S(1)}, s32[8,128]{1,0:T(8,128)S(1)}) custom-call(bf16[512,768]{1,0:T(8,128)(2,1)S(1)} %project_q.1.q, bf16[256,1536]{1,0:T(8,128)(2,1)S(1)} %bitcast.8, bf16[256,1536]{1,0:T(8,128)(2,1)S(1)} %collective-permute-done.1.do_oth, bf16[512,256]{1,0:T(8,128)(2,1)S(1)} %get-tuple-element.33.kv, ...), custom_call_target="tpu_custom_call" | custom-call | flops 603979776 | bytes 3145728 | tf_op jit(solution)/shard_map/attend_last/pallas_call | solution.py:262
  13.8 0.4 collective-permute-done.2.halo
  14.2 6.3 %attend.1 = (bf16[256,1536]{1,0:T(8,128)(2,1)}, bf16[256,1536]{1,0:T(8,128)(2,1)}, bf16[512,384]{1,0:T(8,128)(2,1)S(1)}, bf16[512,384]{1,0:T(8,128)(2,1)S(1)}, f...) custom-call(bf16[512,768]{1,0:T(8,128)(2,1)S(1)} %project_q.1.q, bf16[256,1536]{1,0:T(8,128)(2,1)S(1)} %bitcast.9, ...), custom_call_target="tpu_custom_call" | custom-call | flops 1811939328 | bytes 5242880 | tf_op jit(solution)/shard_map/attend/pallas_call | solution.py:322
  20.5 1.3 %collective-permute-start.3 = (bf16[384,256]{1,0:T(8,128)(2,1)S(1)}, bf16[384,256]{1,0:T(8,128)(2,1)S(1)}, u32[]{:S(2)}, u32[]{:S(2)}) collective-permute-start(bf16[384,256]{1,0:T(8,128)(2,1)S(1)} %get-tuple-element.40), channel_id=1, source_target_pairs={{2,0},{3,1},{4,2},{5,3},{6,4},{7,5},{8,6},{9,7},{10,8},{11,9},{12,... | collective-permute-start | bytes 589832 | tf_op jit(solution)/shard_map/ppermute | solution.py:575
  21.8 0.3 collective-permute-start.9
  22.1 0.9 collective-permute-done.6.value
  23.0 1.2 %collective-permute-start.7 = (bf16[256,1536]{1,0:T(8,128)(2,1)S(1)}, bf16[256,1536]{1,0:T(8,128)(2,1)S(1)}, u32[]{:S(2)}, u32[]{:S(2)}) collective-permute-start(bf16[256,1536]{1,0:T(8,128)(2,1)S(1)} %relay.1.x_own), channel_id=1, source_target_pairs={{0,1},{1,0},{2,3},{3,2},{4,5},{5,4},{6,7},{7,6},{8,9},{9,8},{10,11... | collective-permute-start | bytes 2359304 | tf_op jit(solution)/shard_map/ppermute | solution.py:555
  24.2 1.0 %weight_near.3.near = f32[1536,384]{1,0:T(8,128)S(1)} custom-call(bf16[256,1536]{1,0:T(8,128)(2,1)S(1)} %get-tuple-element.47.x_own, bf16[256,1536]{1,0:T(8,128)(2,1)S(1)} %collective-permute-done.x_oth, bf16[512,384]{1,0:T(8,128)(2,1)S(1)} %get-tuple-element.46.after.g), custom_call_target="tpu_custom_call" | custom-call | flops 60397977600 | bytes 314572800 | tf_op jit(solution)/shard_map/weight_near/pallas_call | solution.py:387
  25.2 3.0 %collective-permute-done.3.arrived = bf16[384,256]{1,0:T(8,128)(2,1)S(1)} collective-permute-done((bf16[384,256]{1,0:T(8,128)(2,1)S(1)}, bf16[384,256]{1,0:T(8,128)(2,1)S(1)}, u32[]{:S(2)}, u32[]{:S(2)}) %collective-permute-start.3) | collective-permute-done | bytes 196640 | tf_op jit(solution)/shard_map/ppermute | solution.py:575
  28.3 0.1 total_kv.1
  28.4 0.3 collective-permute-start.8
  28.7 0.6 weight_near.2.near
  29.3 1.6 %collective-permute-done.9.g = bf16[512,384]{1,0:T(8,128)(2,1)S(1)} collective-permute-done((bf16[512,384]{1,0:T(8,128)(2,1)S(1)}, bf16[512,384]{1,0:T(8,128)(2,1)S(1)}, u32[]{:S(2)}, u32[]{:S(2)}) %collective-permute-start.9) | collective-permute-done | bytes 393248 | tf_op jit(solution)/shard_map/ppermute | solution.py:555
  30.9 0.0 collective-permute-done.7.x_oth
  30.9 2.1 %weight_far.2.rest_0_ = bf16[16,4,2,48,128]{4,3,2,1,0:T(8,128)(2,1)} custom-call(bf16[256,1536]{1,0:T(8,128)(2,1)S(1)} %relay.1.x_own, bf16[256,1536]{1,0:T(8,128)(2,1)S(1)} %collective-permute-done.7.x_oth, f32[1536,384]{1,0:T(8,128)S(1)} %weight_near.3.near, bf16[512,384]{1,0:T(8,128)(2,1)S(1)} %collective-permute-done.9.g), custom_call_target="tpu_custom_call" | custom-call | flops 603979776 | bytes 4194304 | tf_op jit(solution)/shard_map/weight_far/pallas_call | solution.py:446
  33.0 1.0 %collective-permute-done.8.g = bf16[512,128]{1,0:T(8,128)(2,1)S(1)} collective-permute-done((bf16[512,128]{1,0:T(8,128)(2,1)S(1)}, bf16[512,128]{1,0:T(8,128)(2,1)S(1)}, u32[]{:S(2)}, u32[]{:S(2)}) %collective-permute-start.8) | collective-permute-done | bytes 131104 | tf_op jit(solution)/shard_map/ppermute | solution.py:555
  34.0 1.4 %weight_far.3 = bf16[16,4,2,48,128]{4,3,2,1,0:T(8,128)(2,1)} custom-call(bf16[256,1536]{1,0:T(8,128)(2,1)S(1)} %relay.1.x_own, bf16[256,1536]{1,0:T(8,128)(2,1)S(1)} %collective-permute-done.7.x_oth, f32[1536,128]{1,0:T(8,128)S(1)} %weight_near.2.near, bf16[512,128]{1,0:T(8,128)(2,1)S(1)} %collective-permute-done.8.g, ...), custom_call_target="tpu_custom_call", output_to_operand_aliasing={{}: (4, {})} | custom-call | flops 201326592 | bytes 4194304 | tf_op jit(solution)/shard_map/weight_far/pallas_call | solution.py:446
  35.4 0.0 copy-start.1
  35.4 10.1 %all-to-all-start = ((bf16[16,4,2,48,128]{4,3,2,1,0:T(8,128)(2,1)}), bf16[16,4,2,48,128]{4,3,2,1,0:T(8,128)(2,1)S(1)}, u32[]{:S(2)}, u32[]{:S(2)}) async-start(bf16[16,4,2,48,128]{4,3,2,1,0:T(8,128)(2,1)} %weight_far.3), calls=%async_computation | async-start | bytes 3145728 | tf_op jit(solution)/shard_map/all_to_all | solution.py:585
  45.5 3.8 %collective-permute-start.4 = (bf16[256,1536]{1,0:T(8,128)(2,1)}, bf16[256,1536]{1,0:T(8,128)(2,1)S(1)}, u32[]{:S(2)}, u32[]{:S(2)}) collective-permute-start(bf16[256,1536]{1,0:T(8,128)(2,1)} %get-tuple-element.42), channel_id=1, source_target_pairs={{0,1},{1,0},{2,3},{3,2},{4,5},{5,4},{6,7},{7,6},{8,9},{9,8},{10,11... | collective-permute-start | bytes 2359304 | tf_op jit(solution)/shard_map/ppermute | solution.py:555
  49.4 0.1 collective-permute-start.5
  49.5 2.0 %collective-permute-done.5.dkv_in = bf16[256,256]{1,0:T(8,128)(2,1)S(1)} collective-permute-done((bf16[256,256]{1,0:T(8,128)(2,1)S(1)}, bf16[256,256]{1,0:T(8,128)(2,1)S(1)}, u32[]{:S(2)}, u32[]{:S(2)}) %collective-permute-start.5) | collective-permute-done | bytes 131104 | tf_op jit(solution)/shard_map/ppermute | solution.py:555
  51.5 0.1 collective-permute-done.4.mix_in
  51.6 0.0 copy-done.1
  51.6 0.0 copy-start
  51.6 2.3 %copy-done = bf16[1536,1536]{1,0:T(8,128)(2,1)S(1)} copy-done((bf16[1536,1536]{1,0:T(8,128)(2,1)S(1)}, bf16[1536,1536]{1,0:T(8,128)(2,1)}, u32[]{:S(2)}) %copy-start) | copy-done | bytes 4718616
  54.0 0.0 copy-start.3
  54.0 1.1 %copy-done.3 = bf16[256,1536]{1,0:T(8,128)(2,1)S(1)} copy-done((bf16[256,1536]{1,0:T(8,128)(2,1)S(1)}, bf16[256,1536]{1,0:T(8,128)(2,1)}, u32[]{:S(2)}) %copy-start.3) | copy-done | bytes 786456
  55.1 3.0 %grad_tokens.1 = (bf16[256,1536]{1,0:T(8,128)(2,1)}, bf16[256,1536]{1,0:T(8,128)(2,1)}, f32[8,128]{1,0:T(8,128)S(1)}) custom-call(bf16[256,1536]{1,0:T(8,128)(2,1)S(1)} %copy-done.3, bf16[256,256]{1,0:T(8,128)(2,1)S(1)} %get-tuple-element.41.dkv, bf16[256,1536]{1,0:T(8,128)(2,1)S(1)} %collective-permute-done.4.mix_in, ...), custom_call_target="tpu_custom_call" | custom-call | flops 1610612736 | bytes 8388608 | tf_op jit(solution)/shard_map/grad_tokens/pallas_call | solution.py:484
  58.1 9.7 %all-to-all-done.pieces = bf16[16,4,2,48,128]{4,3,2,1,0:T(8,128)(2,1)S(1)} async-done(((bf16[16,4,2,48,128]{4,3,2,1,0:T(8,128)(2,1)}), bf16[16,4,2,48,128]{4,3,2,1,0:T(8,128)(2,1)S(1)}, u32[]{:S(2)}, u32[]{:S(2)}) %all-to-all-start) | async-done | bytes 1572896 | tf_op jit(solution)/shard_map/all_to_all | solution.py:585
  67.8 0.2 sum_plane.1
  68.0 17.6 %all_to_all.15 = bf16[8,48,128]{2,1,0:T(8,128)(2,1)S(1)} all-to-all(bf16[8,48,128]{2,1,0:T(8,128)(2,1)S(1)} %bitcast.10), channel_id=1, replica_groups=mesh['xh'=2,'xl'=2,'yh'=2,'zh'=4,'zl'=2,'yl'=2,'c'=2] {'zh','c'}, dimensions={0} | all-to-all | bytes 196608 | tf_op jit(solution)/shard_map/all_to_all | solution.py:590
  85.7 10.4 %all_to_all.16.blocks = bf16[8,2,48,128]{3,2,1,0:T(8,128)(2,1)S(1)} all-to-all(bf16[8,2,48,128]{3,2,1,0:T(8,128)(2,1)S(1)} %sum_line.1), channel_id=1, replica_groups=mesh['xh'=2,'xl'=2,'yh'=2,'zh'=4,'zl'=2,'yl'=2,'c'=2] {'xh','xl','yh'}, dimensions={0} | all-to-all | bytes 393216 | tf_op jit(solution)/shard_map/all_to_all | solution.py:592
  96.1 0.7 finish.1
  (2 shorter events, 0.0 us)
Async XLA Ops:
  0.6 6.9 %collective-permute-start = (bf16[256,1536]{1,0:T(8,128)(2,1)}, bf16[256,1536]{1,0:T(8,128)(2,1)S(1)}, u32[]{:S(2)}, u32[]{:S(2)}) collective-permute-start(bf16[256,1536]{1,0:T(8,128)(2,1)} %bitcast.13), channel_id=1, source_target_pairs={{0,1},{1,0},{2,3},{3,2},{4,5},{5,4},{6,7},{7,6},{8,9},{9,8},{10,11... | collective-permute-start | bytes 2359304 | tf_op jit(solution)/shard_map/ppermute | solution.py:555
  4.0 7.5 %collective-permute-start.1 = (bf16[256,1536]{1,0:T(8,128)(2,1)}, bf16[256,1536]{1,0:T(8,128)(2,1)S(1)}, u32[]{:S(2)}, u32[]{:S(2)}) collective-permute-start(bf16[256,1536]{1,0:T(8,128)(2,1)} %bitcast.7), channel_id=1, source_target_pairs={{0,1},{1,0},{2,3},{3,2},{4,5},{5,4},{6,7},{7,6},{8,9},{9,8},{10,11... | collective-permute-start | bytes 2359304 | tf_op jit(solution)/shard_map/ppermute | solution.py:555
  4.1 18.9 %collective-permute-start.6 = (bf16[256,1536]{1,0:T(8,128)(2,1)}, bf16[256,1536]{1,0:T(8,128)(2,1)S(1)}, u32[]{:S(2)}, u32[]{:S(2)}) collective-permute-start(bf16[256,1536]{1,0:T(8,128)(2,1)} %bitcast.14), channel_id=1, source_target_pairs={{0,64},{64,0},{1,65},{65,1},{2,66},{66,2},{3,67},{67,3},{4,68},{68... | collective-permute-start | bytes 2359304 | tf_op jit(solution)/shard_map/ppermute | solution.py:555
  7.9 6.2 %collective-permute-start.2 = (bf16[384,256]{1,0:T(8,128)(2,1)S(1)}, bf16[384,256]{1,0:T(8,128)(2,1)S(1)}, u32[]{:S(2)}, u32[]{:S(2)}) collective-permute-start(bf16[384,256]{1,0:T(8,128)(2,1)S(1)} %get-tuple-element.34), channel_id=1, source_target_pairs={{0,2},{1,3},{2,4},{3,5},{4,6},{5,7},{6,8},{7,9},{8,10},{9,11},{10,... | collective-permute-start | bytes 589832 | tf_op jit(solution)/shard_map/ppermute | solution.py:568
  10.6 1.1 %copy-start.2 = (bf16[1,256,1536]{2,1,0:T(8,128)(2,1)S(1)}, bf16[1,256,1536]{2,1,0:T(8,128)(2,1)}, u32[]{:S(2)}) copy-start(bf16[1,256,1536]{2,1,0:T(8,128)(2,1)} %param.9) | copy-start | bytes 2359300
  10.6 1.1 %copy-start.4 = (s32[1,8192]{1,0:T(1,128)S(1)}, s32[1,8192]{1,0:T(1,128)}, u32[]{:S(2)}) copy-start(s32[1,8192]{1,0:T(1,128)} %param.6) | copy-start | bytes 98308
  20.5 7.8 %collective-permute-start.3 = (bf16[384,256]{1,0:T(8,128)(2,1)S(1)}, bf16[384,256]{1,0:T(8,128)(2,1)S(1)}, u32[]{:S(2)}, u32[]{:S(2)}) collective-permute-start(bf16[384,256]{1,0:T(8,128)(2,1)S(1)} %get-tuple-element.40), channel_id=1, source_target_pairs={{2,0},{3,1},{4,2},{5,3},{6,4},{7,5},{8,6},{9,7},{10,8},{11,9},{12,... | collective-permute-start | bytes 589832 | tf_op jit(solution)/shard_map/ppermute | solution.py:575
  21.8 9.1 %collective-permute-start.9 = (bf16[512,384]{1,0:T(8,128)(2,1)S(1)}, bf16[512,384]{1,0:T(8,128)(2,1)S(1)}, u32[]{:S(2)}, u32[]{:S(2)}) collective-permute-start(bf16[512,384]{1,0:T(8,128)(2,1)S(1)} %get-tuple-element.50), channel_id=1, source_target_pairs={{0,64},{64,0},{1,65},{65,1},{2,66},{66,2},{3,67},{67,3},{4,68},{68... | collective-permute-start | bytes 1179656 | tf_op jit(solution)/shard_map/ppermute | solution.py:555
  23.0 8.0 %collective-permute-start.7 = (bf16[256,1536]{1,0:T(8,128)(2,1)S(1)}, bf16[256,1536]{1,0:T(8,128)(2,1)S(1)}, u32[]{:S(2)}, u32[]{:S(2)}) collective-permute-start(bf16[256,1536]{1,0:T(8,128)(2,1)S(1)} %relay.1.x_own), channel_id=1, source_target_pairs={{0,1},{1,0},{2,3},{3,2},{4,5},{5,4},{6,7},{7,6},{8,9},{9,8},{10,11... | collective-permute-start | bytes 2359304 | tf_op jit(solution)/shard_map/ppermute | solution.py:555
  28.4 5.7 %collective-permute-start.8 = (bf16[512,128]{1,0:T(8,128)(2,1)S(1)}, bf16[512,128]{1,0:T(8,128)(2,1)S(1)}, u32[]{:S(2)}, u32[]{:S(2)}) collective-permute-start(bf16[512,128]{1,0:T(8,128)(2,1)S(1)} %get-tuple-element.49), channel_id=1, source_target_pairs={{0,64},{64,0},{1,65},{65,1},{2,66},{66,2},{3,67},{67,3},{4,68},{68... | collective-permute-start | bytes 393224 | tf_op jit(solution)/shard_map/ppermute | solution.py:555
  35.4 16.2 %copy-start.1 = (bf16[1536,512]{1,0:T(8,128)(2,1)S(1)}, bf16[1536,512]{1,0:T(8,128)(2,1)}, u32[]{:S(2)}) copy-start(bf16[1536,512]{1,0:T(8,128)(2,1)} %wkv.3) | copy-start | bytes 4718596
  35.4 32.4 %all-to-all-start = ((bf16[16,4,2,48,128]{4,3,2,1,0:T(8,128)(2,1)}), bf16[16,4,2,48,128]{4,3,2,1,0:T(8,128)(2,1)S(1)}, u32[]{:S(2)}, u32[]{:S(2)}) async-start(bf16[16,4,2,48,128]{4,3,2,1,0:T(8,128)(2,1)} %weight_far.3), calls=%async_computation | async-start | bytes 3145728 | tf_op jit(solution)/shard_map/all_to_all | solution.py:585
  45.5 6.1 %collective-permute-start.4 = (bf16[256,1536]{1,0:T(8,128)(2,1)}, bf16[256,1536]{1,0:T(8,128)(2,1)S(1)}, u32[]{:S(2)}, u32[]{:S(2)}) collective-permute-start(bf16[256,1536]{1,0:T(8,128)(2,1)} %get-tuple-element.42), channel_id=1, source_target_pairs={{0,1},{1,0},{2,3},{3,2},{4,5},{5,4},{6,7},{7,6},{8,9},{9,8},{10,11... | collective-permute-start | bytes 2359304 | tf_op jit(solution)/shard_map/ppermute | solution.py:555
  49.4 2.1 %collective-permute-start.5 = (bf16[256,256]{1,0:T(8,128)(2,1)S(1)}, bf16[256,256]{1,0:T(8,128)(2,1)S(1)}, u32[]{:S(2)}, u32[]{:S(2)}) collective-permute-start(bf16[256,256]{1,0:T(8,128)(2,1)S(1)} %get-tuple-element.43), channel_id=1, source_target_pairs={{0,1},{1,0},{2,3},{3,2},{4,5},{5,4},{6,7},{7,6},{8,9},{9,8},{10,11... | collective-permute-start | bytes 393224 | tf_op jit(solution)/shard_map/ppermute | solution.py:555
  51.6 2.3 %copy-start = (bf16[1536,1536]{1,0:T(8,128)(2,1)S(1)}, bf16[1536,1536]{1,0:T(8,128)(2,1)}, u32[]{:S(2)}) copy-start(bf16[1536,1536]{1,0:T(8,128)(2,1)} %wq.3) | copy-start | bytes 14155780
  54.0 1.1 %copy-start.3 = (bf16[256,1536]{1,0:T(8,128)(2,1)S(1)}, bf16[256,1536]{1,0:T(8,128)(2,1)}, u32[]{:S(2)}) copy-start(bf16[256,1536]{1,0:T(8,128)(2,1)} %get-tuple-element.38.mix) | copy-start | bytes 2359300
